TPU v7x, 32 devices: a whole 2x2x4 slice. The times are simulated.
32 devices in a mesh: cuts: 2 (over x), mode: 8 (over z, y), branch: 2 (over core).
Axes of the slice: x: 2, y: 2, z: 4, core: 2. Of those that a mesh axis runs over, the one named last changes fastest.
Arguments:
- leaves: bfloat16 [8, 2, 32, 512, 512], P('branch', None, ('cuts', 'mode')), parts along dimension 2, may hold values from -0.1875 to 0.1875
- join_order: int32 [7], replicated, may hold values from 0 to 1
- slice_values: int32 [32], P(('cuts', 'mode')), parts along dimension 0, may hold values from 0 to 1
- boundary: bfloat16 [2, 2, 512, 512], replicated, may hold values from -4 to 4
Outputs:
- amplitudes: float32 [2, 32, 512, 512], P(None, ('cuts', 'mode'), 'branch'), parts along dimension 1
There are 2 independent parts, one for each index of `cuts`. A program takes and returns all parts, laid end to end along the dimension named above; an argument that names none is the same for every part. Nothing has to cross between parts.
Inputs may be any that keep to these rules, and one draw needn't show every extreme that they name: `join_order`: 1 puts the second operand of the join on the left.
All inputs are finite; a program needn't handle non-finite values.
Results may differ from a plain program's by a relative error of at most 0.0076.
Values may be sent and summed in bfloat16 or wider, within the bound.
No kernel may reach another device: no remote copies, remote signals or barrier semaphores. Data moves between devices by JAX's collectives and lax.ppermute only.
A program may use at most 64 MiB of HBM per device.

v0:
```python
import jax
import jax.numpy as jnp
from jax import lax
from jax.sharding import PartitionSpec as P


def from_partner(value, axis, bit):
    mask = 2**bit
    pairs = [(source, source ^ mask) for source in range(lax.axis_size(axis))]
    return lax.ppermute(value, axis, pairs)


def complex_sums(left_op, right_op):
    spec = "bij,bjk->bik"
    real_part = jnp.einsum(
        spec, left_op[0], right_op[0], preferred_element_type=jnp.float32
    ) - jnp.einsum(spec, left_op[1], right_op[1], preferred_element_type=jnp.float32)
    imag_part = jnp.einsum(
        spec, left_op[0], right_op[1], preferred_element_type=jnp.float32
    ) + jnp.einsum(spec, left_op[1], right_op[0], preferred_element_type=jnp.float32)
    return jnp.stack([real_part, imag_part])


def complex_product(left_op, right_op):
    return complex_sums(left_op, right_op).astype(jnp.bfloat16)


def join_pair(left_op, right_op, swapped):
    return lax.cond(
        swapped == 1,
        lambda: complex_product(right_op, left_op),
        lambda: complex_product(left_op, right_op),
    )


def split_rows(tensor, blocks):
    shape = tensor.shape
    return tensor.reshape(shape[0], shape[1], blocks, shape[2] // blocks, shape[3])


def merge_rows(tensor):
    shape = tensor.shape
    width = shape[4]
    total_rows = shape[1] * shape[2] * shape[3]
    return tensor.reshape(shape[0], total_rows // width, width, width)


def per_device(leaves, join_order, slice_values, boundary):
    blocks = lax.axis_size("mode")
    branch_index = lax.axis_index("branch")
    base_index = 2 * branch_index
    first_pair = join_pair(leaves[0], leaves[1], join_order[base_index])
    second_pair = join_pair(leaves[2], leaves[3], join_order[base_index + 1])
    first_pair, second_pair = (
        lax.all_to_all(
            split_rows(first_pair, blocks), "mode", split_axis=2, concat_axis=1, tiled=True
        ),
        lax.all_to_all(
            split_rows(second_pair, blocks), "mode", split_axis=2, concat_axis=1, tiled=True
        ),
    )
    first_pair = merge_rows(first_pair)
    second_pair = merge_rows(second_pair)
    middle = join_pair(first_pair, second_pair, join_order[4 + branch_index])
    middle = merge_rows(
        lax.all_to_all(split_rows(middle, blocks), "mode", split_axis=2, concat_axis=1, tiled=True)
    )
    width = middle.shape[3]
    half_rows = width // 2
    chosen = jnp.where(
        slice_values[None, :, None, None] == 1, boundary[1][:, None], boundary[0][:, None]
    )
    top_order = join_order[-1]
    partner = from_partner(middle, "branch", 0)
    is_first = branch_index == 0
    upper = jnp.where(is_first, middle, partner)
    lower = jnp.where(is_first, partner, middle)
    leading = jnp.where(top_order == 1, lower, upper)
    trailing = jnp.where(top_order == 1, upper, lower)
    leading = lax.dynamic_slice_in_dim(leading, branch_index * half_rows, half_rows, 2)
    top_half = complex_product(leading, trailing)
    amplitudes = complex_sums(top_half, chosen)
    return amplitudes


def solution(mesh):
    in_specs = (P("branch", None, ("cuts", "mode"), None, None), P(), P(("cuts", "mode")), P())
    out_specs = P(None, ("cuts", "mode"), "branch", None)
    return jax.shard_map(
        per_device, mesh=mesh, in_specs=in_specs, out_specs=out_specs, check_vma=False
    )
```

profile of v0, /device:TPU:9, one launch (start us, length us, event | category | flops | bytes accessed | tf_op | source)
XLA Modules:
  0.0 194.1 jit_solution(156778789101351986)
XLA Ops:
  0.0 5.7 %slice_bitcast_fusion = (bf16[2,2,512,512]{3,2,1,0:T(8,128)(2,1)}, bf16[2,2,512,512]{3,2,1,0:T(8,128)(2,1)S(1)}, bf16[2,2,512,512]{3,2,1,0:T(8,128)(2,1)}, bf16[2,2,512,512]{3,2,1,0:T(8,128)(2,1)}) fusion(bf16[4,2,2,512,512]{4,3,2,1,0:T(8,128)(2,1)} %param.10), kind=kLoop, calls=%fused_computation.127 | loop fusion | bytes 16777216 | tf_op jit(solution)/shard_map/squeeze | solution.py:53
  7.0 6.6 %conditional.7 = (bf16[2,2,512,512]{3,2,1,0:T(8,128)(2,1)}) conditional(s32[]{:T(128)} %bitcast.45, (bf16[2,2,512,512]{3,2,1,0:T(8,128)(2,1)}, bf16[2,2,512,512]{3,2,1,0:T(8,128)(2,1)}) %tuple.34, (bf16[2,2,512,512]{3,2,1,0:T(8,128)(2,1)}, bf16[2,2,512,512]{3,2,1,0:T(8,128)(2,1)}) %tuple.35), branch_computations={%region_2.0_spmd, %region_3.0_spmd} | conditional | flops 2150629376 | bytes 39845952
  7.1 2.4 %fusion.36 = f32[2,512,512]{2,1,0:T(8,128)S(1)} fusion(bf16[2,2,512,512]{3,2,1,0:T(8,128)(2,1)} %get-tuple-element.49, bf16[2,2,512,512]{3,2,1,0:T(8,128)(2,1)} %get-tuple-element.48), kind=kOutput, calls=%fused_computation.45 | convolution fusion | flops 536870912 | bytes 4194304 | tf_op jit(solution)/shard_map/cond/branch_0_fun/bij,bjk->bik/dot_general | solution.py:18
  11.3 0.7 subtract_bitcast_fusion.2
  12.1 1.6 pad_maximum_fusion.2
  13.6 3.2 %copy.11 = bf16[2,2,8,64,512]{4,3,1,0,2:T(8,128)(2,1)} copy(bf16[2,2,8,64,512]{4,3,2,1,0:T(8,128)(2,1)} %bitcast.213) | data formatting | bytes 4194304 | tf_op jit(solution)/shard_map/reshape | solution.py:38
  16.8 5.7 %all-to-all-start.1 = ((bf16[2,2,8,64,512]{4,3,1,0,2:T(8,128)(2,1)}), bf16[2,2,8,64,512]{4,3,1,0,2:T(8,128)(2,1)}, u32[]{:S(2)}, u32[]{:S(2)}) async-start(bf16[2,2,8,64,512]{4,3,1,0,2:T(8,128)(2,1)} %copy.11), calls=%async_computation.1 | async-start | bytes 4194304 | tf_op jit(solution)/shard_map/all_to_all | solution.py:58
  23.1 4.5 %conditional.6 = (bf16[2,2,512,512]{3,2,1,0:T(8,128)(2,1)S(1)}) conditional(s32[]{:T(128)} %bitcast.38, (bf16[2,2,512,512]{3,2,1,0:T(8,128)(2,1)}, bf16[2,2,512,512]{3,2,1,0:T(8,128)(2,1)S(1)}) %tuple.32, (bf16[2,2,512,512]{3,2,1,0:T(8,128)(2,1)S(1)}, bf16[2,2,512,512]{3,2,1,0:T(8,128)(2,1)}) %tuple.33), branch_computations={%region_0.0_spmd, %region_1.0_spmd} | conditional | flops 2150629376 | bytes 31457316
  23.2 2.1 %fusion.18 = f32[2,512,512]{2,1,0:T(8,128)S(1)} fusion(bf16[2,2,512,512]{3,2,1,0:T(8,128)(2,1)} %get-tuple-element.47, bf16[2,2,512,512]{3,2,1,0:T(8,128)(2,1)S(1)} %get-tuple-element.46), kind=kOutput, calls=%fused_computation.24 | convolution fusion | flops 536870912 | bytes 4194304 | tf_op jit(solution)/shard_map/cond/branch_1_fun/bij,bjk->bik/dot_general | solution.py:18
  27.6 1.5 copy.9
  29.2 39.9 %all-to-all-done.1 = bf16[2,2,8,64,512]{4,3,1,0,2:T(8,128)(2,1)} async-done(((bf16[2,2,8,64,512]{4,3,1,0,2:T(8,128)(2,1)}), bf16[2,2,8,64,512]{4,3,1,0,2:T(8,128)(2,1)}, u32[]{:S(2)}, u32[]{:S(2)}) %all-to-all-start.1) | async-done | bytes 2097184 | tf_op jit(solution)/shard_map/all_to_all | solution.py:58
  69.0 5.6 %all-to-all-start = ((bf16[2,2,8,64,512]{4,3,1,0,2:T(8,128)(2,1)}), bf16[2,2,8,64,512]{4,3,1,0,2:T(8,128)(2,1)}, u32[]{:S(2)}, u32[]{:S(2)}) async-start(bf16[2,2,8,64,512]{4,3,1,0,2:T(8,128)(2,1)} %copy.9), calls=%async_computation | async-start | bytes 4194304 | tf_op jit(solution)/shard_map/all_to_all | solution.py:55
  75.4 1.8 copy.12
  77.2 43.9 %all-to-all-done = bf16[2,2,8,64,512]{4,3,1,0,2:T(8,128)(2,1)} async-done(((bf16[2,2,8,64,512]{4,3,1,0,2:T(8,128)(2,1)}), bf16[2,2,8,64,512]{4,3,1,0,2:T(8,128)(2,1)}, u32[]{:S(2)}, u32[]{:S(2)}) %all-to-all-start) | async-done | bytes 2097184 | tf_op jit(solution)/shard_map/all_to_all | solution.py:55
  121.1 1.8 copy.10
  122.9 3.3 %conditional.8 = (bf16[2,2,512,512]{3,2,1,0:T(8,128)(2,1)S(1)}) conditional(s32[]{:T(128)} %bitcast.37, (bf16[2,2,512,512]{3,2,1,0:T(8,128)(2,1)S(1)}, bf16[2,2,512,512]{3,2,1,0:T(8,128)(2,1)S(1)}) %tuple.55, (bf16[2,2,512,512]{3,2,1,0:T(8,128)(2,1)S(1)}, bf16[2,2,512,512]{3,2,1,0:T(8,128)(2,1)S(1)}) %tuple.56), branch_computations={%region_4.0_spmd, %region_5.0_spmd} | conditional | flops 2150629376 | bytes 23068680
  123.6 0.7 add_bitcast_fusion.4
  126.4 52.0 %all_to_all.45 = bf16[2,2,8,64,512]{4,3,1,0,2:T(8,128)(2,1)S(1)} all-to-all(bf16[2,2,8,64,512]{4,3,1,0,2:T(8,128)(2,1)S(1)} %copy.13), channel_id=1, replica_groups=mesh['cuts'=2,'mode'=8,'branch'=2] {'mode'}, dimensions={2} | all-to-all | bytes 4194304 | tf_op jit(solution)/shard_map/all_to_all | solution.py:66
  178.4 1.5 copy.14
  179.9 2.1 %collective-permute-start = (bf16[2,2,512,512]{3,2,1,0:T(8,128)(2,1)}, bf16[2,2,512,512]{3,2,1,0:T(8,128)(2,1)}, u32[]{:S(2)}, u32[]{:S(2)}) collective-permute-start(bf16[2,2,512,512]{3,2,1,0:T(8,128)(2,1)} %bitcast.59), channel_id=1, source_target_pairs={{0,1},{1,0},{2,3},{3,2},{4,5},{5,4},{6,7},{7,6},{8,9},{9,8},{10,11... | collective-permute-start | bytes 6291464 | tf_op jit(solution)/shard_map/ppermute | solution.py:10
  182.6 1.7 slice_bitcast_fusion.9
  184.6 1.5 collective-permute-done
  186.1 2.6 %broadcast_select_fusion.3 = (bf16[2,2,512,512]{3,2,1,0:T(8,128)(2,1)S(1)}, bf16[2,2,512,512]{3,2,1,0:T(8,128)(2,1)S(1)}, bf16[2,2,512,512]{3,2,1,0:T(8,128)(2,1)S(1)}) fusion(pred[]{:T(512)} %bitcast.36, bf16[2,2,512,512]{3,2,1,0:T(8,128)(2,1)} %collective-permute-done, bf16[2,2,512,512]{3,2,1,0:T(8,128)(2,1)} %bitcast.59, pred[]{:T(512)S(6)} %eq.28), kind=kLoop, calls=%fused_computation.134 | loop fusion | flops 3145728 | bytes 10485762 | tf_op jit(solution)/shard_map/jit(_where)/select_n | solution.py:79
  192.6 1.5 pad_maximum_fusion.6
  (33 shorter events, 11.4 us)
Async XLA Ops:
  0.0 5.7 %copy-start.6 = (s32[7]{0:T(128)S(1)}, s32[7]{0:T(128)}, u32[]{:S(2)}) copy-start(s32[7]{0:T(128)} %param.11) | copy-start | bytes 88
  7.0 2.4 %copy-start.2 = (bf16[2,2,512,512]{3,2,1,0:T(8,128)(2,1)S(1)}, bf16[2,2,512,512]{3,2,1,0:T(8,128)(2,1)}, u32[]{:S(2)}) copy-start(bf16[2,2,512,512]{3,2,1,0:T(8,128)(2,1)} %get-tuple-element.49) | copy-start | bytes 6291460 | tf_op jit(solution)/shard_map/conditional.1
  7.1 2.8 %copy-start.4 = (bf16[2,2,512,512]{3,2,1,0:T(8,128)(2,1)S(1)}, bf16[2,2,512,512]{3,2,1,0:T(8,128)(2,1)}, u32[]{:S(2)}) copy-start(bf16[2,2,512,512]{3,2,1,0:T(8,128)(2,1)} %get-tuple-element.48) | copy-start | bytes 6291460 | tf_op jit(solution)/shard_map/conditional.1
  16.8 52.2 %all-to-all-start.1 = ((bf16[2,2,8,64,512]{4,3,1,0,2:T(8,128)(2,1)}), bf16[2,2,8,64,512]{4,3,1,0,2:T(8,128)(2,1)}, u32[]{:S(2)}, u32[]{:S(2)}) async-start(bf16[2,2,8,64,512]{4,3,1,0,2:T(8,128)(2,1)} %copy.11), calls=%async_computation.1 | async-start | bytes 4194304 | tf_op jit(solution)/shard_map/all_to_all | solution.py:58
  23.2 2.1 %copy-start.1 = (bf16[2,2,512,512]{3,2,1,0:T(8,128)(2,1)S(1)}, bf16[2,2,512,512]{3,2,1,0:T(8,128)(2,1)}, u32[]{:S(2)}) copy-start(bf16[2,2,512,512]{3,2,1,0:T(8,128)(2,1)} %get-tuple-element.47) | copy-start | bytes 6291460 | tf_op jit(solution)/shard_map/conditional
  69.0 52.0 %all-to-all-start = ((bf16[2,2,8,64,512]{4,3,1,0,2:T(8,128)(2,1)}), bf16[2,2,8,64,512]{4,3,1,0,2:T(8,128)(2,1)}, u32[]{:S(2)}, u32[]{:S(2)}) async-start(bf16[2,2,8,64,512]{4,3,1,0,2:T(8,128)(2,1)} %copy.9), calls=%async_computation | async-start | bytes 4194304 | tf_op jit(solution)/shard_map/all_to_all | solution.py:55
  178.4 4.2 %copy-start.7 = (s32[2]{0:T(128)S(1)}, s32[2]{0:T(128)}, u32[]{:S(2)}) copy-start(s32[2]{0:T(128)} %param.12) | copy-start | bytes 28
  179.9 6.2 %collective-permute-start = (bf16[2,2,512,512]{3,2,1,0:T(8,128)(2,1)}, bf16[2,2,512,512]{3,2,1,0:T(8,128)(2,1)}, u32[]{:S(2)}, u32[]{:S(2)}) collective-permute-start(bf16[2,2,512,512]{3,2,1,0:T(8,128)(2,1)} %bitcast.59), channel_id=1, source_target_pairs={{0,1},{1,0},{2,3},{3,2},{4,5},{5,4},{6,7},{7,6},{8,9},{9,8},{10,11... | collective-permute-start | bytes 6291464 | tf_op jit(solution)/shard_map/ppermute | solution.py:10
where the time goes:
time: 196 us; the launch traced here: 194 us
  waiting for transfers between devices  85.3 us (44%)
  blocking collectives  52 us (27%)
  local copies, waits for them, and re-layouts  18.6 us (9%)
  matrix products  15.1 us (8%)
  starting transfers between devices  13.4 us (7%)
  other arithmetic  6.63 us (3%)
  between operations  2.74 us (1%)
    all_to_all x1, blocking collectives, per_device(): lax.all_to_all(split_rows(middle, blocks), 'mode', split_axis=2, concat_a...  52 us
    all_to_all x1, waiting for transfers between devices, per_device(): lax.all_to_all(split_rows(first_pair, blocks), 'mode', split_axis=2, conc...  43.9 us
    all_to_all x1, waiting for transfers between devices, per_device(): lax.all_to_all(split_rows(second_pair, blocks), 'mode', split_axis=2, con...  39.9 us
    dot_general x5, matrix products, complex_sums(): jnp.einsum(spec, left_op[0], right_op[1], preferred_element_type=jnp.floa...  6.06 us
    squeeze x1, local copies, waits for them, and re-layouts, per_device(): second_pair = join_pair(leaves[2], leaves[3], join_order[base_index + 1])  5.73 us
    all_to_all x1, starting transfers between devices, per_device(): lax.all_to_all(split_rows(second_pair, blocks), 'mode', split_axis=2, con...  5.72 us
    all_to_all x1, starting transfers between devices, per_device(): lax.all_to_all(split_rows(first_pair, blocks), 'mode', split_axis=2, conc...  5.64 us
    reshape x3, local copies, waits for them, and re-layouts, split_rows(): tensor.reshape(shape[0], shape[1], blocks, shape[2] // blocks, shape[3])  4.91 us
  transfers between devices with their start and end apart: 3, of which 3 were waited for; matrix products, arithmetic and copies ran while one was open for 5% of the time, Pallas kernels for 0%

commit v1 on v0

--- a/solution.py
+++ b/solution.py
@@ -38,33 +38,38 @@
     return tensor.reshape(shape[0], shape[1], blocks, shape[2] // blocks, shape[3])
 
 
-def merge_rows(tensor):
+def grouped_exchange(tensor, groups):
+    size = len(groups[0])
     shape = tensor.shape
-    width = shape[4]
-    total_rows = shape[1] * shape[2] * shape[3]
-    return tensor.reshape(shape[0], total_rows // width, width, width)
+    batch, width = shape[1], shape[3]
+    viewed = tensor.reshape(shape[0], batch, size, batch, width // (size * batch), width)
+    viewed = jnp.transpose(viewed, (2, 0, 3, 1, 4, 5))
+    moved = lax.all_to_all(viewed, "mode", 0, 0, axis_index_groups=groups, tiled=True)
+    return jnp.transpose(moved, (1, 2, 0, 3, 4, 5)).reshape(shape)
+
+
+def full_exchange(tensor, halves):
+    blocks = lax.axis_size("mode")
+    shape = tensor.shape
+    batch, width = shape[1], shape[3]
+    moved = lax.all_to_all(split_rows(tensor, blocks), "mode", split_axis=2, concat_axis=1, tiled=True)
+    moved = moved.reshape(shape[0], halves, blocks // halves, batch, width // blocks, width)
+    return jnp.transpose(moved, (0, 2, 3, 1, 4, 5)).reshape(shape)
 
 
 def per_device(leaves, join_order, slice_values, boundary):
     blocks = lax.axis_size("mode")
+    halves = leaves.shape[2]
+    size = blocks // halves
+    groups = [[half * size + place for place in range(size)] for half in range(halves)]
     branch_index = lax.axis_index("branch")
     base_index = 2 * branch_index
     first_pair = join_pair(leaves[0], leaves[1], join_order[base_index])
     second_pair = join_pair(leaves[2], leaves[3], join_order[base_index + 1])
-    first_pair, second_pair = (
-        lax.all_to_all(
-            split_rows(first_pair, blocks), "mode", split_axis=2, concat_axis=1, tiled=True
-        ),
-        lax.all_to_all(
-            split_rows(second_pair, blocks), "mode", split_axis=2, concat_axis=1, tiled=True
-        ),
-    )
-    first_pair = merge_rows(first_pair)
-    second_pair = merge_rows(second_pair)
+    first_pair = grouped_exchange(first_pair, groups)
+    second_pair = grouped_exchange(second_pair, groups)
     middle = join_pair(first_pair, second_pair, join_order[4 + branch_index])
-    middle = merge_rows(
-        lax.all_to_all(split_rows(middle, blocks), "mode", split_axis=2, concat_axis=1, tiled=True)
-    )
+    middle = full_exchange(middle, halves)
     width = middle.shape[3]
     half_rows = width // 2
     chosen = jnp.where(

time: 196 us -> 149 us (0.76)
  waiting for transfers between devices: 85.3 us -> 42.1 us
  starting transfers between devices: 13.4 us -> 11 us
    all_to_all x2, waiting for transfers between devices: 83.8 us -> 40.6 us  [grouped_exchange(): lax.all_to_all(viewed, 'mode', 0, 0, axis_index_groups=groups, tiled=True)]
    transpose x0 -> x3, local copies, waits for them, and re-layouts: none -> 6.24 us  [the longest x2 4.7 us: grouped_exchange(): viewed = jnp.transpose(viewed, (2, 0, 3, 1, 4, 5))]
    reshape x3 -> x1, local copies, waits for them, and re-layouts: 4.91 us -> 0.22 us  [split_rows(): tensor.reshape(shape[0], shape[1], blocks, shape[2] // blocks, shape[3])]
    all_to_all x2, starting transfers between devices: 11.4 us -> 8.87 us  [grouped_exchange(): lax.all_to_all(viewed, 'mode', 0, 0, axis_index_groups=groups, tiled=True)]
    all_to_all x3 -> x2, local copies, waits for them, and re-layouts: 5.15 us -> 3.61 us  [grouped_exchange(): lax.all_to_all(viewed, 'mode', 0, 0, axis_index_groups=groups, tiled=True)]
  transfers between devices with their start and end apart: 3 -> 3, of which waited for: 3 -> 3; matrix products, arithmetic and copies ran while one was open for 5% -> 7% of each run, Pallas kernels for 0% -> 0%
where the time goes in v1:
time: 149 us; the launch traced here: 147 us
  blocking collectives  50.9 us (34%)
  waiting for transfers between devices  42.1 us (28%)
  local copies, waits for them, and re-layouts  18.6 us (12%)
  matrix products  15.1 us (10%)
  starting transfers between devices  11 us (7%)
  other arithmetic  6.63 us (4%)
  between operations  2.74 us (2%)
    all_to_all x1, blocking collectives, full_exchange(): lax.all_to_all(split_rows(tensor, blocks), 'mode', split_axis=2, concat_a...  50.9 us
    all_to_all x2, waiting for transfers between devices, grouped_exchange(): lax.all_to_all(viewed, 'mode', 0, 0, axis_index_groups=groups, tiled=True)  40.6 us
    all_to_all x2, starting transfers between devices, grouped_exchange(): lax.all_to_all(viewed, 'mode', 0, 0, axis_index_groups=groups, tiled=True)  8.87 us
    dot_general x5, matrix products, complex_sums(): jnp.einsum(spec, left_op[0], right_op[1], preferred_element_type=jnp.floa...  6.06 us
    squeeze x1, local copies, waits for them, and re-layouts, per_device(): second_pair = join_pair(leaves[2], leaves[3], join_order[base_index + 1])  5.73 us
    transpose x2, local copies, waits for them, and re-layouts, grouped_exchange(): viewed = jnp.transpose(viewed, (2, 0, 3, 1, 4, 5))  4.7 us
    all_to_all x2, local copies, waits for them, and re-layouts, grouped_exchange(): lax.all_to_all(viewed, 'mode', 0, 0, axis_index_groups=groups, tiled=True)  3.61 us
    another operation x4, other arithmetic, complex_sums(): return jnp.stack([real_part, imag_part])  3.45 us
  transfers between devices with their start and end apart: 3, of which 3 were waited for; matrix products, arithmetic and copies ran while one was open for 7% of the time, Pallas kernels for 0%

profile of v1, /device:TPU:9, one launch (start us, length us, event | category | flops | bytes accessed | tf_op | source)
XLA Modules:
  0.0 147.4 jit_solution(13498438580887627510)
XLA Ops:
  0.0 5.7 %slice_bitcast_fusion = (bf16[2,2,512,512]{3,2,1,0:T(8,128)(2,1)}, bf16[2,2,512,512]{3,2,1,0:T(8,128)(2,1)S(1)}, bf16[2,2,512,512]{3,2,1,0:T(8,128)(2,1)}, bf16[2,2,512,512]{3,2,1,0:T(8,128)(2,1)}) fusion(bf16[4,2,2,512,512]{4,3,2,1,0:T(8,128)(2,1)} %param.10), kind=kLoop, calls=%fused_computation.127 | loop fusion | bytes 16777216 | tf_op jit(solution)/shard_map/squeeze | solution.py:68
  7.0 6.6 %conditional.7 = (bf16[2,2,512,512]{3,2,1,0:T(8,128)(2,1)}) conditional(s32[]{:T(128)} %bitcast.45, (bf16[2,2,512,512]{3,2,1,0:T(8,128)(2,1)}, bf16[2,2,512,512]{3,2,1,0:T(8,128)(2,1)}) %tuple.34, (bf16[2,2,512,512]{3,2,1,0:T(8,128)(2,1)}, bf16[2,2,512,512]{3,2,1,0:T(8,128)(2,1)}) %tuple.35), branch_computations={%region_2.0_spmd, %region_3.0_spmd} | conditional | flops 2150629376 | bytes 39845952
  7.1 2.4 %fusion.54 = f32[2,512,512]{2,1,0:T(8,128)S(1)} fusion(bf16[2,2,512,512]{3,2,1,0:T(8,128)(2,1)} %get-tuple-element.51, bf16[2,2,512,512]{3,2,1,0:T(8,128)(2,1)} %get-tuple-element.50), kind=kOutput, calls=%fused_computation.66 | convolution fusion | flops 536870912 | bytes 4194304 | tf_op jit(solution)/shard_map/cond/branch_1_fun/bij,bjk->bik/dot_general | solution.py:18
  11.3 0.7 subtract_bitcast_fusion.3
  12.1 1.6 %pad_maximum_fusion.3 = bf16[2,2,512,512]{3,2,1,0:T(8,128)(2,1)} fusion(bf16[1,2,512,512]{3,2,1,0:T(8,128)(2,1)S(1)} %add_bitcast_fusion.3, bf16[1,2,512,512]{3,2,1,0:T(8,128)(2,1)S(1)} %subtract_bitcast_fusion.3), kind=kLoop, calls=%fused_computation.63 | loop fusion | flops 1048576 | bytes 4194304 | tf_op jit(solution)/shard_map/cond/branch_1_fun/stack | solution.py:21
  13.6 3.2 %copy.19 = bf16[4,2,2,2,64,512]{5,4,3,2,1,0:T(8,128)(2,1)} copy(bf16[4,2,2,2,64,512]{5,4,2,0,3,1:T(8,128)(2,1)} %bitcast.215) | data formatting | bytes 4194304 | tf_op jit(solution)/shard_map/transpose | solution.py:46
  16.8 4.4 %all-to-all-start.1 = ((bf16[4,2,2,2,64,512]{5,4,3,2,1,0:T(8,128)(2,1)}), bf16[4,2,2,2,64,512]{5,4,3,2,1,0:T(8,128)(2,1)}, u32[]{:S(2)}, u32[]{:S(2)}) async-start(bf16[4,2,2,2,64,512]{5,4,3,2,1,0:T(8,128)(2,1)} %copy.19), calls=%async_computation.1 | async-start | bytes 4194304 | tf_op jit(solution)/shard_map/all_to_all | solution.py:47
  21.9 4.5 %conditional.6 = (bf16[2,2,512,512]{3,2,1,0:T(8,128)(2,1)S(1)}) conditional(s32[]{:T(128)} %bitcast.38, (bf16[2,2,512,512]{3,2,1,0:T(8,128)(2,1)}, bf16[2,2,512,512]{3,2,1,0:T(8,128)(2,1)S(1)}) %tuple.32, (bf16[2,2,512,512]{3,2,1,0:T(8,128)(2,1)S(1)}, bf16[2,2,512,512]{3,2,1,0:T(8,128)(2,1)}) %tuple.33), branch_computations={%region_0.0_spmd, %region_1.0_spmd} | conditional | flops 2150629376 | bytes 31457316
  21.9 2.1 %fusion = f32[2,512,512]{2,1,0:T(8,128)S(1)} fusion(bf16[2,2,512,512]{3,2,1,0:T(8,128)(2,1)S(1)} %get-tuple-element.45, bf16[2,2,512,512]{3,2,1,0:T(8,128)(2,1)} %get-tuple-element.44), kind=kOutput, calls=%fused_computation.3 | convolution fusion | flops 536870912 | bytes 4194304 | tf_op jit(solution)/shard_map/cond/branch_0_fun/bij,bjk->bik/dot_general | solution.py:18
  26.3 1.5 %copy.17 = bf16[4,2,2,2,64,512]{5,4,3,2,1,0:T(8,128)(2,1)} copy(bf16[4,2,2,2,64,512]{5,4,2,0,3,1:T(8,128)(2,1)S(1)} %bitcast.216) | data formatting | bytes 4194304 | tf_op jit(solution)/shard_map/transpose | solution.py:46
  27.9 18.4 %all-to-all-done.1 = bf16[4,2,2,2,64,512]{5,4,3,2,1,0:T(8,128)(2,1)} async-done(((bf16[4,2,2,2,64,512]{5,4,3,2,1,0:T(8,128)(2,1)}), bf16[4,2,2,2,64,512]{5,4,3,2,1,0:T(8,128)(2,1)}, u32[]{:S(2)}, u32[]{:S(2)}) %all-to-all-start.1) | async-done | bytes 2097184 | tf_op jit(solution)/shard_map/all_to_all | solution.py:47
  46.3 4.4 %all-to-all-start = ((bf16[4,2,2,2,64,512]{5,4,3,2,1,0:T(8,128)(2,1)}), bf16[4,2,2,2,64,512]{5,4,3,2,1,0:T(8,128)(2,1)}, u32[]{:S(2)}, u32[]{:S(2)}) async-start(bf16[4,2,2,2,64,512]{5,4,3,2,1,0:T(8,128)(2,1)} %copy.17), calls=%async_computation | async-start | bytes 4194304 | tf_op jit(solution)/shard_map/all_to_all | solution.py:47
  51.4 1.8 %copy.20 = bf16[4,2,2,2,64,512]{5,4,3,0,2,1:T(8,128)(2,1)S(1)} copy(bf16[4,2,2,2,64,512]{5,4,3,2,1,0:T(8,128)(2,1)} %all-to-all-done.1) | data formatting | bytes 4194304 | tf_op jit(solution)/shard_map/all_to_all | solution.py:47
  53.2 22.2 %all-to-all-done = bf16[4,2,2,2,64,512]{5,4,3,2,1,0:T(8,128)(2,1)} async-done(((bf16[4,2,2,2,64,512]{5,4,3,2,1,0:T(8,128)(2,1)}), bf16[4,2,2,2,64,512]{5,4,3,2,1,0:T(8,128)(2,1)}, u32[]{:S(2)}, u32[]{:S(2)}) %all-to-all-start) | async-done | bytes 2097184 | tf_op jit(solution)/shard_map/all_to_all | solution.py:47
  75.4 1.8 %copy.18 = bf16[4,2,2,2,64,512]{5,4,3,0,2,1:T(8,128)(2,1)S(1)} copy(bf16[4,2,2,2,64,512]{5,4,3,2,1,0:T(8,128)(2,1)} %all-to-all-done) | data formatting | bytes 4194304 | tf_op jit(solution)/shard_map/all_to_all | solution.py:47
  77.3 3.3 %conditional.8 = (bf16[2,2,512,512]{3,2,1,0:T(8,128)(2,1)S(1)}) conditional(s32[]{:T(128)} %bitcast.37, (bf16[2,2,512,512]{3,2,1,0:T(8,128)(2,1)S(1)}, bf16[2,2,512,512]{3,2,1,0:T(8,128)(2,1)S(1)}) %tuple.55, (bf16[2,2,512,512]{3,2,1,0:T(8,128)(2,1)S(1)}, bf16[2,2,512,512]{3,2,1,0:T(8,128)(2,1)S(1)}) %tuple.56), branch_computations={%region_4.0_spmd, %region_5.0_spmd} | conditional | flops 2150629376 | bytes 23068680
  78.0 0.7 add_bitcast_fusion.4
  80.7 50.9 %all_to_all.25 = bf16[2,2,8,64,512]{4,3,1,0,2:T(8,128)(2,1)S(1)} all-to-all(bf16[2,2,8,64,512]{4,3,1,0,2:T(8,128)(2,1)S(1)} %copy.21), channel_id=1, replica_groups=mesh['cuts'=2,'mode'=8,'branch'=2] {'mode'}, dimensions={2} | all-to-all | bytes 4194304 | tf_op jit(solution)/shard_map/all_to_all | solution.py:55
  131.7 1.5 %copy.23 = bf16[2,4,2,2,64,512]{5,4,3,2,1,0:T(8,128)(2,1)} copy(bf16[2,4,2,2,64,512]{5,4,2,0,1,3:T(8,128)(2,1)S(1)} %bitcast.218) | data formatting | bytes 4194304 | tf_op jit(solution)/shard_map/transpose | solution.py:57
  133.2 2.1 %collective-permute-start = (bf16[2,2,512,512]{3,2,1,0:T(8,128)(2,1)}, bf16[2,2,512,512]{3,2,1,0:T(8,128)(2,1)}, u32[]{:S(2)}, u32[]{:S(2)}) collective-permute-start(bf16[2,2,512,512]{3,2,1,0:T(8,128)(2,1)} %bitcast.60), channel_id=1, source_target_pairs={{0,1},{1,0},{2,3},{3,2},{4,5},{5,4},{6,7},{7,6},{8,9},{9,8},{10,11... | collective-permute-start | bytes 6291464 | tf_op jit(solution)/shard_map/ppermute | solution.py:10
  135.9 1.7 %slice_bitcast_fusion.9 = (bf16[2,512,512]{2,1,0:T(8,128)(2,1)S(1)}, bf16[2,512,512]{2,1,0:T(8,128)(2,1)S(1)}) fusion(bf16[2,2,512,512]{3,2,1,0:T(8,128)(2,1)} %param.13), kind=kLoop, calls=%fused_computation.149 | loop fusion | bytes 4194304 | tf_op jit(solution)/shard_map/jit(_where)/broadcast_in_dim | solution.py:75
  137.9 1.5 %collective-permute-done = bf16[2,2,512,512]{3,2,1,0:T(8,128)(2,1)} collective-permute-done((bf16[2,2,512,512]{3,2,1,0:T(8,128)(2,1)}, bf16[2,2,512,512]{3,2,1,0:T(8,128)(2,1)}, u32[]{:S(2)}, u32[]{:S(2)}) %collective-permute-start) | collective-permute-done | bytes 2097184 | tf_op jit(solution)/shard_map/ppermute | solution.py:10
  139.4 2.6 %broadcast_select_fusion.3 = (bf16[2,2,512,512]{3,2,1,0:T(8,128)(2,1)S(1)}, bf16[2,2,512,512]{3,2,1,0:T(8,128)(2,1)S(1)}, bf16[2,2,512,512]{3,2,1,0:T(8,128)(2,1)S(1)}) fusion(pred[]{:T(512)} %bitcast.36, bf16[2,2,512,512]{3,2,1,0:T(8,128)(2,1)} %collective-permute-done, bf16[2,2,512,512]{3,2,1,0:T(8,128)(2,1)} %bitcast.60, pred[]{:T(512)S(6)} %eq.28), kind=kLoop, calls=%fused_computation.134 | loop fusion | flops 3145728 | bytes 10485762 | tf_op jit(solution)/shard_map/jit(_where)/select_n | solution.py:84
  145.9 1.5 %pad_maximum_fusion.6 = f32[2,2,256,512]{3,2,1,0:T(8,128)} fusion(f32[1,2,256,512]{3,2,1,0:T(8,128)S(1)} %fusion.108, f32[1,2,256,512]{3,2,1,0:T(8,128)S(1)} %fusion.109), kind=kLoop, calls=%fused_computation.126 | loop fusion | flops 524288 | bytes 4194304 | tf_op jit(solution)/shard_map/stack | solution.py:21
  (33 shorter events, 11.4 us)
Async XLA Ops:
  0.0 5.7 %copy-start.6 = (s32[7]{0:T(128)S(1)}, s32[7]{0:T(128)}, u32[]{:S(2)}) copy-start(s32[7]{0:T(128)} %param.11) | copy-start | bytes 88
  7.1 2.4 %copy-start.3 = (bf16[2,2,512,512]{3,2,1,0:T(8,128)(2,1)S(1)}, bf16[2,2,512,512]{3,2,1,0:T(8,128)(2,1)}, u32[]{:S(2)}) copy-start(bf16[2,2,512,512]{3,2,1,0:T(8,128)(2,1)} %get-tuple-element.50) | copy-start | bytes 6291460 | tf_op jit(solution)/shard_map/conditional.1
  7.1 2.8 %copy-start.5 = (bf16[2,2,512,512]{3,2,1,0:T(8,128)(2,1)S(1)}, bf16[2,2,512,512]{3,2,1,0:T(8,128)(2,1)}, u32[]{:S(2)}) copy-start(bf16[2,2,512,512]{3,2,1,0:T(8,128)(2,1)} %get-tuple-element.51) | copy-start | bytes 6291460 | tf_op jit(solution)/shard_map/conditional.1
  16.8 29.5 %all-to-all-start.1 = ((bf16[4,2,2,2,64,512]{5,4,3,2,1,0:T(8,128)(2,1)}), bf16[4,2,2,2,64,512]{5,4,3,2,1,0:T(8,128)(2,1)}, u32[]{:S(2)}, u32[]{:S(2)}) async-start(bf16[4,2,2,2,64,512]{5,4,3,2,1,0:T(8,128)(2,1)} %copy.19), calls=%async_computation.1 | async-start | bytes 4194304 | tf_op jit(solution)/shard_map/all_to_all | solution.py:47
  21.9 2.1 %copy-start = (bf16[2,2,512,512]{3,2,1,0:T(8,128)(2,1)S(1)}, bf16[2,2,512,512]{3,2,1,0:T(8,128)(2,1)}, u32[]{:S(2)}) copy-start(bf16[2,2,512,512]{3,2,1,0:T(8,128)(2,1)} %get-tuple-element.44) | copy-start | bytes 6291460 | tf_op jit(solution)/shard_map/conditional
  46.3 29.2 %all-to-all-start = ((bf16[4,2,2,2,64,512]{5,4,3,2,1,0:T(8,128)(2,1)}), bf16[4,2,2,2,64,512]{5,4,3,2,1,0:T(8,128)(2,1)}, u32[]{:S(2)}, u32[]{:S(2)}) async-start(bf16[4,2,2,2,64,512]{5,4,3,2,1,0:T(8,128)(2,1)} %copy.17), calls=%async_computation | async-start | bytes 4194304 | tf_op jit(solution)/shard_map/all_to_all | solution.py:47
  131.7 4.3 %copy-start.7 = (s32[2]{0:T(128)S(1)}, s32[2]{0:T(128)}, u32[]{:S(2)}) copy-start(s32[2]{0:T(128)} %param.12) | copy-start | bytes 28
  133.2 6.2 %collective-permute-start = (bf16[2,2,512,512]{3,2,1,0:T(8,128)(2,1)}, bf16[2,2,512,512]{3,2,1,0:T(8,128)(2,1)}, u32[]{:S(2)}, u32[]{:S(2)}) collective-permute-start(bf16[2,2,512,512]{3,2,1,0:T(8,128)(2,1)} %bitcast.60), channel_id=1, source_target_pairs={{0,1},{1,0},{2,3},{3,2},{4,5},{5,4},{6,7},{7,6},{8,9},{9,8},{10,11... | collective-permute-start | bytes 6291464 | tf_op jit(solution)/shard_map/ppermute | solution.py:10

commit v2 on v0

v2 whole, which is shorter than its diff:
```python
import functools

import jax
import jax.numpy as jnp
from jax import lax
from jax.experimental import pallas as pl
from jax.experimental.pallas import tpu as pltpu
from jax.sharding import PartitionSpec as P

HBM = pl.BlockSpec(memory_space=pl.ANY)
SMEM = pl.BlockSpec(memory_space=pltpu.SMEM)
VMEM_LIMIT = 40 * 2**20


def complex_dot(left_real, left_imag, right):
    left = jnp.concatenate(
        [
            jnp.concatenate([left_real, -left_imag], axis=1),
            jnp.concatenate([left_imag, left_real], axis=1),
        ],
        axis=0,
    )
    sums = jnp.dot(left, right, preferred_element_type=jnp.float32)
    rows = left_real.shape[0]
    return sums[:rows], sums[rows:]


class Copies:
    def __init__(self, sems):
        self.sems = sems
        self.used = 0

    def start(self, source, target):
        copy = pltpu.make_async_copy(source, target, self.sems.at[self.used])
        self.used += 1
        copy.start()
        return copy


def run_kernel(body, outs, scratch, copies, flops, operands, specs, aliases=None):
    moved = sum(x.size * x.dtype.itemsize for x in outs) + 2**21
    return pl.pallas_call(
        body,
        out_shape=outs,
        in_specs=specs,
        out_specs=[HBM] * len(outs),
        scratch_shapes=list(scratch) + [pltpu.SemaphoreType.DMA((copies,))],
        input_output_aliases=aliases or {},
        compiler_params=pltpu.CompilerParams(vmem_limit_bytes=VMEM_LIMIT),
        cost_estimate=pl.CostEstimate(flops=flops, bytes_accessed=moved, transcendentals=0),
    )(*operands)


class Plan:
    def __init__(self, leaves):
        self.modes = lax.axis_size("mode")
        self.batch = leaves.shape[2]
        self.width = leaves.shape[4]
        self.rows = self.width // self.modes
        self.size = self.modes // self.batch
        self.ways = self.batch
        self.places = self.size // self.ways
        assert self.batch == 2 and lax.axis_size("branch") == 2

    def mode_of(self, high, place, way):
        return (high * self.places + place) * self.ways + way

    def here(self):
        mode = lax.axis_index("mode")
        return mode // self.size, (mode % self.size) // self.ways, mode % self.ways


def first_level(plan, leaves, join_order, role, spans):
    width, batch, rows = plan.width, plan.batch, plan.rows
    lowest, highest = spans[0][0], spans[-1][1]
    total = highest - lowest
    half = width // plan.ways
    chunk_blocks = [(high - low) // rows for low, high in spans]

    def body(order, leaf, *rest):
        outs, (upper, lower, result, sems) = rest[: 2 * len(spans)], rest[2 * len(spans) :]
        copies = Copies(sems)
        branch = lax.axis_index("branch")
        _, _, way = plan.here()
        pair = jnp.where(order[2 * lax.axis_size("branch") + branch] == 1, 1 - role, role)
        swapped = jnp.where(order[2 * branch + pair] == 1, 1, 0)
        first, second = 2 * pair + swapped, 2 * pair + 1 - swapped
        loads = []
        for item in range(batch):
            mine = []
            for place in range(plan.ways):
                target = (way + place) % plan.ways
                mine.append(
                    copies.start(
                        leaf.at[first, :, item, pl.ds(target * half + lowest, total)],
                        upper.at[item, :, place],
                    )
                )
            mine.append(copies.start(leaf.at[second, :, item], lower.at[item]))
            loads.append(mine)
        stores = []
        for item in range(batch):
            for copy in loads[item]:
                copy.wait()
            parts = complex_dot(
                upper[item, 0].reshape(plan.ways * total, width),
                upper[item, 1].reshape(plan.ways * total, width),
                lower[item].reshape(2 * width, width),
            )
            for part in range(2):
                result[item, part] = (
                    parts[part].astype(jnp.bfloat16).reshape(plan.ways, total, width)
                )
            for place in range(plan.ways):
                for index, (low, high) in enumerate(spans):
                    for block in range(chunk_blocks[index]):
                        begin = low - lowest + block * rows
                        stores.append(
                            copies.start(
                                result.at[item, :, place, pl.ds(begin, rows)],
                                outs[2 * index + place].at[:, block, item],
                            )
                        )
        for copy in stores:
            copy.wait()

    outs = [
        jax.ShapeDtypeStruct((2, blocks, batch, rows, width), jnp.bfloat16)
        for blocks in chunk_blocks
        for _ in range(plan.ways)
    ]
    scratch = [
        pltpu.VMEM((batch, 2, plan.ways, total, width), jnp.bfloat16),
        pltpu.VMEM((batch, 2, width, width), jnp.bfloat16),
        pltpu.VMEM((batch, 2, plan.ways, total, width), jnp.bfloat16),
    ]
    copies = batch * (plan.ways + 1) + batch * plan.ways * sum(chunk_blocks)
    flops = 8 * batch * plan.ways * total * width * width
    results = run_kernel(body, outs, scratch, copies, flops, [join_order, leaves], [SMEM, HBM])
    return [results[2 * index : 2 * index + 2] for index in range(len(spans))]


def second_level(plan, left_own, left_way, right_own, right_way, right_places, right_both):
    width, batch, rows, ways, places = plan.width, plan.batch, plan.rows, plan.ways, plan.places
    blocks = left_own.shape[1]
    held = ways * batch * rows
    others = places - 1

    def body(*refs):
        sources = refs[: 4 + 2 * others]
        outs = refs[4 + 2 * others : 4 + 2 * others + ways * batch]
        left, right, result, sems = refs[4 + 2 * others + ways * batch :]
        copies = Copies(sems)
        branch = lax.axis_index("branch")
        high, place, way = plan.here()
        loads = [
            copies.start(sources[0], left.at[:, :, way]),
            copies.start(sources[1], left.at[:, :, 1 - way]),
            copies.start(sources[2], right.at[:, :, place, way]),
            copies.start(sources[3], right.at[:, :, place, 1 - way]),
        ]
        for step in range(1, places):
            other = place ^ step
            loads.append(copies.start(sources[3 + step], right.at[:, :, other, way]))
            loads.append(copies.start(sources[3 + others + step], right.at[:, :, other, 1 - way]))
        for copy in loads:
            copy.wait()
        steps = [(a, b) for a in range(ways) for b in range(batch)]
        stores = []
        for block in range(blocks):
            halves = [
                jnp.concatenate([left[part, block, high ^ a, branch ^ b] for a, b in steps], axis=0)
                for part in range(2)
            ]
            parts = complex_dot(
                halves[0],
                halves[1],
                jnp.concatenate(
                    [right[part, block].reshape(width, width) for part in range(2)], axis=0
                ),
            )
            for part in range(2):
                result[block, part] = (
                    parts[part].astype(jnp.bfloat16).reshape(ways * batch, rows, width)
                )
            for index in range(ways * batch):
                stores.append(copies.start(result.at[block, :, index], outs[index].at[:, block]))
        for copy in stores:
            copy.wait()

    outs = [jax.ShapeDtypeStruct((2, blocks, rows, width), jnp.bfloat16)] * (ways * batch)
    scratch = [
        pltpu.VMEM((2, blocks, ways, batch, rows, width), jnp.bfloat16),
        pltpu.VMEM((2, blocks, places, ways, batch, rows, width), jnp.bfloat16),
        pltpu.VMEM((blocks, 2, ways * batch, rows, width), jnp.bfloat16),
    ]
    copies = 4 + 2 * others + blocks * ways * batch
    operands = [left_own, left_way, right_own, right_way, *right_places, *right_both]
    flops = 8 * blocks * held * width * width
    return run_kernel(body, outs, scratch, copies, flops, operands, [HBM] * len(operands))


def load_operands(plan, copies, order, messages, chunk_blocks, scratch, keep):
    mode = lax.axis_index("mode")
    near, item = (mode // plan.batch) % plan.ways, mode % plan.batch
    top = jnp.where(order[order.shape[0] - 1] == 1, 1, 0)
    steps = [(a, b) for a in range(plan.ways) for b in range(plan.batch)]
    loads = []
    begin = 0
    for chunk, blocks in zip(messages, chunk_blocks):
        for (a, b), message in zip(steps, chunk):
            role = item ^ b ^ top
            loads.append(
                copies.start(message, scratch.at[role, :, pl.ds(begin, blocks), near ^ a])
            )
        begin += blocks
    return loads


def top_operands(plan, scratch, half):
    width = plan.width
    kept = plan.size // 2
    left = [
        scratch[0, part, pl.ds(half * kept, kept)].reshape(width // 2, width) for part in range(2)
    ]
    right = jnp.concatenate([scratch[1, part].reshape(width, width) for part in range(2)], axis=0)
    return left[0], left[1], right


def top_scratch(plan):
    return pltpu.VMEM((2, 2, plan.size, plan.batch, plan.rows, plan.width), jnp.bfloat16)


def top_for_other(plan, join_order, messages):
    flat = [message for chunk in messages for message in chunk]
    count = len(messages[0])
    chunk_blocks = [chunk[0].shape[1] for chunk in messages]
    half_shape = (2, plan.width // 2, plan.width)

    def body(order, *refs):
        sources, (out, operands, result, sems) = refs[: len(flat)], refs[len(flat) :]
        copies = Copies(sems)
        grouped = [sources[i : i + count] for i in range(0, len(flat), count)]
        for copy in load_operands(plan, copies, order, grouped, chunk_blocks, operands, None):
            copy.wait()
        parts = complex_dot(*top_operands(plan, operands, 1 - lax.axis_index("branch")))
        for part in range(2):
            result[part] = parts[part].astype(jnp.bfloat16)
        copies.start(result, out).wait()

    flops = 4 * plan.width**3
    return run_kernel(
        body,
        [jax.ShapeDtypeStruct(half_shape, jnp.bfloat16)],
        [top_scratch(plan), pltpu.VMEM(half_shape, jnp.bfloat16)],
        len(flat) + 1,
        flops,
        [join_order, *flat],
        [SMEM] + [HBM] * len(flat),
    )[0]


def own_amplitudes(plan, join_order, slice_values, boundary, messages):
    flat = [message for chunk in messages for message in chunk]
    count = len(messages[0])
    chunk_blocks = [chunk[0].shape[1] for chunk in messages]
    width = plan.width

    def body(order, values, bound, *refs):
        sources, (out, operands, chosen, result, sems) = refs[: len(flat)], refs[len(flat) :]
        copies = Copies(sems)
        core = lax.axis_index("branch")
        grouped = [sources[i : i + count] for i in range(0, len(flat), count)]
        loads = load_operands(plan, copies, order, grouped, chunk_blocks, operands, None)
        value = jnp.where(values[core] == 1, 1, 0)
        late = copies.start(bound.at[value], chosen)
        for copy in loads:
            copy.wait()
        top = complex_dot(*top_operands(plan, operands, core))
        late.wait()
        parts = complex_dot(
            top[0].astype(jnp.bfloat16),
            top[1].astype(jnp.bfloat16),
            chosen[...].reshape(2 * width, width),
        )
        for part in range(2):
            result[part] = parts[part]
        copies.start(result, out.at[:, core]).wait()

    flops = 8 * plan.width**3
    return run_kernel(
        body,
        [jax.ShapeDtypeStruct((2, plan.batch, width // 2, width), jnp.float32)],
        [
            top_scratch(plan),
            pltpu.VMEM((2, width, width), jnp.bfloat16),
            pltpu.VMEM((2, width // 2, width), jnp.float32),
        ],
        len(flat) + 2,
        flops,
        [join_order, slice_values, boundary, *flat],
        [SMEM, SMEM, HBM] + [HBM] * len(flat),
    )[0]


def other_amplitudes(plan, slice_values, boundary, top, amplitudes):
    width = plan.width

    def body(values, bound, top, _, out, left, chosen, result, sems):
        copies = Copies(sems)
        other = 1 - lax.axis_index("branch")
        value = jnp.where(values[other] == 1, 1, 0)
        loads = [copies.start(top, left), copies.start(bound.at[value], chosen)]
        for copy in loads:
            copy.wait()
        parts = complex_dot(left[0], left[1], chosen[...].reshape(2 * width, width))
        for part in range(2):
            result[part] = parts[part]
        copies.start(result, out.at[:, other]).wait()

    return run_kernel(
        body,
        [jax.ShapeDtypeStruct(amplitudes.shape, jnp.float32)],
        [
            pltpu.VMEM((2, width // 2, width), jnp.bfloat16),
            pltpu.VMEM((2, width, width), jnp.bfloat16),
            pltpu.VMEM((2, width // 2, width), jnp.float32),
        ],
        3,
        4 * width**3,
        [slice_values, boundary, top, amplitudes],
        [SMEM, HBM, HBM, HBM],
        {3: 0},
    )[0]


def per_device(leaves, join_order, slice_values, boundary):
    plan = Plan(leaves)
    modes, ways, places, batch = plan.modes, plan.ways, plan.places, plan.batch
    every = [
        (high, place, way)
        for high in range(batch)
        for place in range(places)
        for way in range(ways)
    ]
    over_ways = [(plan.mode_of(h, p, w), plan.mode_of(h, p, w ^ 1)) for h, p, w in every]

    def over_places(step):
        return [(plan.mode_of(h, p, w), plan.mode_of(h, p ^ step, w)) for h, p, w in every]

    def to_rows(a, b):
        pairs = []
        for h, p, w in every:
            for k in range(2):
                target = (p * ways + (h ^ a)) * batch + (k ^ b)
                pairs.append((plan.mode_of(h, p, w) * 2 + k, target * 2 + w))
        return pairs

    quarter = plan.width // ways // 4
    spans = [(0, 2 * quarter), (2 * quarter, 3 * quarter), (3 * quarter, 4 * quarter)]
    groups = [[0], [1, 2]]
    left, right = {}, {}
    for group in groups:
        right.update(
            zip(group, first_level(plan, leaves, join_order, 1, [spans[c] for c in group]))
        )
        left.update(
            zip(group, first_level(plan, leaves, join_order, 0, [spans[c] for c in group]))
        )
    messages = []
    for chunk in range(len(spans)):
        right_own, right_send = right[chunk]
        left_own, left_send = left[chunk]
        right_way = lax.ppermute(right_send, "mode", over_ways)
        left_way = lax.ppermute(left_send, "mode", over_ways)
        right_places = [
            lax.ppermute(right_own, "mode", over_places(s)) for s in range(1, places)
        ]
        right_both = [lax.ppermute(right_way, "mode", over_places(s)) for s in range(1, places)]
        rows = second_level(
            plan, left_own, left_way, right_own, right_way, right_places, right_both
        )
        messages.append(
            [
                lax.ppermute(rows[a * batch + b], ("mode", "branch"), to_rows(a, b))
                for a in range(ways)
                for b in range(batch)
            ]
        )
    top_other = top_for_other(plan, join_order, messages)
    top_received = lax.ppermute(top_other, "branch", [(0, 1), (1, 0)])
    amplitudes = own_amplitudes(plan, join_order, slice_values, boundary, messages)
    return other_amplitudes(plan, slice_values, boundary, top_received, amplitudes)


def solution(mesh):
    in_specs = (P("branch", None, ("cuts", "mode"), None, None), P(), P(("cuts", "mode")), P())
    out_specs = P(None, ("cuts", "mode"), "branch", None)
    return jax.shard_map(
        per_device, mesh=mesh, in_specs=in_specs, out_specs=out_specs, check_vma=False
    )
```

time: 196 us -> 132 us (0.67)
  the two profiles are of different devices: /device:TPU:9 before, /device:TPU:1 now
where the time goes in v2:
time: 132 us
  waiting for transfers between devices  60.3 us (46%)
  starting transfers between devices  41.8 us (32%)
  Pallas kernels  25.6 us (19%)
  local copies, waits for them, and re-layouts  4.05 us (3%)
    ppermute x12, starting transfers between devices, per_device(): lax.ppermute(rows[a * batch + b], ('mode', 'branch'), to_rows(a, b))  28.3 us
    pallas_call x10, Pallas kernels, run_kernel(): pl.pallas_call(body, out_shape=outs, in_specs=specs, out_specs=[HBM] * le...  25.6 us
    ppermute x12, waiting for transfers between devices, per_device(): lax.ppermute(rows[a * batch + b], ('mode', 'branch'), to_rows(a, b))  24.6 us
    ppermute x3, waiting for transfers between devices, per_device(): lax.ppermute(right_own, 'mode', over_places(s))  18.9 us
    ppermute x3, waiting for transfers between devices, per_device(): right_way = lax.ppermute(right_send, 'mode', over_ways)  8.62 us
    ppermute x3, waiting for transfers between devices, per_device(): left_way = lax.ppermute(left_send, 'mode', over_ways)  8.21 us
    ppermute x3, starting transfers between devices, per_device(): right_way = lax.ppermute(right_send, 'mode', over_ways)  4.79 us
    unnamed x10, local copies, waits for them, and re-layouts  4.05 us
  transfers between devices with their start and end apart: 25, of which 6 were waited for; matrix products, arithmetic and copies ran while one was open for 0% of the time, Pallas kernels for 14%

profile of v2, /device:TPU:1, one launch (start us, length us, event | category | flops | bytes accessed | tf_op | source)
XLA Modules:
  0.0 132.0 jit_solution(15339710794477811150)
XLA Ops:
  0.0 3.4 %copy-done = bf16[4,2,2,512,512]{4,3,2,1,0:T(8,128)(2,1)S(1)} copy-done((bf16[4,2,2,512,512]{4,3,2,1,0:T(8,128)(2,1)S(1)}, bf16[4,2,2,512,512]{4,3,2,1,0:T(8,128)(2,1)}, u32[]{:S(2)}) %copy-start) | copy-done | bytes 8388632
  4.0 3.0 %shard_map.47 = (bf16[2,2,2,64,512]{4,3,2,1,0:T(8,128)(2,1)S(1)}, bf16[2,2,2,64,512]{4,3,2,1,0:T(8,128)(2,1)S(1)}) custom-call(s32[7]{0:T(128)S(1)} %copy-done.2, bf16[4,2,2,512,512]{4,3,2,1,0:T(8,128)(2,1)S(1)} %copy-done), custom_call_target="tpu_custom_call" | custom-call | flops 1073741824 | bytes 3145728 | tf_op jit(solution)/shard_map/pallas_call | solution.py:42
  7.1 2.1 %collective-permute-start.1 = (bf16[2,2,2,64,512]{4,3,2,1,0:T(8,128)(2,1)S(1)}, bf16[2,2,2,64,512]{4,3,2,1,0:T(8,128)(2,1)S(1)}, u32[]{:S(2)}, u32[]{:S(2)}) collective-permute-start(bf16[2,2,2,64,512]{4,3,2,1,0:T(8,128)(2,1)S(1)} %get-tuple-element.32), channel_id=1, source_target_pairs={{0,2},{2,0},{4,6},{6,4},{8,10},{10,8},{12,14},{14,12},{1,3},{3,1},... | collective-permute-start | bytes 1572872 | tf_op jit(solution)/shard_map/ppermute | solution.py:374
  9.2 3.0 %shard_map.49 = (bf16[2,1,2,64,512]{4,3,2,1,0:T(8,128)(2,1)S(1)}, bf16[2,1,2,64,512]{4,3,2,1,0:T(8,128)(2,1)S(1)}, bf16[2,1,2,64,512]{4,3,2,1,0:T(8,128)(2,1)S(1)}, bf16[2,1,2,64,512]{4,3,2,1,0:T(8,128)(2,1)S(1)}) custom-call(s32[7]{0:T(128)S(1)} %copy-done.2, bf16[4,2,2,512,512]{4,3,2,1,0:T(8,128)(2,1)S(1)} %copy-done), custom_call_target="tpu_custom_call" | custom-call | flops 1073741824 | bytes 3145728 | tf_op jit(solution)/shard_map/pallas_call | solution.py:42
  12.3 3.0 %shard_map.50 = (bf16[2,1,2,64,512]{4,3,2,1,0:T(8,128)(2,1)S(1)}, bf16[2,1,2,64,512]{4,3,2,1,0:T(8,128)(2,1)S(1)}, bf16[2,1,2,64,512]{4,3,2,1,0:T(8,128)(2,1)S(1)}, bf16[2,1,2,64,512]{4,3,2,1,0:T(8,128)(2,1)S(1)}) custom-call(s32[7]{0:T(128)S(1)} %copy-done.2, bf16[4,2,2,512,512]{4,3,2,1,0:T(8,128)(2,1)S(1)} %copy-done), custom_call_target="tpu_custom_call" | custom-call | flops 1073741824 | bytes 3145728 | tf_op jit(solution)/shard_map/pallas_call | solution.py:42
  15.3 1.5 %collective-permute-start.9 = (bf16[2,1,2,64,512]{4,3,2,1,0:T(8,128)(2,1)S(1)}, bf16[2,1,2,64,512]{4,3,2,1,0:T(8,128)(2,1)S(1)}, u32[]{:S(2)}, u32[]{:S(2)}) collective-permute-start(bf16[2,1,2,64,512]{4,3,2,1,0:T(8,128)(2,1)S(1)} %get-tuple-element.40), channel_id=1, source_target_pairs={{0,2},{2,0},{4,6},{6,4},{8,10},{10,8},{12,14},{14,12},{1,3},{3,1},... | collective-permute-start | bytes 786440 | tf_op jit(solution)/shard_map/ppermute | solution.py:374
  18.3 8.1 %collective-permute-done.8.refs_1_ = bf16[2,1,2,64,512]{4,3,2,1,0:T(8,128)(2,1)S(1)} collective-permute-done((bf16[2,1,2,64,512]{4,3,2,1,0:T(8,128)(2,1)S(1)}, bf16[2,1,2,64,512]{4,3,2,1,0:T(8,128)(2,1)S(1)}, u32[]{:S(2)}, u32[]{:S(2)}) %collective-permute-start.8) | collective-permute-done | bytes 262176 | tf_op jit(solution)/shard_map/ppermute | solution.py:375
  27.6 4.5 %collective-permute-done.9.refs_3_ = bf16[2,1,2,64,512]{4,3,2,1,0:T(8,128)(2,1)S(1)} collective-permute-done((bf16[2,1,2,64,512]{4,3,2,1,0:T(8,128)(2,1)S(1)}, bf16[2,1,2,64,512]{4,3,2,1,0:T(8,128)(2,1)S(1)}, u32[]{:S(2)}, u32[]{:S(2)}) %collective-permute-start.9) | collective-permute-done | bytes 262176 | tf_op jit(solution)/shard_map/ppermute | solution.py:374
  33.3 3.0 %shard_map.46 = (bf16[2,2,2,64,512]{4,3,2,1,0:T(8,128)(2,1)S(1)}, bf16[2,2,2,64,512]{4,3,2,1,0:T(8,128)(2,1)S(1)}) custom-call(s32[7]{0:T(128)S(1)} %copy-done.2, bf16[4,2,2,512,512]{4,3,2,1,0:T(8,128)(2,1)S(1)} %copy-done), custom_call_target="tpu_custom_call" | custom-call | flops 1073741824 | bytes 3145728 | tf_op jit(solution)/shard_map/pallas_call | solution.py:42
  39.2 4.1 %collective-permute-done.17.refs_3_ = bf16[2,1,2,64,512]{4,3,2,1,0:T(8,128)(2,1)S(1)} collective-permute-done((bf16[2,1,2,64,512]{4,3,2,1,0:T(8,128)(2,1)S(1)}, bf16[2,1,2,64,512]{4,3,2,1,0:T(8,128)(2,1)S(1)}, u32[]{:S(2)}, u32[]{:S(2)}) %collective-permute-start.17) | collective-permute-done | bytes 262176 | tf_op jit(solution)/shard_map/ppermute | solution.py:374
  46.0 18.9 %collective-permute-done.18.refs_4_ = bf16[2,1,2,64,512]{4,3,2,1,0:T(8,128)(2,1)S(1)} collective-permute-done((bf16[2,1,2,64,512]{4,3,2,1,0:T(8,128)(2,1)S(1)}, bf16[2,1,2,64,512]{4,3,2,1,0:T(8,128)(2,1)S(1)}, u32[]{:S(2)}, u32[]{:S(2)}) %collective-permute-start.18) | collective-permute-done | bytes 262176 | tf_op jit(solution)/shard_map/ppermute | solution.py:377
  65.0 10.0 %collective-permute-start.12 = (bf16[2,1,64,512]{3,2,1,0:T(8,128)(2,1)S(1)}, bf16[2,1,64,512]{3,2,1,0:T(8,128)(2,1)S(1)}, u32[]{:S(2)}, u32[]{:S(2)}) collective-permute-start(bf16[2,1,64,512]{3,2,1,0:T(8,128)(2,1)S(1)} %get-tuple-element.41), channel_id=1, source_target_pairs={{0,0},{1,2},{2,1},{3,3},{4,8},{5,10},{6,9},{7,11},{8,4},{9,6},{10,... | collective-permute-start | bytes 393224 | tf_op jit(solution)/shard_map/ppermute | solution.py:385
  76.4 1.9 %collective-permute-start.14 = (bf16[2,1,64,512]{3,2,1,0:T(8,128)(2,1)S(1)}, bf16[2,1,64,512]{3,2,1,0:T(8,128)(2,1)S(1)}, u32[]{:S(2)}, u32[]{:S(2)}) collective-permute-start(bf16[2,1,64,512]{3,2,1,0:T(8,128)(2,1)S(1)} %get-tuple-element.43), channel_id=1, source_target_pairs={{0,4},{1,6},{2,5},{3,7},{4,12},{5,14},{6,13},{7,15},{8,0},{9,2},{1... | collective-permute-start | bytes 393224 | tf_op jit(solution)/shard_map/ppermute | solution.py:385
  78.2 3.1 %collective-permute-start.15 = (bf16[2,1,64,512]{3,2,1,0:T(8,128)(2,1)S(1)}, bf16[2,1,64,512]{3,2,1,0:T(8,128)(2,1)S(1)}, u32[]{:S(2)}, u32[]{:S(2)}) collective-permute-start(bf16[2,1,64,512]{3,2,1,0:T(8,128)(2,1)S(1)} %get-tuple-element.44), channel_id=1, source_target_pairs={{0,6},{1,4},{2,7},{3,5},{4,14},{5,12},{6,15},{7,13},{8,2},{9,0},{1... | collective-permute-start | bytes 393224 | tf_op jit(solution)/shard_map/ppermute | solution.py:385
  81.4 2.3 %collective-permute-start.20 = (bf16[2,1,64,512]{3,2,1,0:T(8,128)(2,1)S(1)}, bf16[2,1,64,512]{3,2,1,0:T(8,128)(2,1)S(1)}, u32[]{:S(2)}, u32[]{:S(2)}) collective-permute-start(bf16[2,1,64,512]{3,2,1,0:T(8,128)(2,1)S(1)} %get-tuple-element.49), channel_id=1, source_target_pairs={{0,0},{1,2},{2,1},{3,3},{4,8},{5,10},{6,9},{7,11},{8,4},{9,6},{10,... | collective-permute-start | bytes 393224 | tf_op jit(solution)/shard_map/ppermute | solution.py:385
  83.7 2.5 %shard_map.48 = (bf16[2,2,64,512]{3,2,1,0:T(8,128)(2,1)S(1)}, bf16[2,2,64,512]{3,2,1,0:T(8,128)(2,1)S(1)}, bf16[2,2,64,512]{3,2,1,0:T(8,128)(2,1)S(1)}, bf16[2,2,64,512]{3,2,1,0:T(8,128)(2,1)S(1)}) custom-call(bf16[2,2,2,64,512]{4,3,2,1,0:T(8,128)(2,1)S(1)} %get-tuple-element.29.refs_0_, bf16[2,2,2,64,512]{4,3,2,1,0:T(8,128)(2,1)S(1)} %collective-permute-done.refs_1_, ...), custom_call_target="tpu_custom_call" | custom-call | flops 1073741824 | bytes 3145728 | tf_op jit(solution)/shard_map/pallas_call | solution.py:42
  86.2 2.2 %collective-permute-start.22 = (bf16[2,1,64,512]{3,2,1,0:T(8,128)(2,1)S(1)}, bf16[2,1,64,512]{3,2,1,0:T(8,128)(2,1)S(1)}, u32[]{:S(2)}, u32[]{:S(2)}) collective-permute-start(bf16[2,1,64,512]{3,2,1,0:T(8,128)(2,1)S(1)} %get-tuple-element.51), channel_id=1, source_target_pairs={{0,4},{1,6},{2,5},{3,7},{4,12},{5,14},{6,13},{7,15},{8,0},{9,2},{1... | collective-permute-start | bytes 393224 | tf_op jit(solution)/shard_map/ppermute | solution.py:385
  88.5 3.7 %collective-permute-start.4 = (bf16[2,2,64,512]{3,2,1,0:T(8,128)(2,1)S(1)}, bf16[2,2,64,512]{3,2,1,0:T(8,128)(2,1)S(1)}, u32[]{:S(2)}, u32[]{:S(2)}) collective-permute-start(bf16[2,2,64,512]{3,2,1,0:T(8,128)(2,1)S(1)} %get-tuple-element.33), channel_id=1, source_target_pairs={{0,0},{1,2},{2,1},{3,3},{4,8},{5,10},{6,9},{7,11},{8,4},{9,6},{10,... | collective-permute-start | bytes 786440 | tf_op jit(solution)/shard_map/ppermute | solution.py:385
  92.3 2.3 %collective-permute-start.6 = (bf16[2,2,64,512]{3,2,1,0:T(8,128)(2,1)S(1)}, bf16[2,2,64,512]{3,2,1,0:T(8,128)(2,1)S(1)}, u32[]{:S(2)}, u32[]{:S(2)}) collective-permute-start(bf16[2,2,64,512]{3,2,1,0:T(8,128)(2,1)S(1)} %get-tuple-element.35), channel_id=1, source_target_pairs={{0,4},{1,6},{2,5},{3,7},{4,12},{5,14},{6,13},{7,15},{8,0},{9,2},{1... | collective-permute-start | bytes 786440 | tf_op jit(solution)/shard_map/ppermute | solution.py:385
  97.2 24.5 %collective-permute-done.23.refs_11_ = bf16[2,1,64,512]{3,2,1,0:T(8,128)(2,1)S(1)} collective-permute-done((bf16[2,1,64,512]{3,2,1,0:T(8,128)(2,1)S(1)}, bf16[2,1,64,512]{3,2,1,0:T(8,128)(2,1)S(1)}, u32[]{:S(2)}, u32[]{:S(2)}) %collective-permute-start.23) | collective-permute-done | bytes 131104 | tf_op jit(solution)/shard_map/ppermute | solution.py:385
  121.8 2.2 %shard_map.53 = bf16[2,256,512]{2,1,0:T(8,128)(2,1)S(1)} custom-call(s32[7]{0:T(128)S(1)} %copy-done.3, bf16[2,2,64,512]{3,2,1,0:T(8,128)(2,1)S(1)} %collective-permute-done.4.refs_0_, bf16[2,2,64,512]{3,2,1,0:T(8,128)(2,1)S(1)} %collective-permute-done.5.refs_1_, bf16[2,2,64,512]{3,2,1,0:T(8,128)(2,1)S(1)} %collective-permute-done.6.refs_2_, ...), custom_call_target="tpu_custom_call" | custom-call | flops 536870912 | bytes 2621440 | tf_op jit(solution)/shard_map/pallas_call | solution.py:42
  124.0 1.6 %collective-permute-start.24 = (bf16[2,256,512]{2,1,0:T(8,128)(2,1)S(1)}, bf16[2,256,512]{2,1,0:T(8,128)(2,1)S(1)}, u32[]{:S(2)}, u32[]{:S(2)}) collective-permute-start(bf16[2,256,512]{2,1,0:T(8,128)(2,1)S(1)} %shard_map.53), channel_id=1, source_target_pairs={{0,1},{1,0},{2,3},{3,2},{4,5},{5,4},{6,7},{7,6},{8,9},{9,8},{10,11... | collective-permute-start | bytes 1572872 | tf_op jit(solution)/shard_map/ppermute | solution.py:391
  125.7 3.9 %shard_map.54._ = f32[2,2,256,512]{3,2,1,0:T(8,128)} custom-call(s32[7]{0:T(128)S(1)} %copy-done.3, s32[2]{0:T(128)S(1)} %copy-done.4, bf16[2,2,512,512]{3,2,1,0:T(8,128)(2,1)S(1)} %copy-done.1, bf16[2,2,64,512]{3,2,1,0:T(8,128)(2,1)S(1)} %collective-permute-done.4.refs_0_, bf16[2,2,64,512]{3,2,1,0:T(8,128)(2,1)S(1)} %collective-permute-done.5.refs_1_, ...), custom_call_target="tpu_custom_call" | custom-call | flops 1073741824 | bytes 4194304 | tf_op jit(solution)/shard_map/pallas_call | solution.py:42
  129.6 2.4 %shard_map.55 = f32[2,2,256,512]{3,2,1,0:T(8,128)} custom-call(s32[2]{0:T(128)S(1)} %copy-done.4, bf16[2,2,512,512]{3,2,1,0:T(8,128)(2,1)S(1)} %copy-done.1, bf16[2,256,512]{2,1,0:T(8,128)(2,1)S(1)} %collective-permute-done.24.top, f32[2,2,256,512]{3,2,1,0:T(8,128)} %shard_map.54._), custom_call_target="tpu_custom_call", output_to_operand_aliasing={{}: (3, {})} | custom-call | flops 536870912 | bytes 4194304 | tf_op jit(solution)/shard_map/pallas_call | solution.py:42
  (46 shorter events, 14.3 us)
Async XLA Ops:
  7.1 31.8 %collective-permute-start.1 = (bf16[2,2,2,64,512]{4,3,2,1,0:T(8,128)(2,1)S(1)}, bf16[2,2,2,64,512]{4,3,2,1,0:T(8,128)(2,1)S(1)}, u32[]{:S(2)}, u32[]{:S(2)}) collective-permute-start(bf16[2,2,2,64,512]{4,3,2,1,0:T(8,128)(2,1)S(1)} %get-tuple-element.32), channel_id=1, source_target_pairs={{0,2},{2,0},{4,6},{6,4},{8,10},{10,8},{12,14},{14,12},{1,3},{3,1},... | collective-permute-start | bytes 1572872 | tf_op jit(solution)/shard_map/ppermute | solution.py:374
  12.2 14.2 %collective-permute-start.8 = (bf16[2,1,2,64,512]{4,3,2,1,0:T(8,128)(2,1)S(1)}, bf16[2,1,2,64,512]{4,3,2,1,0:T(8,128)(2,1)S(1)}, u32[]{:S(2)}, u32[]{:S(2)}) collective-permute-start(bf16[2,1,2,64,512]{4,3,2,1,0:T(8,128)(2,1)S(1)} %get-tuple-element.38), channel_id=1, source_target_pairs={{0,2},{2,0},{4,6},{6,4},{8,10},{10,8},{12,14},{14,12},{1,3},{3,1},... | collective-permute-start | bytes 786440 | tf_op jit(solution)/shard_map/ppermute | solution.py:375
  15.3 16.8 %collective-permute-start.9 = (bf16[2,1,2,64,512]{4,3,2,1,0:T(8,128)(2,1)S(1)}, bf16[2,1,2,64,512]{4,3,2,1,0:T(8,128)(2,1)S(1)}, u32[]{:S(2)}, u32[]{:S(2)}) collective-permute-start(bf16[2,1,2,64,512]{4,3,2,1,0:T(8,128)(2,1)S(1)} %get-tuple-element.40), channel_id=1, source_target_pairs={{0,2},{2,0},{4,6},{6,4},{8,10},{10,8},{12,14},{14,12},{1,3},{3,1},... | collective-permute-start | bytes 786440 | tf_op jit(solution)/shard_map/ppermute | solution.py:374
  16.8 19.5 %collective-permute-start.10 = (bf16[2,1,2,64,512]{4,3,2,1,0:T(8,128)(2,1)S(1)}, bf16[2,1,2,64,512]{4,3,2,1,0:T(8,128)(2,1)S(1)}, u32[]{:S(2)}, u32[]{:S(2)}) collective-permute-start(bf16[2,1,2,64,512]{4,3,2,1,0:T(8,128)(2,1)S(1)} %get-tuple-element.39.refs_2_), channel_id=1, source_target_pairs={{0,4},{2,6},{4,0},{6,2},{8,12},{10,14},{12,8},{14,10},{1,5},{3,7},... | collective-permute-start | bytes 786440 | tf_op jit(solution)/shard_map/ppermute | solution.py:377
  18.1 19.6 %collective-permute-start.16 = (bf16[2,1,2,64,512]{4,3,2,1,0:T(8,128)(2,1)S(1)}, bf16[2,1,2,64,512]{4,3,2,1,0:T(8,128)(2,1)S(1)}, u32[]{:S(2)}, u32[]{:S(2)}) collective-permute-start(bf16[2,1,2,64,512]{4,3,2,1,0:T(8,128)(2,1)S(1)} %get-tuple-element.46), channel_id=1, source_target_pairs={{0,2},{2,0},{4,6},{6,4},{8,10},{10,8},{12,14},{14,12},{1,3},{3,1},... | collective-permute-start | bytes 786440 | tf_op jit(solution)/shard_map/ppermute | solution.py:375
  26.5 16.9 %collective-permute-start.17 = (bf16[2,1,2,64,512]{4,3,2,1,0:T(8,128)(2,1)S(1)}, bf16[2,1,2,64,512]{4,3,2,1,0:T(8,128)(2,1)S(1)}, u32[]{:S(2)}, u32[]{:S(2)}) collective-permute-start(bf16[2,1,2,64,512]{4,3,2,1,0:T(8,128)(2,1)S(1)} %get-tuple-element.48), channel_id=1, source_target_pairs={{0,2},{2,0},{4,6},{6,4},{8,10},{10,8},{12,14},{14,12},{1,3},{3,1},... | collective-permute-start | bytes 786440 | tf_op jit(solution)/shard_map/ppermute | solution.py:374
  32.1 12.4 %collective-permute-start.11 = (bf16[2,1,2,64,512]{4,3,2,1,0:T(8,128)(2,1)S(1)}, bf16[2,1,2,64,512]{4,3,2,1,0:T(8,128)(2,1)S(1)}, u32[]{:S(2)}, u32[]{:S(2)}) collective-permute-start(bf16[2,1,2,64,512]{4,3,2,1,0:T(8,128)(2,1)S(1)} %collective-permute-done.9.refs_3_), channel_id=1, source_target_pairs={{0,4},{2,6},{4,0},{6,2},{8,12},{10,14},{12,8},{14,10},{1,5},{3,7},... | collective-permute-start | bytes 786440 | tf_op jit(solution)/shard_map/ppermute | solution.py:379
  36.3 40.1 %collective-permute-start = (bf16[2,2,2,64,512]{4,3,2,1,0:T(8,128)(2,1)S(1)}, bf16[2,2,2,64,512]{4,3,2,1,0:T(8,128)(2,1)S(1)}, u32[]{:S(2)}, u32[]{:S(2)}) collective-permute-start(bf16[2,2,2,64,512]{4,3,2,1,0:T(8,128)(2,1)S(1)} %get-tuple-element.30), channel_id=1, source_target_pairs={{0,2},{2,0},{4,6},{6,4},{8,10},{10,8},{12,14},{14,12},{1,3},{3,1},... | collective-permute-start | bytes 1572872 | tf_op jit(solution)/shard_map/ppermute | solution.py:375
  37.7 40.5 %collective-permute-start.2 = (bf16[2,2,2,64,512]{4,3,2,1,0:T(8,128)(2,1)S(1)}, bf16[2,2,2,64,512]{4,3,2,1,0:T(8,128)(2,1)S(1)}, u32[]{:S(2)}, u32[]{:S(2)}) collective-permute-start(bf16[2,2,2,64,512]{4,3,2,1,0:T(8,128)(2,1)S(1)} %get-tuple-element.31.refs_2_), channel_id=1, source_target_pairs={{0,4},{2,6},{4,0},{6,2},{8,12},{10,14},{12,8},{14,10},{1,5},{3,7},... | collective-permute-start | bytes 1572872 | tf_op jit(solution)/shard_map/ppermute | solution.py:377
  38.9 44.8 %collective-permute-start.3 = (bf16[2,2,2,64,512]{4,3,2,1,0:T(8,128)(2,1)S(1)}, bf16[2,2,2,64,512]{4,3,2,1,0:T(8,128)(2,1)S(1)}, u32[]{:S(2)}, u32[]{:S(2)}) collective-permute-start(bf16[2,2,2,64,512]{4,3,2,1,0:T(8,128)(2,1)S(1)} %collective-permute-done.1.refs_3_), channel_id=1, source_target_pairs={{0,4},{2,6},{4,0},{6,2},{8,12},{10,14},{12,8},{14,10},{1,5},{3,7},... | collective-permute-start | bytes 1572872 | tf_op jit(solution)/shard_map/ppermute | solution.py:379
  43.3 21.6 %collective-permute-start.18 = (bf16[2,1,2,64,512]{4,3,2,1,0:T(8,128)(2,1)S(1)}, bf16[2,1,2,64,512]{4,3,2,1,0:T(8,128)(2,1)S(1)}, u32[]{:S(2)}, u32[]{:S(2)}) collective-permute-start(bf16[2,1,2,64,512]{4,3,2,1,0:T(8,128)(2,1)S(1)} %get-tuple-element.47.refs_2_), channel_id=1, source_target_pairs={{0,4},{2,6},{4,0},{6,2},{8,12},{10,14},{12,8},{14,10},{1,5},{3,7},... | collective-permute-start | bytes 786440 | tf_op jit(solution)/shard_map/ppermute | solution.py:377
  44.5 30.5 %collective-permute-start.19 = (bf16[2,1,2,64,512]{4,3,2,1,0:T(8,128)(2,1)S(1)}, bf16[2,1,2,64,512]{4,3,2,1,0:T(8,128)(2,1)S(1)}, u32[]{:S(2)}, u32[]{:S(2)}) collective-permute-start(bf16[2,1,2,64,512]{4,3,2,1,0:T(8,128)(2,1)S(1)} %collective-permute-done.17.refs_3_), channel_id=1, source_target_pairs={{0,4},{2,6},{4,0},{6,2},{8,12},{10,14},{12,8},{14,10},{1,5},{3,7},... | collective-permute-start | bytes 786440 | tf_op jit(solution)/shard_map/ppermute | solution.py:379
  65.0 16.4 %collective-permute-start.12 = (bf16[2,1,64,512]{3,2,1,0:T(8,128)(2,1)S(1)}, bf16[2,1,64,512]{3,2,1,0:T(8,128)(2,1)S(1)}, u32[]{:S(2)}, u32[]{:S(2)}) collective-permute-start(bf16[2,1,64,512]{3,2,1,0:T(8,128)(2,1)S(1)} %get-tuple-element.41), channel_id=1, source_target_pairs={{0,0},{1,2},{2,1},{3,3},{4,8},{5,10},{6,9},{7,11},{8,4},{9,6},{10,... | collective-permute-start | bytes 393224 | tf_op jit(solution)/shard_map/ppermute | solution.py:385
  75.0 11.3 %collective-permute-start.13 = (bf16[2,1,64,512]{3,2,1,0:T(8,128)(2,1)S(1)}, bf16[2,1,64,512]{3,2,1,0:T(8,128)(2,1)S(1)}, u32[]{:S(2)}, u32[]{:S(2)}) collective-permute-start(bf16[2,1,64,512]{3,2,1,0:T(8,128)(2,1)S(1)} %get-tuple-element.42), channel_id=1, source_target_pairs={{0,2},{1,0},{2,3},{3,1},{4,10},{5,8},{6,11},{7,9},{8,6},{9,4},{10,... | collective-permute-start | bytes 393224 | tf_op jit(solution)/shard_map/ppermute | solution.py:385
  76.4 12.1 %collective-permute-start.14 = (bf16[2,1,64,512]{3,2,1,0:T(8,128)(2,1)S(1)}, bf16[2,1,64,512]{3,2,1,0:T(8,128)(2,1)S(1)}, u32[]{:S(2)}, u32[]{:S(2)}) collective-permute-start(bf16[2,1,64,512]{3,2,1,0:T(8,128)(2,1)S(1)} %get-tuple-element.43), channel_id=1, source_target_pairs={{0,4},{1,6},{2,5},{3,7},{4,12},{5,14},{6,13},{7,15},{8,0},{9,2},{1... | collective-permute-start | bytes 393224 | tf_op jit(solution)/shard_map/ppermute | solution.py:385
  78.2 14.0 %collective-permute-start.15 = (bf16[2,1,64,512]{3,2,1,0:T(8,128)(2,1)S(1)}, bf16[2,1,64,512]{3,2,1,0:T(8,128)(2,1)S(1)}, u32[]{:S(2)}, u32[]{:S(2)}) collective-permute-start(bf16[2,1,64,512]{3,2,1,0:T(8,128)(2,1)S(1)} %get-tuple-element.44), channel_id=1, source_target_pairs={{0,6},{1,4},{2,7},{3,5},{4,14},{5,12},{6,15},{7,13},{8,2},{9,0},{1... | collective-permute-start | bytes 393224 | tf_op jit(solution)/shard_map/ppermute | solution.py:385
  81.4 10.9 %collective-permute-start.20 = (bf16[2,1,64,512]{3,2,1,0:T(8,128)(2,1)S(1)}, bf16[2,1,64,512]{3,2,1,0:T(8,128)(2,1)S(1)}, u32[]{:S(2)}, u32[]{:S(2)}) collective-permute-start(bf16[2,1,64,512]{3,2,1,0:T(8,128)(2,1)S(1)} %get-tuple-element.49), channel_id=1, source_target_pairs={{0,0},{1,2},{2,1},{3,3},{4,8},{5,10},{6,9},{7,11},{8,4},{9,6},{10,... | collective-permute-start | bytes 393224 | tf_op jit(solution)/shard_map/ppermute | solution.py:385
  83.7 11.0 %collective-permute-start.21 = (bf16[2,1,64,512]{3,2,1,0:T(8,128)(2,1)S(1)}, bf16[2,1,64,512]{3,2,1,0:T(8,128)(2,1)S(1)}, u32[]{:S(2)}, u32[]{:S(2)}) collective-permute-start(bf16[2,1,64,512]{3,2,1,0:T(8,128)(2,1)S(1)} %get-tuple-element.50), channel_id=1, source_target_pairs={{0,2},{1,0},{2,3},{3,1},{4,10},{5,8},{6,11},{7,9},{8,6},{9,4},{10,... | collective-permute-start | bytes 393224 | tf_op jit(solution)/shard_map/ppermute | solution.py:385
  86.2 9.5 %collective-permute-start.22 = (bf16[2,1,64,512]{3,2,1,0:T(8,128)(2,1)S(1)}, bf16[2,1,64,512]{3,2,1,0:T(8,128)(2,1)S(1)}, u32[]{:S(2)}, u32[]{:S(2)}) collective-permute-start(bf16[2,1,64,512]{3,2,1,0:T(8,128)(2,1)S(1)} %get-tuple-element.51), channel_id=1, source_target_pairs={{0,4},{1,6},{2,5},{3,7},{4,12},{5,14},{6,13},{7,15},{8,0},{9,2},{1... | collective-permute-start | bytes 393224 | tf_op jit(solution)/shard_map/ppermute | solution.py:385
  88.5 33.3 %collective-permute-start.4 = (bf16[2,2,64,512]{3,2,1,0:T(8,128)(2,1)S(1)}, bf16[2,2,64,512]{3,2,1,0:T(8,128)(2,1)S(1)}, u32[]{:S(2)}, u32[]{:S(2)}) collective-permute-start(bf16[2,2,64,512]{3,2,1,0:T(8,128)(2,1)S(1)} %get-tuple-element.33), channel_id=1, source_target_pairs={{0,0},{1,2},{2,1},{3,3},{4,8},{5,10},{6,9},{7,11},{8,4},{9,6},{10,... | collective-permute-start | bytes 786440 | tf_op jit(solution)/shard_map/ppermute | solution.py:385
  92.3 29.5 %collective-permute-start.5 = (bf16[2,2,64,512]{3,2,1,0:T(8,128)(2,1)S(1)}, bf16[2,2,64,512]{3,2,1,0:T(8,128)(2,1)S(1)}, u32[]{:S(2)}, u32[]{:S(2)}) collective-permute-start(bf16[2,2,64,512]{3,2,1,0:T(8,128)(2,1)S(1)} %get-tuple-element.34), channel_id=1, source_target_pairs={{0,2},{1,0},{2,3},{3,1},{4,10},{5,8},{6,11},{7,9},{8,6},{9,4},{10,... | collective-permute-start | bytes 786440 | tf_op jit(solution)/shard_map/ppermute | solution.py:385
  92.3 29.4 %collective-permute-start.6 = (bf16[2,2,64,512]{3,2,1,0:T(8,128)(2,1)S(1)}, bf16[2,2,64,512]{3,2,1,0:T(8,128)(2,1)S(1)}, u32[]{:S(2)}, u32[]{:S(2)}) collective-permute-start(bf16[2,2,64,512]{3,2,1,0:T(8,128)(2,1)S(1)} %get-tuple-element.35), channel_id=1, source_target_pairs={{0,4},{1,6},{2,5},{3,7},{4,12},{5,14},{6,13},{7,15},{8,0},{9,2},{1... | collective-permute-start | bytes 786440 | tf_op jit(solution)/shard_map/ppermute | solution.py:385
  94.7 27.1 %collective-permute-start.7 = (bf16[2,2,64,512]{3,2,1,0:T(8,128)(2,1)S(1)}, bf16[2,2,64,512]{3,2,1,0:T(8,128)(2,1)S(1)}, u32[]{:S(2)}, u32[]{:S(2)}) collective-permute-start(bf16[2,2,64,512]{3,2,1,0:T(8,128)(2,1)S(1)} %get-tuple-element.36), channel_id=1, source_target_pairs={{0,6},{1,4},{2,7},{3,5},{4,14},{5,12},{6,15},{7,13},{8,2},{9,0},{1... | collective-permute-start | bytes 786440 | tf_op jit(solution)/shard_map/ppermute | solution.py:385
  95.7 26.0 %collective-permute-start.23 = (bf16[2,1,64,512]{3,2,1,0:T(8,128)(2,1)S(1)}, bf16[2,1,64,512]{3,2,1,0:T(8,128)(2,1)S(1)}, u32[]{:S(2)}, u32[]{:S(2)}) collective-permute-start(bf16[2,1,64,512]{3,2,1,0:T(8,128)(2,1)S(1)} %get-tuple-element.52), channel_id=1, source_target_pairs={{0,6},{1,4},{2,7},{3,5},{4,14},{5,12},{6,15},{7,13},{8,2},{9,0},{1... | collective-permute-start | bytes 393224 | tf_op jit(solution)/shard_map/ppermute | solution.py:385
  (6 other events, 134.0 us)

commit v3 on v2

--- a/solution.py
+++ b/solution.py
@@ -7,9 +7,10 @@
 from jax.experimental.pallas import tpu as pltpu
 from jax.sharding import PartitionSpec as P
 
-HBM = pl.BlockSpec(memory_space=pl.ANY)
+ANY = pl.BlockSpec(memory_space=pl.ANY)
 SMEM = pl.BlockSpec(memory_space=pltpu.SMEM)
 VMEM_LIMIT = 40 * 2**20
+VMEM_MOST = 60 * 2**20
 
 
 def complex_dot(left_real, left_imag, right):
@@ -37,16 +38,16 @@
         return copy
 
 
-def run_kernel(body, outs, scratch, copies, flops, operands, specs, aliases=None):
+def run_kernel(body, outs, scratch, copies, flops, operands, specs, aliases=None, limit=VMEM_LIMIT):
     moved = sum(x.size * x.dtype.itemsize for x in outs) + 2**21
     return pl.pallas_call(
         body,
         out_shape=outs,
         in_specs=specs,
-        out_specs=[HBM] * len(outs),
+        out_specs=[ANY] * len(outs),
         scratch_shapes=list(scratch) + [pltpu.SemaphoreType.DMA((copies,))],
         input_output_aliases=aliases or {},
-        compiler_params=pltpu.CompilerParams(vmem_limit_bytes=VMEM_LIMIT),
+        compiler_params=pltpu.CompilerParams(vmem_limit_bytes=limit),
         cost_estimate=pl.CostEstimate(flops=flops, bytes_accessed=moved, transcendentals=0),
     )(*operands)
 
@@ -70,99 +71,93 @@
         return mode // self.size, (mode % self.size) // self.ways, mode % self.ways
 
 
-def first_level(plan, leaves, join_order, role, spans):
-    width, batch, rows = plan.width, plan.batch, plan.rows
-    lowest, highest = spans[0][0], spans[-1][1]
-    total = highest - lowest
-    half = width // plan.ways
-    chunk_blocks = [(high - low) // rows for low, high in spans]
+def first_level(plan, leaves, join_order, role, parts, limit):
+    width, batch, rows, ways = plan.width, plan.batch, plan.rows, plan.ways
+    half = width // ways
 
     def body(order, leaf, *rest):
-        outs, (upper, lower, result, sems) = rest[: 2 * len(spans)], rest[2 * len(spans) :]
+        outs, (upper, lower, result, sems) = rest[:-4], rest[-4:]
         copies = Copies(sems)
         branch = lax.axis_index("branch")
         _, _, way = plan.here()
         pair = jnp.where(order[2 * lax.axis_size("branch") + branch] == 1, 1 - role, role)
         swapped = jnp.where(order[2 * branch + pair] == 1, 1, 0)
         first, second = 2 * pair + swapped, 2 * pair + 1 - swapped
-        loads = []
-        for item in range(batch):
-            mine = []
-            for place in range(plan.ways):
-                target = (way + place) % plan.ways
-                mine.append(
-                    copies.start(
-                        leaf.at[first, :, item, pl.ds(target * half + lowest, total)],
-                        upper.at[item, :, place],
-                    )
-                )
-            mine.append(copies.start(leaf.at[second, :, item], lower.at[item]))
-            loads.append(mine)
+        loads = [
+            [
+                copies.start(leaf.at[second, :, item], lower.at[item]),
+                copies.start(leaf.at[first, :, item], upper.at[item]),
+            ]
+            for item in range(batch)
+        ]
         stores = []
         for item in range(batch):
             for copy in loads[item]:
                 copy.wait()
-            parts = complex_dot(
-                upper[item, 0].reshape(plan.ways * total, width),
-                upper[item, 1].reshape(plan.ways * total, width),
-                lower[item].reshape(2 * width, width),
+            sums = complex_dot(
+                upper[item, 0], upper[item, 1], lower[item].reshape(2 * width, width)
             )
             for part in range(2):
-                result[item, part] = (
-                    parts[part].astype(jnp.bfloat16).reshape(plan.ways, total, width)
-                )
-            for place in range(plan.ways):
-                for index, (low, high) in enumerate(spans):
-                    for block in range(chunk_blocks[index]):
-                        begin = low - lowest + block * rows
-                        stores.append(
-                            copies.start(
-                                result.at[item, :, place, pl.ds(begin, rows)],
-                                outs[2 * index + place].at[:, block, item],
-                            )
-                        )
+                result[item, part] = sums[part].astype(jnp.bfloat16)
+            for side, target in enumerate((way, 1 - way)):
+                begin = 0
+                for chunk, blocks in enumerate(parts):
+                    for block in range(blocks):
+                        source = result.at[item, :, pl.ds(target * half + begin, rows)]
+                        place = outs[2 * chunk + side].at[:, block, item]
+                        stores.append(copies.start(source, place))
+                        begin += rows
         for copy in stores:
             copy.wait()
 
     outs = [
         jax.ShapeDtypeStruct((2, blocks, batch, rows, width), jnp.bfloat16)
-        for blocks in chunk_blocks
-        for _ in range(plan.ways)
+        for blocks in parts
+        for _ in range(ways)
     ]
-    scratch = [
-        pltpu.VMEM((batch, 2, plan.ways, total, width), jnp.bfloat16),
-        pltpu.VMEM((batch, 2, width, width), jnp.bfloat16),
-        pltpu.VMEM((batch, 2, plan.ways, total, width), jnp.bfloat16),
-    ]
-    copies = batch * (plan.ways + 1) + batch * plan.ways * sum(chunk_blocks)
-    flops = 8 * batch * plan.ways * total * width * width
-    results = run_kernel(body, outs, scratch, copies, flops, [join_order, leaves], [SMEM, HBM])
-    return [results[2 * index : 2 * index + 2] for index in range(len(spans))]
-
-
-def second_level(plan, left_own, left_way, right_own, right_way, right_places, right_both):
+    scratch = [pltpu.VMEM((batch, 2, width, width), jnp.bfloat16) for _ in range(3)]
+    copies = 2 * batch + batch * ways * sum(parts)
+    flops = 8 * batch * width**3
+    results = run_kernel(
+        body, outs, scratch, copies, flops, [join_order, leaves], [SMEM, ANY], limit=limit
+    )
+    return [results[2 * index : 2 * index + 2] for index in range(len(parts))]
+
+
+def once_arrived(value, after):
+    def body(*refs):
+        pass
+
+    return pl.pallas_call(
+        body,
+        out_shape=jax.ShapeDtypeStruct(value.shape, value.dtype),
+        in_specs=[ANY] * (1 + len(after)),
+        out_specs=ANY,
+        input_output_aliases={0: 0},
+    )(value, *after)
+
+
+def second_level(plan, blocks, operands, pick):
     width, batch, rows, ways, places = plan.width, plan.batch, plan.rows, plan.ways, plan.places
-    blocks = left_own.shape[1]
     held = ways * batch * rows
-    others = places - 1
 
     def body(*refs):
-        sources = refs[: 4 + 2 * others]
-        outs = refs[4 + 2 * others : 4 + 2 * others + ways * batch]
-        left, right, result, sems = refs[4 + 2 * others + ways * batch :]
+        left_kept, left_sent, right_kept, right_sent, others = pick(refs[: len(operands)])
+        rest = refs[len(operands) :]
+        outs, (left, right, result, sems) = rest[:-4], rest[-4:]
         copies = Copies(sems)
         branch = lax.axis_index("branch")
         high, place, way = plan.here()
         loads = [
-            copies.start(sources[0], left.at[:, :, way]),
-            copies.start(sources[1], left.at[:, :, 1 - way]),
-            copies.start(sources[2], right.at[:, :, place, way]),
-            copies.start(sources[3], right.at[:, :, place, 1 - way]),
+            copies.start(left_kept, left.at[:, :, way]),
+            copies.start(left_sent, left.at[:, :, 1 - way]),
+            copies.start(right_kept, right.at[:, :, place, way]),
+            copies.start(right_sent, right.at[:, :, place, 1 - way]),
         ]
-        for step in range(1, places):
-            other = place ^ step
-            loads.append(copies.start(sources[3 + step], right.at[:, :, other, way]))
-            loads.append(copies.start(sources[3 + others + step], right.at[:, :, other, 1 - way]))
+        for step, (kept, sent) in enumerate(others):
+            other = place ^ (step + 1)
+            loads.append(copies.start(kept, right.at[:, :, other, way]))
+            loads.append(copies.start(sent, right.at[:, :, other, 1 - way]))
         for copy in loads:
             copy.wait()
         steps = [(a, b) for a in range(ways) for b in range(batch)]
@@ -194,10 +189,9 @@
         pltpu.VMEM((2, blocks, places, ways, batch, rows, width), jnp.bfloat16),
         pltpu.VMEM((blocks, 2, ways * batch, rows, width), jnp.bfloat16),
     ]
-    copies = 4 + 2 * others + blocks * ways * batch
-    operands = [left_own, left_way, right_own, right_way, *right_places, *right_both]
+    copies = 4 + 2 * (places - 1) + blocks * ways * batch
     flops = 8 * blocks * held * width * width
-    return run_kernel(body, outs, scratch, copies, flops, operands, [HBM] * len(operands))
+    return run_kernel(body, outs, scratch, copies, flops, operands, [ANY] * len(operands))
 
 
 def load_operands(plan, copies, order, messages, chunk_blocks, scratch, keep):
@@ -256,7 +250,7 @@
         len(flat) + 1,
         flops,
         [join_order, *flat],
-        [SMEM] + [HBM] * len(flat),
+        [SMEM] + [ANY] * len(flat),
     )[0]
 
 
@@ -299,7 +293,7 @@
         len(flat) + 2,
         flops,
         [join_order, slice_values, boundary, *flat],
-        [SMEM, SMEM, HBM] + [HBM] * len(flat),
+        [SMEM, SMEM, ANY] + [ANY] * len(flat),
     )[0]
 
 
@@ -329,7 +323,7 @@
         3,
         4 * width**3,
         [slice_values, boundary, top, amplitudes],
-        [SMEM, HBM, HBM, HBM],
+        [SMEM, ANY, ANY, ANY],
         {3: 0},
     )[0]
 
@@ -356,37 +350,41 @@
                 pairs.append((plan.mode_of(h, p, w) * 2 + k, target * 2 + w))
         return pairs
 
-    quarter = plan.width // ways // 4
-    spans = [(0, 2 * quarter), (2 * quarter, 3 * quarter), (3 * quarter, 4 * quarter)]
-    groups = [[0], [1, 2]]
-    left, right = {}, {}
-    for group in groups:
-        right.update(
-            zip(group, first_level(plan, leaves, join_order, 1, [spans[c] for c in group]))
-        )
-        left.update(
-            zip(group, first_level(plan, leaves, join_order, 0, [spans[c] for c in group]))
-        )
+    parts = [plan.size // 2] * 2
+    right = first_level(plan, leaves, join_order, 1, parts, VMEM_MOST)
+    left = first_level(plan, leaves, join_order, 0, parts, VMEM_LIMIT)
+    others = range(1, places)
+    steps = [(a, b) for a in range(ways) for b in range(batch)]
     messages = []
-    for chunk in range(len(spans)):
-        right_own, right_send = right[chunk]
-        left_own, left_send = left[chunk]
-        right_way = lax.ppermute(right_send, "mode", over_ways)
-        left_way = lax.ppermute(left_send, "mode", over_ways)
-        right_places = [
-            lax.ppermute(right_own, "mode", over_places(s)) for s in range(1, places)
+    order = list(range(len(steps)))[::-1]
+    arrived = []
+    for chunk, blocks in enumerate(parts):
+        right_kept, right_sent = right[chunk]
+        left_kept, left_sent = left[chunk]
+        right_sent = lax.ppermute(right_sent, "mode", over_ways)
+        kept_there = [lax.ppermute(right_kept, "mode", over_places(step)) for step in others]
+        left_sent = lax.ppermute(left_sent, "mode", over_ways)
+        sent_there = [lax.ppermute(right_sent, "mode", over_places(step)) for step in others]
+        operands = [
+            left_kept,
+            left_sent,
+            right_kept,
+            right_sent,
+            *kept_there,
+            *sent_there,
+            *arrived[:3],
         ]
-        right_both = [lax.ppermute(right_way, "mode", over_places(s)) for s in range(1, places)]
-        rows = second_level(
-            plan, left_own, left_way, right_own, right_way, right_places, right_both
-        )
-        messages.append(
-            [
-                lax.ppermute(rows[a * batch + b], ("mode", "branch"), to_rows(a, b))
-                for a in range(ways)
-                for b in range(batch)
-            ]
-        )
+
+        def pick(refs):
+            there = refs[4 : 2 + 2 * places]
+            pairs = list(zip(there[: places - 1], there[places - 1 :]))
+            return refs[0], refs[1], refs[2], refs[3], pairs
+
+        rows = second_level(plan, blocks, operands, pick)
+        arrived = [
+            lax.ppermute(rows[i], ("mode", "branch"), to_rows(*steps[i])) for i in order
+        ]
+        messages.append(arrived[::-1])
     top_other = top_for_other(plan, join_order, messages)
     top_received = lax.ppermute(top_other, "branch", [(0, 1), (1, 0)])
     amplitudes = own_amplitudes(plan, join_order, slice_values, boundary, messages)

time: 132 us -> 108 us (0.82)
  waiting for transfers between devices: 60.3 us -> 46 us
  starting transfers between devices: 41.8 us -> 35.7 us
  Pallas kernels: 25.6 us -> 23 us
    ppermute x24 -> x16, waiting for transfers between devices: 60.3 us -> 46 us  [the longest x8 25.8 us: per_device(): lax.ppermute(rows[i], ('mode', 'branch'), to_rows(*steps[i]))]
    ppermute x24 -> x16, starting transfers between devices: 40.2 us -> 33.2 us  [the longest x8 24.4 us: per_device(): lax.ppermute(rows[i], ('mode', 'branch'), to_rows(*steps[i]))]
    pallas_call x10 -> x7, Pallas kernels: 25.6 us -> 23 us  [run_kernel(): pl.pallas_call(body, out_shape=outs, in_specs=specs, out_specs=[ANY] * le...]
    unnamed x10 -> x12, local copies, waits for them, and re-layouts: 4.05 us -> 3.41 us
  transfers between devices with their start and end apart: 25 -> 17, of which waited for: 6 -> 9; matrix products, arithmetic and copies ran while one was open for 0% -> 0% of each run, Pallas kernels for 14% -> 12%
where the time goes in v3:
time: 108 us
  waiting for transfers between devices  46 us (43%)
  starting transfers between devices  35.7 us (33%)
  Pallas kernels  23 us (21%)
  local copies, waits for them, and re-layouts  3.41 us (3%)
    ppermute x8, waiting for transfers between devices, per_device(): lax.ppermute(rows[i], ('mode', 'branch'), to_rows(*steps[i]))  25.8 us
    ppermute x8, starting transfers between devices, per_device(): lax.ppermute(rows[i], ('mode', 'branch'), to_rows(*steps[i]))  24.4 us
    pallas_call x7, Pallas kernels, run_kernel(): pl.pallas_call(body, out_shape=outs, in_specs=specs, out_specs=[ANY] * le...  23 us
    ppermute x2, waiting for transfers between devices, per_device(): left_sent = lax.ppermute(left_sent, 'mode', over_ways)  10.9 us
    ppermute x2, waiting for transfers between devices, per_device(): right_sent = lax.ppermute(right_sent, 'mode', over_ways)  9.36 us
    unnamed x12, local copies, waits for them, and re-layouts  3.41 us
    ppermute x1, starting transfers between devices, per_device(): top_received = lax.ppermute(top_other, 'branch', [(0, 1), (1, 0)])  2.55 us
    ppermute x2, starting transfers between devices, per_device(): left_sent = lax.ppermute(left_sent, 'mode', over_ways)  2.45 us
  transfers between devices with their start and end apart: 17, of which 9 were waited for; matrix products, arithmetic and copies ran while one was open for 0% of the time, Pallas kernels for 12%

profile of v3, /device:TPU:1, one launch (start us, length us, event | category | flops | bytes accessed | tf_op | source)
XLA Modules:
  0.0 108.3 jit_solution(17341622781220569345)
XLA Ops:
  0.0 6.0 %shard_map.47 = (bf16[2,2,2,64,512]{4,3,2,1,0:T(8,128)(2,1)}, bf16[2,2,2,64,512]{4,3,2,1,0:T(8,128)(2,1)}, bf16[2,2,2,64,512]{4,3,2,1,0:T(8,128)(2,1)}, bf16[2,2,2,64,512]{4,3,2,1,0:T(8,128)(2,1)}) custom-call(s32[7]{0:T(128)} %order.7, bf16[4,2,2,512,512]{4,3,2,1,0:T(8,128)(2,1)} %leaf.3), custom_call_target="tpu_custom_call" | custom-call | flops 2147483648 | bytes 4194304 | tf_op jit(solution)/shard_map/pallas_call | solution.py:43
  6.0 2.1 %collective-permute-start.1 = (bf16[2,2,2,64,512]{4,3,2,1,0:T(8,128)(2,1)}, bf16[2,2,2,64,512]{4,3,2,1,0:T(8,128)(2,1)S(1)}, u32[]{:S(2)}, u32[]{:S(2)}) collective-permute-start(bf16[2,2,2,64,512]{4,3,2,1,0:T(8,128)(2,1)} %get-tuple-element.24), channel_id=1, source_target_pairs={{0,2},{2,0},{4,6},{6,4},{8,10},{10,8},{12,14},{14,12},{1,3},{3,1},... | collective-permute-start | bytes 1572872 | tf_op jit(solution)/shard_map/ppermute | solution.py:364
  8.2 1.3 %collective-permute-start.2 = (bf16[2,2,2,64,512]{4,3,2,1,0:T(8,128)(2,1)}, bf16[2,2,2,64,512]{4,3,2,1,0:T(8,128)(2,1)S(1)}, u32[]{:S(2)}, u32[]{:S(2)}) collective-permute-start(bf16[2,2,2,64,512]{4,3,2,1,0:T(8,128)(2,1)} %get-tuple-element.23.refs_2_), channel_id=1, source_target_pairs={{0,4},{2,6},{4,0},{6,2},{8,12},{10,14},{12,8},{14,10},{1,5},{3,7},... | collective-permute-start | bytes 1572872 | tf_op jit(solution)/shard_map/ppermute | solution.py:365
  9.7 3.4 %copy-done = bf16[4,2,2,512,512]{4,3,2,1,0:T(8,128)(2,1)S(1)} copy-done((bf16[4,2,2,512,512]{4,3,2,1,0:T(8,128)(2,1)S(1)}, bf16[4,2,2,512,512]{4,3,2,1,0:T(8,128)(2,1)}, u32[]{:S(2)}) %copy-start) | copy-done | bytes 8388632
  13.1 4.9 %shard_map.46 = (bf16[2,2,2,64,512]{4,3,2,1,0:T(8,128)(2,1)S(1)}, bf16[2,2,2,64,512]{4,3,2,1,0:T(8,128)(2,1)S(1)}, bf16[2,2,2,64,512]{4,3,2,1,0:T(8,128)(2,1)S(1)}, bf16[2,2,2,64,512]{4,3,2,1,0:T(8,128)(2,1)S(1)}) custom-call(s32[7]{0:T(128)S(1)} %copy-done.2, bf16[4,2,2,512,512]{4,3,2,1,0:T(8,128)(2,1)S(1)} %copy-done), custom_call_target="tpu_custom_call" | custom-call | flops 2147483648 | bytes 4194304 | tf_op jit(solution)/shard_map/pallas_call | solution.py:43
  18.0 1.3 %collective-permute-start = (bf16[2,2,2,64,512]{4,3,2,1,0:T(8,128)(2,1)S(1)}, bf16[2,2,2,64,512]{4,3,2,1,0:T(8,128)(2,1)S(1)}, u32[]{:S(2)}, u32[]{:S(2)}) collective-permute-start(bf16[2,2,2,64,512]{4,3,2,1,0:T(8,128)(2,1)S(1)} %get-tuple-element.22), channel_id=1, source_target_pairs={{0,2},{2,0},{4,6},{6,4},{8,10},{10,8},{12,14},{14,12},{1,3},{3,1},... | collective-permute-start | bytes 1572872 | tf_op jit(solution)/shard_map/ppermute | solution.py:366
  22.6 8.6 %collective-permute-done.9.refs_3_ = bf16[2,2,2,64,512]{4,3,2,1,0:T(8,128)(2,1)S(1)} collective-permute-done((bf16[2,2,2,64,512]{4,3,2,1,0:T(8,128)(2,1)}, bf16[2,2,2,64,512]{4,3,2,1,0:T(8,128)(2,1)S(1)}, u32[]{:S(2)}, u32[]{:S(2)}) %collective-permute-start.9) | collective-permute-done | bytes 524320 | tf_op jit(solution)/shard_map/ppermute | solution.py:364
  32.4 10.0 %collective-permute-done.refs_1_ = bf16[2,2,2,64,512]{4,3,2,1,0:T(8,128)(2,1)S(1)} collective-permute-done((bf16[2,2,2,64,512]{4,3,2,1,0:T(8,128)(2,1)S(1)}, bf16[2,2,2,64,512]{4,3,2,1,0:T(8,128)(2,1)S(1)}, u32[]{:S(2)}, u32[]{:S(2)}) %collective-permute-start) | collective-permute-done | bytes 524320 | tf_op jit(solution)/shard_map/ppermute | solution.py:366
  42.5 2.4 %shard_map.48 = (bf16[2,2,64,512]{3,2,1,0:T(8,128)(2,1)S(1)}, bf16[2,2,64,512]{3,2,1,0:T(8,128)(2,1)S(1)}, bf16[2,2,64,512]{3,2,1,0:T(8,128)(2,1)S(1)}, bf16[2,2,64,512]{3,2,1,0:T(8,128)(2,1)S(1)}) custom-call(bf16[2,2,2,64,512]{4,3,2,1,0:T(8,128)(2,1)S(1)} %get-tuple-element.21.refs_0_, bf16[2,2,2,64,512]{4,3,2,1,0:T(8,128)(2,1)S(1)} %collective-permute-done.refs_1_, ...), custom_call_target="tpu_custom_call" | custom-call | flops 1073741824 | bytes 3145728 | tf_op jit(solution)/shard_map/pallas_call | solution.py:43
  44.9 2.1 %collective-permute-start.5 = (bf16[2,2,64,512]{3,2,1,0:T(8,128)(2,1)S(1)}, bf16[2,2,64,512]{3,2,1,0:T(8,128)(2,1)S(1)}, u32[]{:S(2)}, u32[]{:S(2)}) collective-permute-start(bf16[2,2,64,512]{3,2,1,0:T(8,128)(2,1)S(1)} %get-tuple-element.26), channel_id=1, source_target_pairs={{0,2},{1,0},{2,3},{3,1},{4,10},{5,8},{6,11},{7,9},{8,6},{9,4},{10,... | collective-permute-start | bytes 786440 | tf_op jit(solution)/shard_map/ppermute | solution.py:385
  47.1 2.7 %collective-permute-start.6 = (bf16[2,2,64,512]{3,2,1,0:T(8,128)(2,1)S(1)}, bf16[2,2,64,512]{3,2,1,0:T(8,128)(2,1)S(1)}, u32[]{:S(2)}, u32[]{:S(2)}) collective-permute-start(bf16[2,2,64,512]{3,2,1,0:T(8,128)(2,1)S(1)} %get-tuple-element.27), channel_id=1, source_target_pairs={{0,4},{1,6},{2,5},{3,7},{4,12},{5,14},{6,13},{7,15},{8,0},{9,2},{1... | collective-permute-start | bytes 786440 | tf_op jit(solution)/shard_map/ppermute | solution.py:385
  49.8 3.1 %collective-permute-start.7 = (bf16[2,2,64,512]{3,2,1,0:T(8,128)(2,1)S(1)}, bf16[2,2,64,512]{3,2,1,0:T(8,128)(2,1)S(1)}, u32[]{:S(2)}, u32[]{:S(2)}) collective-permute-start(bf16[2,2,64,512]{3,2,1,0:T(8,128)(2,1)S(1)} %get-tuple-element.28), channel_id=1, source_target_pairs={{0,6},{1,4},{2,7},{3,5},{4,14},{5,12},{6,15},{7,13},{8,2},{9,0},{1... | collective-permute-start | bytes 786440 | tf_op jit(solution)/shard_map/ppermute | solution.py:385
  53.7 4.5 %collective-permute-start.4 = (bf16[2,2,64,512]{3,2,1,0:T(8,128)(2,1)S(1)}, bf16[2,2,64,512]{3,2,1,0:T(8,128)(2,1)S(1)}, u32[]{:S(2)}, u32[]{:S(2)}) collective-permute-start(bf16[2,2,64,512]{3,2,1,0:T(8,128)(2,1)S(1)} %get-tuple-element.25), channel_id=1, source_target_pairs={{0,0},{1,2},{2,1},{3,3},{4,8},{5,10},{6,9},{7,11},{8,4},{9,6},{10,... | collective-permute-start | bytes 786440 | tf_op jit(solution)/shard_map/ppermute | solution.py:385
  58.2 5.3 %collective-permute-done.6.refs_7_.refs_2_ = bf16[2,2,64,512]{3,2,1,0:T(8,128)(2,1)S(1)} collective-permute-done((bf16[2,2,64,512]{3,2,1,0:T(8,128)(2,1)S(1)}, bf16[2,2,64,512]{3,2,1,0:T(8,128)(2,1)S(1)}, u32[]{:S(2)}, u32[]{:S(2)}) %collective-permute-start.6) | collective-permute-done | bytes 262176 | tf_op jit(solution)/shard_map/ppermute | solution.py:385
  63.5 2.4 %shard_map.49 = (bf16[2,2,64,512]{3,2,1,0:T(8,128)(2,1)S(1)}, bf16[2,2,64,512]{3,2,1,0:T(8,128)(2,1)S(1)}, bf16[2,2,64,512]{3,2,1,0:T(8,128)(2,1)S(1)}, bf16[2,2,64,512]{3,2,1,0:T(8,128)(2,1)S(1)}) custom-call(bf16[2,2,2,64,512]{4,3,2,1,0:T(8,128)(2,1)S(1)} %get-tuple-element.29.refs_0_, bf16[2,2,2,64,512]{4,3,2,1,0:T(8,128)(2,1)S(1)} %collective-permute-done.8.refs_1_, ...), custom_call_target="tpu_custom_call" | custom-call | flops 1073741824 | bytes 3145728 | tf_op jit(solution)/shard_map/pallas_call | solution.py:43
  66.0 8.8 %collective-permute-start.12 = (bf16[2,2,64,512]{3,2,1,0:T(8,128)(2,1)S(1)}, bf16[2,2,64,512]{3,2,1,0:T(8,128)(2,1)S(1)}, u32[]{:S(2)}, u32[]{:S(2)}) collective-permute-start(bf16[2,2,64,512]{3,2,1,0:T(8,128)(2,1)S(1)} %get-tuple-element.33), channel_id=1, source_target_pairs={{0,0},{1,2},{2,1},{3,3},{4,8},{5,10},{6,9},{7,11},{8,4},{9,6},{10,... | collective-permute-start | bytes 786440 | tf_op jit(solution)/shard_map/ppermute | solution.py:385
  76.1 1.9 %collective-permute-start.15 = (bf16[2,2,64,512]{3,2,1,0:T(8,128)(2,1)S(1)}, bf16[2,2,64,512]{3,2,1,0:T(8,128)(2,1)S(1)}, u32[]{:S(2)}, u32[]{:S(2)}) collective-permute-start(bf16[2,2,64,512]{3,2,1,0:T(8,128)(2,1)S(1)} %get-tuple-element.36), channel_id=1, source_target_pairs={{0,6},{1,4},{2,7},{3,5},{4,14},{5,12},{6,15},{7,13},{8,2},{9,0},{1... | collective-permute-start | bytes 786440 | tf_op jit(solution)/shard_map/ppermute | solution.py:385
  78.0 2.4 %collective-permute-done.12.refs_4_ = bf16[2,2,64,512]{3,2,1,0:T(8,128)(2,1)S(1)} collective-permute-done((bf16[2,2,64,512]{3,2,1,0:T(8,128)(2,1)S(1)}, bf16[2,2,64,512]{3,2,1,0:T(8,128)(2,1)S(1)}, u32[]{:S(2)}, u32[]{:S(2)}) %collective-permute-start.12) | collective-permute-done | bytes 262176 | tf_op jit(solution)/shard_map/ppermute | solution.py:385
  81.6 13.3 %collective-permute-done.14.refs_6_ = bf16[2,2,64,512]{3,2,1,0:T(8,128)(2,1)S(1)} collective-permute-done((bf16[2,2,64,512]{3,2,1,0:T(8,128)(2,1)S(1)}, bf16[2,2,64,512]{3,2,1,0:T(8,128)(2,1)S(1)}, u32[]{:S(2)}, u32[]{:S(2)}) %collective-permute-start.14) | collective-permute-done | bytes 262176 | tf_op jit(solution)/shard_map/ppermute | solution.py:385
  95.0 3.5 %collective-permute-done.15.refs_7_ = bf16[2,2,64,512]{3,2,1,0:T(8,128)(2,1)S(1)} collective-permute-done((bf16[2,2,64,512]{3,2,1,0:T(8,128)(2,1)S(1)}, bf16[2,2,64,512]{3,2,1,0:T(8,128)(2,1)S(1)}, u32[]{:S(2)}, u32[]{:S(2)}) %collective-permute-start.15) | collective-permute-done | bytes 262176 | tf_op jit(solution)/shard_map/ppermute | solution.py:385
  98.5 1.6 %shard_map.50 = bf16[2,256,512]{2,1,0:T(8,128)(2,1)S(1)} custom-call(s32[7]{0:T(128)S(1)} %copy-done.2, bf16[2,2,64,512]{3,2,1,0:T(8,128)(2,1)S(1)} %collective-permute-done.4.refs_0_, bf16[2,2,64,512]{3,2,1,0:T(8,128)(2,1)S(1)} %collective-permute-done.5.refs_8_.refs_1_, bf16[2,2,64,512]{3,2,1,0:T(8,128)(2,1)S(1)} %collective-permute-done.6.refs_7_.refs_2_, ...), custom_call_target="tpu_custom_call" | custom-call | flops 536870912 | bytes 2621440 | tf_op jit(solution)/shard_map/pallas_call | solution.py:43
  100.0 2.6 %collective-permute-start.16 = (bf16[2,256,512]{2,1,0:T(8,128)(2,1)S(1)}, bf16[2,256,512]{2,1,0:T(8,128)(2,1)S(1)}, u32[]{:S(2)}, u32[]{:S(2)}) collective-permute-start(bf16[2,256,512]{2,1,0:T(8,128)(2,1)S(1)} %shard_map.50), channel_id=1, source_target_pairs={{0,1},{1,0},{2,3},{3,2},{4,5},{5,4},{6,7},{7,6},{8,9},{9,8},{10,11... | collective-permute-start | bytes 1572872 | tf_op jit(solution)/shard_map/ppermute | solution.py:389
  102.6 3.3 %shard_map.51._ = f32[2,2,256,512]{3,2,1,0:T(8,128)} custom-call(s32[7]{0:T(128)S(1)} %copy-done.2, s32[2]{0:T(128)S(1)} %copy-done.3, bf16[2,2,512,512]{3,2,1,0:T(8,128)(2,1)S(1)} %copy-done.1, bf16[2,2,64,512]{3,2,1,0:T(8,128)(2,1)S(1)} %collective-permute-done.4.refs_0_, bf16[2,2,64,512]{3,2,1,0:T(8,128)(2,1)S(1)} %collective-permute-done.5.refs_8_.refs_1_, ...), custom_call_target="tpu_custom_call" | custom-call | flops 1073741824 | bytes 4194304 | tf_op jit(solution)/shard_map/pallas_call | solution.py:43
  105.9 2.4 %shard_map.52 = f32[2,2,256,512]{3,2,1,0:T(8,128)} custom-call(s32[2]{0:T(128)S(1)} %copy-done.3, bf16[2,2,512,512]{3,2,1,0:T(8,128)(2,1)S(1)} %copy-done.1, bf16[2,256,512]{2,1,0:T(8,128)(2,1)S(1)} %collective-permute-done.16.top, f32[2,2,256,512]{3,2,1,0:T(8,128)} %shard_map.51._), custom_call_target="tpu_custom_call", output_to_operand_aliasing={{}: (3, {})} | custom-call | flops 536870912 | bytes 4194304 | tf_op jit(solution)/shard_map/pallas_call | solution.py:43
  (29 shorter events, 8.3 us)
Async XLA Ops:
  0.0 9.7 %copy-start.2 = (s32[7]{0:T(128)S(1)}, s32[7]{0:T(128)}, u32[]{:S(2)}) copy-start(s32[7]{0:T(128)} %order.7) | copy-start | bytes 88
  6.0 14.0 %collective-permute-start.1 = (bf16[2,2,2,64,512]{4,3,2,1,0:T(8,128)(2,1)}, bf16[2,2,2,64,512]{4,3,2,1,0:T(8,128)(2,1)S(1)}, u32[]{:S(2)}, u32[]{:S(2)}) collective-permute-start(bf16[2,2,2,64,512]{4,3,2,1,0:T(8,128)(2,1)} %get-tuple-element.24), channel_id=1, source_target_pairs={{0,2},{2,0},{4,6},{6,4},{8,10},{10,8},{12,14},{14,12},{1,3},{3,1},... | collective-permute-start | bytes 1572872 | tf_op jit(solution)/shard_map/ppermute | solution.py:364
  8.2 13.3 %collective-permute-start.2 = (bf16[2,2,2,64,512]{4,3,2,1,0:T(8,128)(2,1)}, bf16[2,2,2,64,512]{4,3,2,1,0:T(8,128)(2,1)S(1)}, u32[]{:S(2)}, u32[]{:S(2)}) collective-permute-start(bf16[2,2,2,64,512]{4,3,2,1,0:T(8,128)(2,1)} %get-tuple-element.23.refs_2_), channel_id=1, source_target_pairs={{0,4},{2,6},{4,0},{6,2},{8,12},{10,14},{12,8},{14,10},{1,5},{3,7},... | collective-permute-start | bytes 1572872 | tf_op jit(solution)/shard_map/ppermute | solution.py:365
  9.4 21.8 %collective-permute-start.9 = (bf16[2,2,2,64,512]{4,3,2,1,0:T(8,128)(2,1)}, bf16[2,2,2,64,512]{4,3,2,1,0:T(8,128)(2,1)S(1)}, u32[]{:S(2)}, u32[]{:S(2)}) collective-permute-start(bf16[2,2,2,64,512]{4,3,2,1,0:T(8,128)(2,1)} %get-tuple-element.32), channel_id=1, source_target_pairs={{0,2},{2,0},{4,6},{6,4},{8,10},{10,8},{12,14},{14,12},{1,3},{3,1},... | collective-permute-start | bytes 1572872 | tf_op jit(solution)/shard_map/ppermute | solution.py:364
  9.7 3.4 %copy-start = (bf16[4,2,2,512,512]{4,3,2,1,0:T(8,128)(2,1)S(1)}, bf16[4,2,2,512,512]{4,3,2,1,0:T(8,128)(2,1)}, u32[]{:S(2)}) copy-start(bf16[4,2,2,512,512]{4,3,2,1,0:T(8,128)(2,1)} %leaf.3) | copy-start | bytes 25165828
  13.1 8.2 %copy-start.4 = (bf16[2,2,2,64,512]{4,3,2,1,0:T(8,128)(2,1)S(1)}, bf16[2,2,2,64,512]{4,3,2,1,0:T(8,128)(2,1)}, u32[]{:S(2)}) copy-start(bf16[2,2,2,64,512]{4,3,2,1,0:T(8,128)(2,1)} %get-tuple-element.31.refs_2_) | copy-start | bytes 1572868
  13.1 29.4 %copy-start.5 = (bf16[2,2,2,64,512]{4,3,2,1,0:T(8,128)(2,1)S(1)}, bf16[2,2,2,64,512]{4,3,2,1,0:T(8,128)(2,1)}, u32[]{:S(2)}) copy-start(bf16[2,2,2,64,512]{4,3,2,1,0:T(8,128)(2,1)} %get-tuple-element.23.refs_2_) | copy-start | bytes 1572868
  18.0 24.5 %collective-permute-start = (bf16[2,2,2,64,512]{4,3,2,1,0:T(8,128)(2,1)S(1)}, bf16[2,2,2,64,512]{4,3,2,1,0:T(8,128)(2,1)S(1)}, u32[]{:S(2)}, u32[]{:S(2)}) collective-permute-start(bf16[2,2,2,64,512]{4,3,2,1,0:T(8,128)(2,1)S(1)} %get-tuple-element.22), channel_id=1, source_target_pairs={{0,2},{2,0},{4,6},{6,4},{8,10},{10,8},{12,14},{14,12},{1,3},{3,1},... | collective-permute-start | bytes 1572872 | tf_op jit(solution)/shard_map/ppermute | solution.py:366
  20.0 22.5 %collective-permute-start.3 = (bf16[2,2,2,64,512]{4,3,2,1,0:T(8,128)(2,1)S(1)}, bf16[2,2,2,64,512]{4,3,2,1,0:T(8,128)(2,1)S(1)}, u32[]{:S(2)}, u32[]{:S(2)}) collective-permute-start(bf16[2,2,2,64,512]{4,3,2,1,0:T(8,128)(2,1)S(1)} %collective-permute-done.1.refs_3_), channel_id=1, source_target_pairs={{0,4},{2,6},{4,0},{6,2},{8,12},{10,14},{12,8},{14,10},{1,5},{3,7},... | collective-permute-start | bytes 1572872 | tf_op jit(solution)/shard_map/ppermute | solution.py:367
  21.2 28.6 %collective-permute-start.10 = (bf16[2,2,2,64,512]{4,3,2,1,0:T(8,128)(2,1)S(1)}, bf16[2,2,2,64,512]{4,3,2,1,0:T(8,128)(2,1)S(1)}, u32[]{:S(2)}, u32[]{:S(2)}) collective-permute-start(bf16[2,2,2,64,512]{4,3,2,1,0:T(8,128)(2,1)S(1)} %copy-done.4), channel_id=1, source_target_pairs={{0,4},{2,6},{4,0},{6,2},{8,12},{10,14},{12,8},{14,10},{1,5},{3,7},... | collective-permute-start | bytes 1572872 | tf_op jit(solution)/shard_map/ppermute | solution.py:365
  21.5 32.2 %collective-permute-start.8 = (bf16[2,2,2,64,512]{4,3,2,1,0:T(8,128)(2,1)S(1)}, bf16[2,2,2,64,512]{4,3,2,1,0:T(8,128)(2,1)S(1)}, u32[]{:S(2)}, u32[]{:S(2)}) collective-permute-start(bf16[2,2,2,64,512]{4,3,2,1,0:T(8,128)(2,1)S(1)} %get-tuple-element.30), channel_id=1, source_target_pairs={{0,2},{2,0},{4,6},{6,4},{8,10},{10,8},{12,14},{14,12},{1,3},{3,1},... | collective-permute-start | bytes 1572872 | tf_op jit(solution)/shard_map/ppermute | solution.py:366
  31.2 27.0 %collective-permute-start.11 = (bf16[2,2,2,64,512]{4,3,2,1,0:T(8,128)(2,1)S(1)}, bf16[2,2,2,64,512]{4,3,2,1,0:T(8,128)(2,1)S(1)}, u32[]{:S(2)}, u32[]{:S(2)}) collective-permute-start(bf16[2,2,2,64,512]{4,3,2,1,0:T(8,128)(2,1)S(1)} %collective-permute-done.9.refs_3_), channel_id=1, source_target_pairs={{0,4},{2,6},{4,0},{6,2},{8,12},{10,14},{12,8},{14,10},{1,5},{3,7},... | collective-permute-start | bytes 1572872 | tf_op jit(solution)/shard_map/ppermute | solution.py:367
  44.9 13.3 %collective-permute-start.5 = (bf16[2,2,64,512]{3,2,1,0:T(8,128)(2,1)S(1)}, bf16[2,2,64,512]{3,2,1,0:T(8,128)(2,1)S(1)}, u32[]{:S(2)}, u32[]{:S(2)}) collective-permute-start(bf16[2,2,64,512]{3,2,1,0:T(8,128)(2,1)S(1)} %get-tuple-element.26), channel_id=1, source_target_pairs={{0,2},{1,0},{2,3},{3,1},{4,10},{5,8},{6,11},{7,9},{8,6},{9,4},{10,... | collective-permute-start | bytes 786440 | tf_op jit(solution)/shard_map/ppermute | solution.py:385
  47.1 16.4 %collective-permute-start.6 = (bf16[2,2,64,512]{3,2,1,0:T(8,128)(2,1)S(1)}, bf16[2,2,64,512]{3,2,1,0:T(8,128)(2,1)S(1)}, u32[]{:S(2)}, u32[]{:S(2)}) collective-permute-start(bf16[2,2,64,512]{3,2,1,0:T(8,128)(2,1)S(1)} %get-tuple-element.27), channel_id=1, source_target_pairs={{0,4},{1,6},{2,5},{3,7},{4,12},{5,14},{6,13},{7,15},{8,0},{9,2},{1... | collective-permute-start | bytes 786440 | tf_op jit(solution)/shard_map/ppermute | solution.py:385
  49.8 13.7 %collective-permute-start.7 = (bf16[2,2,64,512]{3,2,1,0:T(8,128)(2,1)S(1)}, bf16[2,2,64,512]{3,2,1,0:T(8,128)(2,1)S(1)}, u32[]{:S(2)}, u32[]{:S(2)}) collective-permute-start(bf16[2,2,64,512]{3,2,1,0:T(8,128)(2,1)S(1)} %get-tuple-element.28), channel_id=1, source_target_pairs={{0,6},{1,4},{2,7},{3,5},{4,14},{5,12},{6,15},{7,13},{8,2},{9,0},{1... | collective-permute-start | bytes 786440 | tf_op jit(solution)/shard_map/ppermute | solution.py:385
  53.7 24.3 %collective-permute-start.4 = (bf16[2,2,64,512]{3,2,1,0:T(8,128)(2,1)S(1)}, bf16[2,2,64,512]{3,2,1,0:T(8,128)(2,1)S(1)}, u32[]{:S(2)}, u32[]{:S(2)}) collective-permute-start(bf16[2,2,64,512]{3,2,1,0:T(8,128)(2,1)S(1)} %get-tuple-element.25), channel_id=1, source_target_pairs={{0,0},{1,2},{2,1},{3,3},{4,8},{5,10},{6,9},{7,11},{8,4},{9,6},{10,... | collective-permute-start | bytes 786440 | tf_op jit(solution)/shard_map/ppermute | solution.py:385
  66.0 36.6 %copy-start.1 = (bf16[2,2,512,512]{3,2,1,0:T(8,128)(2,1)S(1)}, bf16[2,2,512,512]{3,2,1,0:T(8,128)(2,1)}, u32[]{:S(2)}) copy-start(bf16[2,2,512,512]{3,2,1,0:T(8,128)(2,1)} %bound.3) | copy-start | bytes 6291460
  66.0 36.6 %copy-start.3 = (s32[2]{0:T(128)S(1)}, s32[2]{0:T(128)}, u32[]{:S(2)}) copy-start(s32[2]{0:T(128)} %values.3) | copy-start | bytes 28
  66.0 14.4 %collective-permute-start.12 = (bf16[2,2,64,512]{3,2,1,0:T(8,128)(2,1)S(1)}, bf16[2,2,64,512]{3,2,1,0:T(8,128)(2,1)S(1)}, u32[]{:S(2)}, u32[]{:S(2)}) collective-permute-start(bf16[2,2,64,512]{3,2,1,0:T(8,128)(2,1)S(1)} %get-tuple-element.33), channel_id=1, source_target_pairs={{0,0},{1,2},{2,1},{3,3},{4,8},{5,10},{6,9},{7,11},{8,4},{9,6},{10,... | collective-permute-start | bytes 786440 | tf_op jit(solution)/shard_map/ppermute | solution.py:385
  74.8 6.8 %collective-permute-start.13 = (bf16[2,2,64,512]{3,2,1,0:T(8,128)(2,1)S(1)}, bf16[2,2,64,512]{3,2,1,0:T(8,128)(2,1)S(1)}, u32[]{:S(2)}, u32[]{:S(2)}) collective-permute-start(bf16[2,2,64,512]{3,2,1,0:T(8,128)(2,1)S(1)} %get-tuple-element.34), channel_id=1, source_target_pairs={{0,2},{1,0},{2,3},{3,1},{4,10},{5,8},{6,11},{7,9},{8,6},{9,4},{10,... | collective-permute-start | bytes 786440 | tf_op jit(solution)/shard_map/ppermute | solution.py:385
  74.9 20.1 %collective-permute-start.14 = (bf16[2,2,64,512]{3,2,1,0:T(8,128)(2,1)S(1)}, bf16[2,2,64,512]{3,2,1,0:T(8,128)(2,1)S(1)}, u32[]{:S(2)}, u32[]{:S(2)}) collective-permute-start(bf16[2,2,64,512]{3,2,1,0:T(8,128)(2,1)S(1)} %get-tuple-element.35), channel_id=1, source_target_pairs={{0,4},{1,6},{2,5},{3,7},{4,12},{5,14},{6,13},{7,15},{8,0},{9,2},{1... | collective-permute-start | bytes 786440 | tf_op jit(solution)/shard_map/ppermute | solution.py:385
  76.1 22.3 %collective-permute-start.15 = (bf16[2,2,64,512]{3,2,1,0:T(8,128)(2,1)S(1)}, bf16[2,2,64,512]{3,2,1,0:T(8,128)(2,1)S(1)}, u32[]{:S(2)}, u32[]{:S(2)}) collective-permute-start(bf16[2,2,64,512]{3,2,1,0:T(8,128)(2,1)S(1)} %get-tuple-element.36), channel_id=1, source_target_pairs={{0,6},{1,4},{2,7},{3,5},{4,14},{5,12},{6,15},{7,13},{8,2},{9,0},{1... | collective-permute-start | bytes 786440 | tf_op jit(solution)/shard_map/ppermute | solution.py:385
  100.0 5.9 %collective-permute-start.16 = (bf16[2,256,512]{2,1,0:T(8,128)(2,1)S(1)}, bf16[2,256,512]{2,1,0:T(8,128)(2,1)S(1)}, u32[]{:S(2)}, u32[]{:S(2)}) collective-permute-start(bf16[2,256,512]{2,1,0:T(8,128)(2,1)S(1)} %shard_map.50), channel_id=1, source_target_pairs={{0,1},{1,0},{2,3},{3,2},{4,5},{5,4},{6,7},{7,6},{8,9},{9,8},{10,11... | collective-permute-start | bytes 1572872 | tf_op jit(solution)/shard_map/ppermute | solution.py:389

commit v4 on v3

--- a/solution.py
+++ b/solution.py
@@ -62,6 +62,7 @@
         self.ways = self.batch
         self.places = self.size // self.ways
         assert self.batch == 2 and lax.axis_size("branch") == 2
+        self.steps = [(1, 1), (1, 0), (0, 1), (0, 0)]
 
     def mode_of(self, high, place, way):
         return (high * self.places + place) * self.ways + way
@@ -71,70 +72,77 @@
         return mode // self.size, (mode % self.size) // self.ways, mode % self.ways
 
 
-def first_level(plan, leaves, join_order, role, parts, limit):
+def first_level(plan, leaves, join_order, jobs, limit):
     width, batch, rows, ways = plan.width, plan.batch, plan.rows, plan.ways
     half = width // ways
+    chunks = [blocks for _, _, parts in jobs for blocks in parts]
+    totals = [sum(parts) * rows for _, _, parts in jobs]
 
     def body(order, leaf, *rest):
-        outs, (upper, lower, result, sems) = rest[:-4], rest[-4:]
-        copies = Copies(sems)
+        outs, rest = rest[: 2 * len(chunks)], rest[2 * len(chunks) :]
+        copies = Copies(rest[-1])
         branch = lax.axis_index("branch")
         _, _, way = plan.here()
-        pair = jnp.where(order[2 * lax.axis_size("branch") + branch] == 1, 1 - role, role)
-        swapped = jnp.where(order[2 * branch + pair] == 1, 1, 0)
-        first, second = 2 * pair + swapped, 2 * pair + 1 - swapped
-        loads = [
-            [
-                copies.start(leaf.at[second, :, item], lower.at[item]),
-                copies.start(leaf.at[first, :, item], upper.at[item]),
-            ]
-            for item in range(batch)
-        ]
+        loads = []
+        for index, (role, begin, parts) in enumerate(jobs):
+            upper, lower, _ = rest[3 * index : 3 * index + 3]
+            pair = jnp.where(order[2 * lax.axis_size("branch") + branch] == 1, 1 - role, role)
+            swapped = jnp.where(order[2 * branch + pair] == 1, 1, 0)
+            first, second = 2 * pair + swapped, 2 * pair + 1 - swapped
+            for item in range(batch):
+                mine = [copies.start(leaf.at[second, :, item], lower.at[item])]
+                for side, target in enumerate((way, 1 - way)):
+                    span = pl.ds(target * half + begin * rows, totals[index])
+                    source = leaf.at[first, :, item, span]
+                    mine.append(copies.start(source, upper.at[item, :, side]))
+                loads.append(mine)
         stores = []
-        for item in range(batch):
-            for copy in loads[item]:
-                copy.wait()
-            sums = complex_dot(
-                upper[item, 0], upper[item, 1], lower[item].reshape(2 * width, width)
-            )
-            for part in range(2):
-                result[item, part] = sums[part].astype(jnp.bfloat16)
-            for side, target in enumerate((way, 1 - way)):
-                begin = 0
-                for chunk, blocks in enumerate(parts):
-                    for block in range(blocks):
-                        source = result.at[item, :, pl.ds(target * half + begin, rows)]
-                        place = outs[2 * chunk + side].at[:, block, item]
-                        stores.append(copies.start(source, place))
-                        begin += rows
+        given = 0
+        for index, (role, begin, parts) in enumerate(jobs):
+            upper, lower, result = rest[3 * index : 3 * index + 3]
+            total = totals[index]
+            for item in range(batch):
+                for copy in loads[index * batch + item]:
+                    copy.wait()
+                sums = complex_dot(
+                    upper[item, 0].reshape(ways * total, width),
+                    upper[item, 1].reshape(ways * total, width),
+                    lower[item].reshape(2 * width, width),
+                )
+                for part in range(2):
+                    result[item, part] = (
+                        sums[part].astype(jnp.bfloat16).reshape(ways, total, width)
+                    )
+                for side in range(ways):
+                    done = 0
+                    for chunk, blocks in enumerate(parts):
+                        for block in range(blocks):
+                            source = result.at[item, :, side, pl.ds(done, rows)]
+                            place = outs[2 * (given + chunk) + side].at[:, block, item]
+                            stores.append(copies.start(source, place))
+                            done += rows
+            given += len(parts)
         for copy in stores:
             copy.wait()
 
     outs = [
         jax.ShapeDtypeStruct((2, blocks, batch, rows, width), jnp.bfloat16)
-        for blocks in parts
+        for blocks in chunks
         for _ in range(ways)
     ]
-    scratch = [pltpu.VMEM((batch, 2, width, width), jnp.bfloat16) for _ in range(3)]
-    copies = 2 * batch + batch * ways * sum(parts)
-    flops = 8 * batch * width**3
+    scratch = []
+    for total in totals:
+        scratch += [
+            pltpu.VMEM((batch, 2, ways, total, width), jnp.bfloat16),
+            pltpu.VMEM((batch, 2, width, width), jnp.bfloat16),
+            pltpu.VMEM((batch, 2, ways, total, width), jnp.bfloat16),
+        ]
+    copies = len(jobs) * batch * (1 + ways) + batch * ways * sum(chunks)
+    flops = 8 * batch * ways * sum(totals) * width**2
     results = run_kernel(
         body, outs, scratch, copies, flops, [join_order, leaves], [SMEM, ANY], limit=limit
     )
-    return [results[2 * index : 2 * index + 2] for index in range(len(parts))]
-
-
-def once_arrived(value, after):
-    def body(*refs):
-        pass
-
-    return pl.pallas_call(
-        body,
-        out_shape=jax.ShapeDtypeStruct(value.shape, value.dtype),
-        in_specs=[ANY] * (1 + len(after)),
-        out_specs=ANY,
-        input_output_aliases={0: 0},
-    )(value, *after)
+    return [results[2 * index : 2 * index + 2] for index in range(len(chunks))]
 
 
 def second_level(plan, blocks, operands, pick):
@@ -160,11 +168,10 @@
             loads.append(copies.start(sent, right.at[:, :, other, 1 - way]))
         for copy in loads:
             copy.wait()
-        steps = [(a, b) for a in range(ways) for b in range(batch)]
         stores = []
         for block in range(blocks):
             halves = [
-                jnp.concatenate([left[part, block, high ^ a, branch ^ b] for a, b in steps], axis=0)
+                jnp.concatenate([left[part, block, high ^ a, branch ^ b] for a, b in plan.steps], axis=0)
                 for part in range(2)
             ]
             parts = complex_dot(
@@ -194,15 +201,14 @@
     return run_kernel(body, outs, scratch, copies, flops, operands, [ANY] * len(operands))
 
 
-def load_operands(plan, copies, order, messages, chunk_blocks, scratch, keep):
+def load_operands(plan, copies, order, messages, chunk_blocks, scratch):
     mode = lax.axis_index("mode")
     near, item = (mode // plan.batch) % plan.ways, mode % plan.batch
     top = jnp.where(order[order.shape[0] - 1] == 1, 1, 0)
-    steps = [(a, b) for a in range(plan.ways) for b in range(plan.batch)]
     loads = []
     begin = 0
     for chunk, blocks in zip(messages, chunk_blocks):
-        for (a, b), message in zip(steps, chunk):
+        for (a, b), message in zip(plan.steps, chunk):
             role = item ^ b ^ top
             loads.append(
                 copies.start(message, scratch.at[role, :, pl.ds(begin, blocks), near ^ a])
@@ -235,7 +241,7 @@
         sources, (out, operands, result, sems) = refs[: len(flat)], refs[len(flat) :]
         copies = Copies(sems)
         grouped = [sources[i : i + count] for i in range(0, len(flat), count)]
-        for copy in load_operands(plan, copies, order, grouped, chunk_blocks, operands, None):
+        for copy in load_operands(plan, copies, order, grouped, chunk_blocks, operands):
             copy.wait()
         parts = complex_dot(*top_operands(plan, operands, 1 - lax.axis_index("branch")))
         for part in range(2):
@@ -265,7 +271,7 @@
         copies = Copies(sems)
         core = lax.axis_index("branch")
         grouped = [sources[i : i + count] for i in range(0, len(flat), count)]
-        loads = load_operands(plan, copies, order, grouped, chunk_blocks, operands, None)
+        loads = load_operands(plan, copies, order, grouped, chunk_blocks, operands)
         value = jnp.where(values[core] == 1, 1, 0)
         late = copies.start(bound.at[value], chosen)
         for copy in loads:
@@ -350,13 +356,15 @@
                 pairs.append((plan.mode_of(h, p, w) * 2 + k, target * 2 + w))
         return pairs
 
-    parts = [plan.size // 2] * 2
-    right = first_level(plan, leaves, join_order, 1, parts, VMEM_MOST)
-    left = first_level(plan, leaves, join_order, 0, parts, VMEM_LIMIT)
+    quarter = plan.size // 4
+    parts = [x * quarter for x in (2,2,)]
+    now, later = parts[:1], parts[1:]
+    jobs = [(0, 0, parts), (1, sum(now), later)]
+    first = first_level(plan, leaves, join_order, [(1, 0, now)], VMEM_MOST)
+    rest = first_level(plan, leaves, join_order, jobs, VMEM_LIMIT)
+    left, right = rest[: len(parts)], first + rest[len(parts) :]
     others = range(1, places)
-    steps = [(a, b) for a in range(ways) for b in range(batch)]
     messages = []
-    order = list(range(len(steps)))[::-1]
     arrived = []
     for chunk, blocks in enumerate(parts):
         right_kept, right_sent = right[chunk]
@@ -372,7 +380,7 @@
             right_sent,
             *kept_there,
             *sent_there,
-            *arrived[:3],
+            *arrived[1:],
         ]
 
         def pick(refs):
@@ -382,9 +390,10 @@
 
         rows = second_level(plan, blocks, operands, pick)
         arrived = [
-            lax.ppermute(rows[i], ("mode", "branch"), to_rows(*steps[i])) for i in order
+            lax.ppermute(value, ("mode", "branch"), to_rows(a, b))
+            for value, (a, b) in zip(rows, plan.steps)
         ]
-        messages.append(arrived[::-1])
+        messages.append(arrived)
     top_other = top_for_other(plan, join_order, messages)
     top_received = lax.ppermute(top_other, "branch", [(0, 1), (1, 0)])
     amplitudes = own_amplitudes(plan, join_order, slice_values, boundary, messages)

time: 108 us -> 103 us (0.954)
  the two profiles are of different devices: /device:TPU:1 before, /device:TPU:9 now
where the time goes in v4:
time: 103 us
  waiting for transfers between devices  41.5 us (40%)
  starting transfers between devices  33.9 us (33%)
  Pallas kernels  23.9 us (23%)
  local copies, waits for them, and re-layouts  3.4 us (3%)
    ppermute x8, starting transfers between devices, per_device(): lax.ppermute(value, ('mode', 'branch'), to_rows(a, b))  25.1 us
    pallas_call x7, Pallas kernels, run_kernel(): pl.pallas_call(body, out_shape=outs, in_specs=specs, out_specs=[ANY] * le...  23.9 us
    ppermute x8, waiting for transfers between devices, per_device(): lax.ppermute(value, ('mode', 'branch'), to_rows(a, b))  20.7 us
    ppermute x2, waiting for transfers between devices, per_device(): left_sent = lax.ppermute(left_sent, 'mode', over_ways)  12.1 us
    ppermute x2, waiting for transfers between devices, per_device(): right_sent = lax.ppermute(right_sent, 'mode', over_ways)  8.72 us
    unnamed x10, local copies, waits for them, and re-layouts  3.4 us
    ppermute x2, starting transfers between devices, per_device(): lax.ppermute(right_sent, 'mode', over_places(step))  2.59 us
    ppermute x1, starting transfers between devices, per_device(): top_received = lax.ppermute(top_other, 'branch', [(0, 1), (1, 0)])  2.56 us
  transfers between devices with their start and end apart: 17, of which 8 were waited for; matrix products, arithmetic and copies ran while one was open for 0% of the time, Pallas kernels for 15%

profile of v4, /device:TPU:9, one launch (start us, length us, event | category | flops | bytes accessed | tf_op | source)
XLA Modules:
  0.0 102.9 jit_solution(4974964028964741666)
XLA Ops:
  0.0 4.5 %shard_map.47 = (bf16[2,2,2,64,512]{4,3,2,1,0:T(8,128)(2,1)}, bf16[2,2,2,64,512]{4,3,2,1,0:T(8,128)(2,1)}) custom-call(s32[7]{0:T(128)} %order.7, bf16[4,2,2,512,512]{4,3,2,1,0:T(8,128)(2,1)} %leaf.3), custom_call_target="tpu_custom_call" | custom-call | flops 1073741824 | bytes 3145728 | tf_op jit(solution)/shard_map/pallas_call | solution.py:43
  4.5 1.3 %collective-permute-start.1 = (bf16[2,2,2,64,512]{4,3,2,1,0:T(8,128)(2,1)}, bf16[2,2,2,64,512]{4,3,2,1,0:T(8,128)(2,1)S(1)}, u32[]{:S(2)}, u32[]{:S(2)}) collective-permute-start(bf16[2,2,2,64,512]{4,3,2,1,0:T(8,128)(2,1)} %get-tuple-element.24), channel_id=1, source_target_pairs={{0,2},{2,0},{4,6},{6,4},{8,10},{10,8},{12,14},{14,12},{1,3},{3,1},... | collective-permute-start | bytes 1572872 | tf_op jit(solution)/shard_map/ppermute | solution.py:372
  6.0 3.4 %copy-done = bf16[4,2,2,512,512]{4,3,2,1,0:T(8,128)(2,1)S(1)} copy-done((bf16[4,2,2,512,512]{4,3,2,1,0:T(8,128)(2,1)S(1)}, bf16[4,2,2,512,512]{4,3,2,1,0:T(8,128)(2,1)}, u32[]{:S(2)}) %copy-start) | copy-done | bytes 8388632
  9.4 7.4 %shard_map.46 = (bf16[2,2,2,64,512]{4,3,2,1,0:T(8,128)(2,1)S(1)}, bf16[2,2,2,64,512]{4,3,2,1,0:T(8,128)(2,1)S(1)}, bf16[2,2,2,64,512]{4,3,2,1,0:T(8,128)(2,1)S(1...) custom-call(s32[7]{0:T(128)S(1)} %copy-done.2, ...), custom_call_target="tpu_custom_call" | custom-call | flops 3221225472 | bytes 5242880 | tf_op jit(solution)/shard_map/pallas_call | solution.py:43
  16.9 1.4 %collective-permute-start = (bf16[2,2,2,64,512]{4,3,2,1,0:T(8,128)(2,1)S(1)}, bf16[2,2,2,64,512]{4,3,2,1,0:T(8,128)(2,1)S(1)}, u32[]{:S(2)}, u32[]{:S(2)}) collective-permute-start(bf16[2,2,2,64,512]{4,3,2,1,0:T(8,128)(2,1)S(1)} %get-tuple-element.22), channel_id=1, source_target_pairs={{0,2},{2,0},{4,6},{6,4},{8,10},{10,8},{12,14},{14,12},{1,3},{3,1},... | collective-permute-start | bytes 1572872 | tf_op jit(solution)/shard_map/ppermute | solution.py:374
  20.3 8.7 %collective-permute-done.9.refs_3_ = bf16[2,2,2,64,512]{4,3,2,1,0:T(8,128)(2,1)S(1)} collective-permute-done((bf16[2,2,2,64,512]{4,3,2,1,0:T(8,128)(2,1)S(1)}, bf16[2,2,2,64,512]{4,3,2,1,0:T(8,128)(2,1)S(1)}, u32[]{:S(2)}, u32[]{:S(2)}) %collective-permute-start.9) | collective-permute-done | bytes 524320 | tf_op jit(solution)/shard_map/ppermute | solution.py:372
  30.3 9.9 %collective-permute-done.refs_1_ = bf16[2,2,2,64,512]{4,3,2,1,0:T(8,128)(2,1)S(1)} collective-permute-done((bf16[2,2,2,64,512]{4,3,2,1,0:T(8,128)(2,1)S(1)}, bf16[2,2,2,64,512]{4,3,2,1,0:T(8,128)(2,1)S(1)}, u32[]{:S(2)}, u32[]{:S(2)}) %collective-permute-start) | collective-permute-done | bytes 524320 | tf_op jit(solution)/shard_map/ppermute | solution.py:374
  40.2 2.4 %shard_map.48 = (bf16[2,2,64,512]{3,2,1,0:T(8,128)(2,1)S(1)}, bf16[2,2,64,512]{3,2,1,0:T(8,128)(2,1)S(1)}, bf16[2,2,64,512]{3,2,1,0:T(8,128)(2,1)S(1)}, bf16[2,2,64,512]{3,2,1,0:T(8,128)(2,1)S(1)}) custom-call(bf16[2,2,2,64,512]{4,3,2,1,0:T(8,128)(2,1)S(1)} %get-tuple-element.21.refs_0_, bf16[2,2,2,64,512]{4,3,2,1,0:T(8,128)(2,1)S(1)} %collective-permute-done.refs_1_, ...), custom_call_target="tpu_custom_call" | custom-call | flops 1073741824 | bytes 3145728 | tf_op jit(solution)/shard_map/pallas_call | solution.py:43
  42.7 6.1 %collective-permute-start.5 = (bf16[2,2,64,512]{3,2,1,0:T(8,128)(2,1)S(1)}, bf16[2,2,64,512]{3,2,1,0:T(8,128)(2,1)S(1)}, u32[]{:S(2)}, u32[]{:S(2)}) collective-permute-start(bf16[2,2,64,512]{3,2,1,0:T(8,128)(2,1)S(1)} %get-tuple-element.26), channel_id=1, source_target_pairs={{0,4},{1,6},{2,5},{3,7},{4,12},{5,14},{6,13},{7,15},{8,0},{9,2},{1... | collective-permute-start | bytes 786440 | tf_op jit(solution)/shard_map/ppermute | solution.py:393
  49.3 2.2 %collective-permute-done.8.refs_1_ = bf16[2,2,2,64,512]{4,3,2,1,0:T(8,128)(2,1)S(1)} collective-permute-done((bf16[2,2,2,64,512]{4,3,2,1,0:T(8,128)(2,1)S(1)}, bf16[2,2,2,64,512]{4,3,2,1,0:T(8,128)(2,1)S(1)}, u32[]{:S(2)}, u32[]{:S(2)}) %collective-permute-start.8) | collective-permute-done | bytes 524320 | tf_op jit(solution)/shard_map/ppermute | solution.py:374
  51.4 8.1 %collective-permute-start.7 = (bf16[2,2,64,512]{3,2,1,0:T(8,128)(2,1)S(1)}, bf16[2,2,64,512]{3,2,1,0:T(8,128)(2,1)S(1)}, u32[]{:S(2)}, u32[]{:S(2)}) collective-permute-start(bf16[2,2,64,512]{3,2,1,0:T(8,128)(2,1)S(1)} %get-tuple-element.28), channel_id=1, source_target_pairs={{0,0},{1,2},{2,1},{3,3},{4,8},{5,10},{6,9},{7,11},{8,4},{9,6},{10,... | collective-permute-start | bytes 786440 | tf_op jit(solution)/shard_map/ppermute | solution.py:393
  59.6 1.5 %collective-permute-start.4 = (bf16[2,2,64,512]{3,2,1,0:T(8,128)(2,1)S(1)}, bf16[2,2,64,512]{3,2,1,0:T(8,128)(2,1)S(1)}, u32[]{:S(2)}, u32[]{:S(2)}) collective-permute-start(bf16[2,2,64,512]{3,2,1,0:T(8,128)(2,1)S(1)} %get-tuple-element.25), channel_id=1, source_target_pairs={{0,6},{1,4},{2,7},{3,5},{4,14},{5,12},{6,15},{7,13},{8,2},{9,0},{1... | collective-permute-start | bytes 786440 | tf_op jit(solution)/shard_map/ppermute | solution.py:393
  61.1 4.0 %collective-permute-done.7.refs_8_.refs_3_ = bf16[2,2,64,512]{3,2,1,0:T(8,128)(2,1)S(1)} collective-permute-done((bf16[2,2,64,512]{3,2,1,0:T(8,128)(2,1)S(1)}, bf16[2,2,64,512]{3,2,1,0:T(8,128)(2,1)S(1)}, u32[]{:S(2)}, u32[]{:S(2)}) %collective-permute-start.7) | collective-permute-done | bytes 262176 | tf_op jit(solution)/shard_map/ppermute | solution.py:393
  65.1 2.4 %shard_map.49 = (bf16[2,2,64,512]{3,2,1,0:T(8,128)(2,1)S(1)}, bf16[2,2,64,512]{3,2,1,0:T(8,128)(2,1)S(1)}, bf16[2,2,64,512]{3,2,1,0:T(8,128)(2,1)S(1)}, bf16[2,2,64,512]{3,2,1,0:T(8,128)(2,1)S(1)}) custom-call(bf16[2,2,2,64,512]{4,3,2,1,0:T(8,128)(2,1)S(1)} %get-tuple-element.29.refs_0_, bf16[2,2,2,64,512]{4,3,2,1,0:T(8,128)(2,1)S(1)} %collective-permute-done.8.refs_1_, ...), custom_call_target="tpu_custom_call" | custom-call | flops 1073741824 | bytes 3145728 | tf_op jit(solution)/shard_map/pallas_call | solution.py:43
  67.7 2.0 %collective-permute-start.13 = (bf16[2,2,64,512]{3,2,1,0:T(8,128)(2,1)S(1)}, bf16[2,2,64,512]{3,2,1,0:T(8,128)(2,1)S(1)}, u32[]{:S(2)}, u32[]{:S(2)}) collective-permute-start(bf16[2,2,64,512]{3,2,1,0:T(8,128)(2,1)S(1)} %get-tuple-element.34), channel_id=1, source_target_pairs={{0,4},{1,6},{2,5},{3,7},{4,12},{5,14},{6,13},{7,15},{8,0},{9,2},{1... | collective-permute-start | bytes 786440 | tf_op jit(solution)/shard_map/ppermute | solution.py:393
  69.6 4.4 %collective-permute-start.14 = (bf16[2,2,64,512]{3,2,1,0:T(8,128)(2,1)S(1)}, bf16[2,2,64,512]{3,2,1,0:T(8,128)(2,1)S(1)}, u32[]{:S(2)}, u32[]{:S(2)}) collective-permute-start(bf16[2,2,64,512]{3,2,1,0:T(8,128)(2,1)S(1)} %get-tuple-element.35), channel_id=1, source_target_pairs={{0,2},{1,0},{2,3},{3,1},{4,10},{5,8},{6,11},{7,9},{8,6},{9,4},{10,... | collective-permute-start | bytes 786440 | tf_op jit(solution)/shard_map/ppermute | solution.py:393
  74.0 2.4 %collective-permute-start.15 = (bf16[2,2,64,512]{3,2,1,0:T(8,128)(2,1)S(1)}, bf16[2,2,64,512]{3,2,1,0:T(8,128)(2,1)S(1)}, u32[]{:S(2)}, u32[]{:S(2)}) collective-permute-start(bf16[2,2,64,512]{3,2,1,0:T(8,128)(2,1)S(1)} %get-tuple-element.36), channel_id=1, source_target_pairs={{0,0},{1,2},{2,1},{3,3},{4,8},{5,10},{6,9},{7,11},{8,4},{9,6},{10,... | collective-permute-start | bytes 786440 | tf_op jit(solution)/shard_map/ppermute | solution.py:393
  76.6 5.2 %collective-permute-done.13.refs_5_ = bf16[2,2,64,512]{3,2,1,0:T(8,128)(2,1)S(1)} collective-permute-done((bf16[2,2,64,512]{3,2,1,0:T(8,128)(2,1)S(1)}, bf16[2,2,64,512]{3,2,1,0:T(8,128)(2,1)S(1)}, u32[]{:S(2)}, u32[]{:S(2)}) %collective-permute-start.13) | collective-permute-done | bytes 262176 | tf_op jit(solution)/shard_map/ppermute | solution.py:393
  81.8 5.6 %collective-permute-done.14.refs_6_ = bf16[2,2,64,512]{3,2,1,0:T(8,128)(2,1)S(1)} collective-permute-done((bf16[2,2,64,512]{3,2,1,0:T(8,128)(2,1)S(1)}, bf16[2,2,64,512]{3,2,1,0:T(8,128)(2,1)S(1)}, u32[]{:S(2)}, u32[]{:S(2)}) %collective-permute-start.14) | collective-permute-done | bytes 262176 | tf_op jit(solution)/shard_map/ppermute | solution.py:393
  87.5 5.6 %collective-permute-done.15.refs_7_ = bf16[2,2,64,512]{3,2,1,0:T(8,128)(2,1)S(1)} collective-permute-done((bf16[2,2,64,512]{3,2,1,0:T(8,128)(2,1)S(1)}, bf16[2,2,64,512]{3,2,1,0:T(8,128)(2,1)S(1)}, u32[]{:S(2)}, u32[]{:S(2)}) %collective-permute-start.15) | collective-permute-done | bytes 262176 | tf_op jit(solution)/shard_map/ppermute | solution.py:393
  93.1 1.6 %shard_map.50 = bf16[2,256,512]{2,1,0:T(8,128)(2,1)S(1)} custom-call(s32[7]{0:T(128)S(1)} %copy-done.2, bf16[2,2,64,512]{3,2,1,0:T(8,128)(2,1)S(1)} %collective-permute-done.4.refs_0_, bf16[2,2,64,512]{3,2,1,0:T(8,128)(2,1)S(1)} %collective-permute-done.5.refs_6_.refs_1_, bf16[2,2,64,512]{3,2,1,0:T(8,128)(2,1)S(1)} %collective-permute-done.6.refs_7_.refs_2_, ...), custom_call_target="tpu_custom_call" | custom-call | flops 536870912 | bytes 2621440 | tf_op jit(solution)/shard_map/pallas_call | solution.py:43
  94.6 2.6 %collective-permute-start.16 = (bf16[2,256,512]{2,1,0:T(8,128)(2,1)S(1)}, bf16[2,256,512]{2,1,0:T(8,128)(2,1)S(1)}, u32[]{:S(2)}, u32[]{:S(2)}) collective-permute-start(bf16[2,256,512]{2,1,0:T(8,128)(2,1)S(1)} %shard_map.50), channel_id=1, source_target_pairs={{0,1},{1,0},{2,3},{3,2},{4,5},{5,4},{6,7},{7,6},{8,9},{9,8},{10,11... | collective-permute-start | bytes 1572872 | tf_op jit(solution)/shard_map/ppermute | solution.py:398
  97.2 3.3 %shard_map.51._ = f32[2,2,256,512]{3,2,1,0:T(8,128)} custom-call(s32[7]{0:T(128)S(1)} %copy-done.2, s32[2]{0:T(128)S(1)} %copy-done.3, bf16[2,2,512,512]{3,2,1,0:T(8,128)(2,1)S(1)} %copy-done.1, bf16[2,2,64,512]{3,2,1,0:T(8,128)(2,1)S(1)} %collective-permute-done.4.refs_0_, bf16[2,2,64,512]{3,2,1,0:T(8,128)(2,1)S(1)} %collective-permute-done.5.refs_6_.refs_1_, ...), custom_call_target="tpu_custom_call" | custom-call | flops 1073741824 | bytes 4194304 | tf_op jit(solution)/shard_map/pallas_call | solution.py:43
  100.5 2.4 %shard_map.52 = f32[2,2,256,512]{3,2,1,0:T(8,128)} custom-call(s32[2]{0:T(128)S(1)} %copy-done.3, bf16[2,2,512,512]{3,2,1,0:T(8,128)(2,1)S(1)} %copy-done.1, bf16[2,256,512]{2,1,0:T(8,128)(2,1)S(1)} %collective-permute-done.16.top, f32[2,2,256,512]{3,2,1,0:T(8,128)} %shard_map.51._), custom_call_target="tpu_custom_call", output_to_operand_aliasing={{}: (3, {})} | custom-call | flops 536870912 | bytes 4194304 | tf_op jit(solution)/shard_map/pallas_call | solution.py:43
  (27 shorter events, 4.4 us)
Async XLA Ops:
  0.0 6.0 %copy-start.2 = (s32[7]{0:T(128)S(1)}, s32[7]{0:T(128)}, u32[]{:S(2)}) copy-start(s32[7]{0:T(128)} %order.7) | copy-start | bytes 88
  4.5 13.8 %collective-permute-start.1 = (bf16[2,2,2,64,512]{4,3,2,1,0:T(8,128)(2,1)}, bf16[2,2,2,64,512]{4,3,2,1,0:T(8,128)(2,1)S(1)}, u32[]{:S(2)}, u32[]{:S(2)}) collective-permute-start(bf16[2,2,2,64,512]{4,3,2,1,0:T(8,128)(2,1)} %get-tuple-element.24), channel_id=1, source_target_pairs={{0,2},{2,0},{4,6},{6,4},{8,10},{10,8},{12,14},{14,12},{1,3},{3,1},... | collective-permute-start | bytes 1572872 | tf_op jit(solution)/shard_map/ppermute | solution.py:372
  5.8 14.0 %collective-permute-start.2 = (bf16[2,2,2,64,512]{4,3,2,1,0:T(8,128)(2,1)}, bf16[2,2,2,64,512]{4,3,2,1,0:T(8,128)(2,1)S(1)}, u32[]{:S(2)}, u32[]{:S(2)}) collective-permute-start(bf16[2,2,2,64,512]{4,3,2,1,0:T(8,128)(2,1)} %get-tuple-element.23.refs_2_), channel_id=1, source_target_pairs={{0,4},{2,6},{4,0},{6,2},{8,12},{10,14},{12,8},{14,10},{1,5},{3,7},... | collective-permute-start | bytes 1572872 | tf_op jit(solution)/shard_map/ppermute | solution.py:373
  6.0 3.4 %copy-start = (bf16[4,2,2,512,512]{4,3,2,1,0:T(8,128)(2,1)S(1)}, bf16[4,2,2,512,512]{4,3,2,1,0:T(8,128)(2,1)}, u32[]{:S(2)}) copy-start(bf16[4,2,2,512,512]{4,3,2,1,0:T(8,128)(2,1)} %leaf.3) | copy-start | bytes 25165828
  9.3 30.9 %copy-start.4 = (bf16[2,2,2,64,512]{4,3,2,1,0:T(8,128)(2,1)S(1)}, bf16[2,2,2,64,512]{4,3,2,1,0:T(8,128)(2,1)}, u32[]{:S(2)}) copy-start(bf16[2,2,2,64,512]{4,3,2,1,0:T(8,128)(2,1)} %get-tuple-element.23.refs_2_) | copy-start | bytes 1572868
  16.7 12.2 %collective-permute-start.9 = (bf16[2,2,2,64,512]{4,3,2,1,0:T(8,128)(2,1)S(1)}, bf16[2,2,2,64,512]{4,3,2,1,0:T(8,128)(2,1)S(1)}, u32[]{:S(2)}, u32[]{:S(2)}) collective-permute-start(bf16[2,2,2,64,512]{4,3,2,1,0:T(8,128)(2,1)S(1)} %get-tuple-element.32), channel_id=1, source_target_pairs={{0,2},{2,0},{4,6},{6,4},{8,10},{10,8},{12,14},{14,12},{1,3},{3,1},... | collective-permute-start | bytes 1572872 | tf_op jit(solution)/shard_map/ppermute | solution.py:372
  16.9 23.3 %collective-permute-start = (bf16[2,2,2,64,512]{4,3,2,1,0:T(8,128)(2,1)S(1)}, bf16[2,2,2,64,512]{4,3,2,1,0:T(8,128)(2,1)S(1)}, u32[]{:S(2)}, u32[]{:S(2)}) collective-permute-start(bf16[2,2,2,64,512]{4,3,2,1,0:T(8,128)(2,1)S(1)} %get-tuple-element.22), channel_id=1, source_target_pairs={{0,2},{2,0},{4,6},{6,4},{8,10},{10,8},{12,14},{14,12},{1,3},{3,1},... | collective-permute-start | bytes 1572872 | tf_op jit(solution)/shard_map/ppermute | solution.py:374
  18.3 21.9 %collective-permute-start.3 = (bf16[2,2,2,64,512]{4,3,2,1,0:T(8,128)(2,1)S(1)}, bf16[2,2,2,64,512]{4,3,2,1,0:T(8,128)(2,1)S(1)}, u32[]{:S(2)}, u32[]{:S(2)}) collective-permute-start(bf16[2,2,2,64,512]{4,3,2,1,0:T(8,128)(2,1)S(1)} %collective-permute-done.1.refs_3_), channel_id=1, source_target_pairs={{0,4},{2,6},{4,0},{6,2},{8,12},{10,14},{12,8},{14,10},{1,5},{3,7},... | collective-permute-start | bytes 1572872 | tf_op jit(solution)/shard_map/ppermute | solution.py:375
  19.6 31.9 %collective-permute-start.8 = (bf16[2,2,2,64,512]{4,3,2,1,0:T(8,128)(2,1)S(1)}, bf16[2,2,2,64,512]{4,3,2,1,0:T(8,128)(2,1)S(1)}, u32[]{:S(2)}, u32[]{:S(2)}) collective-permute-start(bf16[2,2,2,64,512]{4,3,2,1,0:T(8,128)(2,1)S(1)} %get-tuple-element.30), channel_id=1, source_target_pairs={{0,2},{2,0},{4,6},{6,4},{8,10},{10,8},{12,14},{14,12},{1,3},{3,1},... | collective-permute-start | bytes 1572872 | tf_op jit(solution)/shard_map/ppermute | solution.py:374
  19.8 39.8 %collective-permute-start.10 = (bf16[2,2,2,64,512]{4,3,2,1,0:T(8,128)(2,1)S(1)}, bf16[2,2,2,64,512]{4,3,2,1,0:T(8,128)(2,1)S(1)}, u32[]{:S(2)}, u32[]{:S(2)}) collective-permute-start(bf16[2,2,2,64,512]{4,3,2,1,0:T(8,128)(2,1)S(1)} %get-tuple-element.31.refs_2_), channel_id=1, source_target_pairs={{0,4},{2,6},{4,0},{6,2},{8,12},{10,14},{12,8},{14,10},{1,5},{3,7},... | collective-permute-start | bytes 1572872 | tf_op jit(solution)/shard_map/ppermute | solution.py:373
  29.0 32.1 %collective-permute-start.11 = (bf16[2,2,2,64,512]{4,3,2,1,0:T(8,128)(2,1)S(1)}, bf16[2,2,2,64,512]{4,3,2,1,0:T(8,128)(2,1)S(1)}, u32[]{:S(2)}, u32[]{:S(2)}) collective-permute-start(bf16[2,2,2,64,512]{4,3,2,1,0:T(8,128)(2,1)S(1)} %collective-permute-done.9.refs_3_), channel_id=1, source_target_pairs={{0,4},{2,6},{4,0},{6,2},{8,12},{10,14},{12,8},{14,10},{1,5},{3,7},... | collective-permute-start | bytes 1572872 | tf_op jit(solution)/shard_map/ppermute | solution.py:375
  42.7 18.5 %collective-permute-start.5 = (bf16[2,2,64,512]{3,2,1,0:T(8,128)(2,1)S(1)}, bf16[2,2,64,512]{3,2,1,0:T(8,128)(2,1)S(1)}, u32[]{:S(2)}, u32[]{:S(2)}) collective-permute-start(bf16[2,2,64,512]{3,2,1,0:T(8,128)(2,1)S(1)} %get-tuple-element.26), channel_id=1, source_target_pairs={{0,4},{1,6},{2,5},{3,7},{4,12},{5,14},{6,13},{7,15},{8,0},{9,2},{1... | collective-permute-start | bytes 786440 | tf_op jit(solution)/shard_map/ppermute | solution.py:393
  48.8 12.4 %collective-permute-start.6 = (bf16[2,2,64,512]{3,2,1,0:T(8,128)(2,1)S(1)}, bf16[2,2,64,512]{3,2,1,0:T(8,128)(2,1)S(1)}, u32[]{:S(2)}, u32[]{:S(2)}) collective-permute-start(bf16[2,2,64,512]{3,2,1,0:T(8,128)(2,1)S(1)} %get-tuple-element.27), channel_id=1, source_target_pairs={{0,2},{1,0},{2,3},{3,1},{4,10},{5,8},{6,11},{7,9},{8,6},{9,4},{10,... | collective-permute-start | bytes 786440 | tf_op jit(solution)/shard_map/ppermute | solution.py:393
  51.4 13.7 %collective-permute-start.7 = (bf16[2,2,64,512]{3,2,1,0:T(8,128)(2,1)S(1)}, bf16[2,2,64,512]{3,2,1,0:T(8,128)(2,1)S(1)}, u32[]{:S(2)}, u32[]{:S(2)}) collective-permute-start(bf16[2,2,64,512]{3,2,1,0:T(8,128)(2,1)S(1)} %get-tuple-element.28), channel_id=1, source_target_pairs={{0,0},{1,2},{2,1},{3,3},{4,8},{5,10},{6,9},{7,11},{8,4},{9,6},{10,... | collective-permute-start | bytes 786440 | tf_op jit(solution)/shard_map/ppermute | solution.py:393
  59.6 16.8 %collective-permute-start.4 = (bf16[2,2,64,512]{3,2,1,0:T(8,128)(2,1)S(1)}, bf16[2,2,64,512]{3,2,1,0:T(8,128)(2,1)S(1)}, u32[]{:S(2)}, u32[]{:S(2)}) collective-permute-start(bf16[2,2,64,512]{3,2,1,0:T(8,128)(2,1)S(1)} %get-tuple-element.25), channel_id=1, source_target_pairs={{0,6},{1,4},{2,7},{3,5},{4,14},{5,12},{6,15},{7,13},{8,2},{9,0},{1... | collective-permute-start | bytes 786440 | tf_op jit(solution)/shard_map/ppermute | solution.py:393
  67.6 29.6 %copy-start.1 = (bf16[2,2,512,512]{3,2,1,0:T(8,128)(2,1)S(1)}, bf16[2,2,512,512]{3,2,1,0:T(8,128)(2,1)}, u32[]{:S(2)}) copy-start(bf16[2,2,512,512]{3,2,1,0:T(8,128)(2,1)} %bound.3) | copy-start | bytes 6291460
  67.6 29.6 %copy-start.3 = (s32[2]{0:T(128)S(1)}, s32[2]{0:T(128)}, u32[]{:S(2)}) copy-start(s32[2]{0:T(128)} %values.3) | copy-start | bytes 28
  67.6 9.0 %collective-permute-start.12 = (bf16[2,2,64,512]{3,2,1,0:T(8,128)(2,1)S(1)}, bf16[2,2,64,512]{3,2,1,0:T(8,128)(2,1)S(1)}, u32[]{:S(2)}, u32[]{:S(2)}) collective-permute-start(bf16[2,2,64,512]{3,2,1,0:T(8,128)(2,1)S(1)} %get-tuple-element.33), channel_id=1, source_target_pairs={{0,6},{1,4},{2,7},{3,5},{4,14},{5,12},{6,15},{7,13},{8,2},{9,0},{1... | collective-permute-start | bytes 786440 | tf_op jit(solution)/shard_map/ppermute | solution.py:393
  67.7 14.2 %collective-permute-start.13 = (bf16[2,2,64,512]{3,2,1,0:T(8,128)(2,1)S(1)}, bf16[2,2,64,512]{3,2,1,0:T(8,128)(2,1)S(1)}, u32[]{:S(2)}, u32[]{:S(2)}) collective-permute-start(bf16[2,2,64,512]{3,2,1,0:T(8,128)(2,1)S(1)} %get-tuple-element.34), channel_id=1, source_target_pairs={{0,4},{1,6},{2,5},{3,7},{4,12},{5,14},{6,13},{7,15},{8,0},{9,2},{1... | collective-permute-start | bytes 786440 | tf_op jit(solution)/shard_map/ppermute | solution.py:393
  69.6 17.8 %collective-permute-start.14 = (bf16[2,2,64,512]{3,2,1,0:T(8,128)(2,1)S(1)}, bf16[2,2,64,512]{3,2,1,0:T(8,128)(2,1)S(1)}, u32[]{:S(2)}, u32[]{:S(2)}) collective-permute-start(bf16[2,2,64,512]{3,2,1,0:T(8,128)(2,1)S(1)} %get-tuple-element.35), channel_id=1, source_target_pairs={{0,2},{1,0},{2,3},{3,1},{4,10},{5,8},{6,11},{7,9},{8,6},{9,4},{10,... | collective-permute-start | bytes 786440 | tf_op jit(solution)/shard_map/ppermute | solution.py:393
  74.0 19.1 %collective-permute-start.15 = (bf16[2,2,64,512]{3,2,1,0:T(8,128)(2,1)S(1)}, bf16[2,2,64,512]{3,2,1,0:T(8,128)(2,1)S(1)}, u32[]{:S(2)}, u32[]{:S(2)}) collective-permute-start(bf16[2,2,64,512]{3,2,1,0:T(8,128)(2,1)S(1)} %get-tuple-element.36), channel_id=1, source_target_pairs={{0,0},{1,2},{2,1},{3,3},{4,8},{5,10},{6,9},{7,11},{8,4},{9,6},{10,... | collective-permute-start | bytes 786440 | tf_op jit(solution)/shard_map/ppermute | solution.py:393
  94.6 5.9 %collective-permute-start.16 = (bf16[2,256,512]{2,1,0:T(8,128)(2,1)S(1)}, bf16[2,256,512]{2,1,0:T(8,128)(2,1)S(1)}, u32[]{:S(2)}, u32[]{:S(2)}) collective-permute-start(bf16[2,256,512]{2,1,0:T(8,128)(2,1)S(1)} %shard_map.50), channel_id=1, source_target_pairs={{0,1},{1,0},{2,3},{3,2},{4,5},{5,4},{6,7},{7,6},{8,9},{9,8},{10,11... | collective-permute-start | bytes 1572872 | tf_op jit(solution)/shard_map/ppermute | solution.py:398

commit v5 on v4

--- a/solution.py
+++ b/solution.py
@@ -9,6 +9,7 @@
 
 ANY = pl.BlockSpec(memory_space=pl.ANY)
 SMEM = pl.BlockSpec(memory_space=pltpu.SMEM)
+VMEM = pl.BlockSpec(memory_space=pltpu.VMEM)
 VMEM_LIMIT = 40 * 2**20
 VMEM_MOST = 60 * 2**20
 
@@ -111,16 +112,15 @@
                 )
                 for part in range(2):
                     result[item, part] = (
-                        sums[part].astype(jnp.bfloat16).reshape(ways, total, width)
+                        sums[part].astype(jnp.bfloat16).reshape(ways, total // rows, rows, width)
                     )
                 for side in range(ways):
                     done = 0
                     for chunk, blocks in enumerate(parts):
-                        for block in range(blocks):
-                            source = result.at[item, :, side, pl.ds(done, rows)]
-                            place = outs[2 * (given + chunk) + side].at[:, block, item]
-                            stores.append(copies.start(source, place))
-                            done += rows
+                        source = result.at[item, :, side, pl.ds(done, blocks)]
+                        place = outs[2 * (given + chunk) + side].at[:, :, item]
+                        stores.append(copies.start(source, place))
+                        done += blocks
             given += len(parts)
         for copy in stores:
             copy.wait()
@@ -135,9 +135,9 @@
         scratch += [
             pltpu.VMEM((batch, 2, ways, total, width), jnp.bfloat16),
             pltpu.VMEM((batch, 2, width, width), jnp.bfloat16),
-            pltpu.VMEM((batch, 2, ways, total, width), jnp.bfloat16),
+            pltpu.VMEM((batch, 2, ways, total // rows, rows, width), jnp.bfloat16),
         ]
-    copies = len(jobs) * batch * (1 + ways) + batch * ways * sum(chunks)
+    copies = len(jobs) * batch * (1 + ways) + batch * ways * len(chunks)
     flops = 8 * batch * ways * sum(totals) * width**2
     results = run_kernel(
         body, outs, scratch, copies, flops, [join_order, leaves], [SMEM, ANY], limit=limit
@@ -156,20 +156,23 @@
         copies = Copies(sems)
         branch = lax.axis_index("branch")
         high, place, way = plan.here()
-        loads = [
-            copies.start(left_kept, left.at[:, :, way]),
-            copies.start(left_sent, left.at[:, :, 1 - way]),
-            copies.start(right_kept, right.at[:, :, place, way]),
-            copies.start(right_sent, right.at[:, :, place, 1 - way]),
-        ]
-        for step, (kept, sent) in enumerate(others):
-            other = place ^ (step + 1)
-            loads.append(copies.start(kept, right.at[:, :, other, way]))
-            loads.append(copies.start(sent, right.at[:, :, other, 1 - way]))
-        for copy in loads:
-            copy.wait()
+        loads = []
+        for block in range(blocks):
+            mine = [
+                copies.start(right_kept.at[:, block], right.at[:, block, place, way]),
+                copies.start(right_sent.at[:, block], right.at[:, block, place, 1 - way]),
+            ]
+            for step, (kept, sent) in enumerate(others):
+                other = place ^ (step + 1)
+                mine.append(copies.start(kept.at[:, block], right.at[:, block, other, way]))
+                mine.append(copies.start(sent.at[:, block], right.at[:, block, other, 1 - way]))
+            mine.append(copies.start(left_kept.at[:, block], left.at[:, block, way]))
+            mine.append(copies.start(left_sent.at[:, block], left.at[:, block, 1 - way]))
+            loads.append(mine)
         stores = []
         for block in range(blocks):
+            for copy in loads[block]:
+                copy.wait()
             halves = [
                 jnp.concatenate([left[part, block, high ^ a, branch ^ b] for a, b in plan.steps], axis=0)
                 for part in range(2)
@@ -196,7 +199,7 @@
         pltpu.VMEM((2, blocks, places, ways, batch, rows, width), jnp.bfloat16),
         pltpu.VMEM((blocks, 2, ways * batch, rows, width), jnp.bfloat16),
     ]
-    copies = 4 + 2 * (places - 1) + blocks * ways * batch
+    copies = blocks * (2 + 2 * places + ways * batch)
     flops = 8 * blocks * held * width * width
     return run_kernel(body, outs, scratch, copies, flops, operands, [ANY] * len(operands))
 
@@ -231,7 +234,7 @@
     return pltpu.VMEM((2, 2, plan.size, plan.batch, plan.rows, plan.width), jnp.bfloat16)
 
 
-def top_for_other(plan, join_order, messages):
+def top_half(plan, join_order, messages, own):
     flat = [message for chunk in messages for message in chunk]
     count = len(messages[0])
     chunk_blocks = [chunk[0].shape[1] for chunk in messages]
@@ -240,97 +243,52 @@
     def body(order, *refs):
         sources, (out, operands, result, sems) = refs[: len(flat)], refs[len(flat) :]
         copies = Copies(sems)
+        core = lax.axis_index("branch")
         grouped = [sources[i : i + count] for i in range(0, len(flat), count)]
         for copy in load_operands(plan, copies, order, grouped, chunk_blocks, operands):
             copy.wait()
-        parts = complex_dot(*top_operands(plan, operands, 1 - lax.axis_index("branch")))
+        parts = complex_dot(*top_operands(plan, operands, core if own else 1 - core))
         for part in range(2):
             result[part] = parts[part].astype(jnp.bfloat16)
         copies.start(result, out).wait()
 
-    flops = 4 * plan.width**3
     return run_kernel(
         body,
         [jax.ShapeDtypeStruct(half_shape, jnp.bfloat16)],
         [top_scratch(plan), pltpu.VMEM(half_shape, jnp.bfloat16)],
         len(flat) + 1,
-        flops,
+        4 * plan.width**3,
         [join_order, *flat],
         [SMEM] + [ANY] * len(flat),
     )[0]
 
 
-def own_amplitudes(plan, join_order, slice_values, boundary, messages):
-    flat = [message for chunk in messages for message in chunk]
-    count = len(messages[0])
-    chunk_blocks = [chunk[0].shape[1] for chunk in messages]
+def boundary_products(plan, slice_values, boundary, top_own, top_received):
     width = plan.width
-
-    def body(order, values, bound, *refs):
-        sources, (out, operands, chosen, result, sems) = refs[: len(flat)], refs[len(flat) :]
+    shape = (2, plan.batch, width // 2, width)
+
+    def body(values, bound, own, received, out, result, sems):
         copies = Copies(sems)
         core = lax.axis_index("branch")
-        grouped = [sources[i : i + count] for i in range(0, len(flat), count)]
-        loads = load_operands(plan, copies, order, grouped, chunk_blocks, operands)
-        value = jnp.where(values[core] == 1, 1, 0)
-        late = copies.start(bound.at[value], chosen)
-        for copy in loads:
+        stores = []
+        for index, (top, item) in enumerate(((own, core), (received, 1 - core))):
+            value = jnp.where(values[item] == 1, 1, 0)
+            chosen = bound[value].reshape(2 * width, width)
+            parts = complex_dot(top[0], top[1], chosen)
+            for part in range(2):
+                result[index, part] = parts[part]
+            stores.append(copies.start(result.at[index], out.at[:, item]))
+        for copy in stores:
             copy.wait()
-        top = complex_dot(*top_operands(plan, operands, core))
-        late.wait()
-        parts = complex_dot(
-            top[0].astype(jnp.bfloat16),
-            top[1].astype(jnp.bfloat16),
-            chosen[...].reshape(2 * width, width),
-        )
-        for part in range(2):
-            result[part] = parts[part]
-        copies.start(result, out.at[:, core]).wait()
-
-    flops = 8 * plan.width**3
+
     return run_kernel(
         body,
-        [jax.ShapeDtypeStruct((2, plan.batch, width // 2, width), jnp.float32)],
-        [
-            top_scratch(plan),
-            pltpu.VMEM((2, width, width), jnp.bfloat16),
-            pltpu.VMEM((2, width // 2, width), jnp.float32),
-        ],
-        len(flat) + 2,
-        flops,
-        [join_order, slice_values, boundary, *flat],
-        [SMEM, SMEM, ANY] + [ANY] * len(flat),
-    )[0]
-
-
-def other_amplitudes(plan, slice_values, boundary, top, amplitudes):
-    width = plan.width
-
-    def body(values, bound, top, _, out, left, chosen, result, sems):
-        copies = Copies(sems)
-        other = 1 - lax.axis_index("branch")
-        value = jnp.where(values[other] == 1, 1, 0)
-        loads = [copies.start(top, left), copies.start(bound.at[value], chosen)]
-        for copy in loads:
-            copy.wait()
-        parts = complex_dot(left[0], left[1], chosen[...].reshape(2 * width, width))
-        for part in range(2):
-            result[part] = parts[part]
-        copies.start(result, out.at[:, other]).wait()
-
-    return run_kernel(
-        body,
-        [jax.ShapeDtypeStruct(amplitudes.shape, jnp.float32)],
-        [
-            pltpu.VMEM((2, width // 2, width), jnp.bfloat16),
-            pltpu.VMEM((2, width, width), jnp.bfloat16),
-            pltpu.VMEM((2, width // 2, width), jnp.float32),
-        ],
-        3,
-        4 * width**3,
-        [slice_values, boundary, top, amplitudes],
-        [SMEM, ANY, ANY, ANY],
-        {3: 0},
+        [jax.ShapeDtypeStruct(shape, jnp.float32)],
+        [pltpu.VMEM((plan.batch, 2, width // 2, width), jnp.float32)],
+        plan.batch,
+        8 * width**3,
+        [slice_values, boundary, top_own, top_received],
+        [SMEM, VMEM, VMEM, VMEM],
     )[0]
 
 
@@ -357,7 +315,7 @@
         return pairs
 
     quarter = plan.size // 4
-    parts = [x * quarter for x in (2,2,)]
+    parts = [x * quarter for x in (2, 2)]
     now, later = parts[:1], parts[1:]
     jobs = [(0, 0, parts), (1, sum(now), later)]
     first = first_level(plan, leaves, join_order, [(1, 0, now)], VMEM_MOST)
@@ -380,7 +338,7 @@
             right_sent,
             *kept_there,
             *sent_there,
-            *arrived[1:],
+            *arrived[2:],
         ]
 
         def pick(refs):
@@ -394,10 +352,10 @@
             for value, (a, b) in zip(rows, plan.steps)
         ]
         messages.append(arrived)
-    top_other = top_for_other(plan, join_order, messages)
+    top_other = top_half(plan, join_order, messages, False)
     top_received = lax.ppermute(top_other, "branch", [(0, 1), (1, 0)])
-    amplitudes = own_amplitudes(plan, join_order, slice_values, boundary, messages)
-    return other_amplitudes(plan, slice_values, boundary, top_received, amplitudes)
+    top_own = top_half(plan, join_order, messages, True)
+    return boundary_products(plan, slice_values, boundary, top_own, top_received)
 
 
 def solution(mesh):

time: 103 us -> 100 us (0.971)
  starting transfers between devices: 33.9 us -> 29.1 us
  waiting for transfers between devices: 41.5 us -> 45.7 us
  Pallas kernels: 23.9 us -> 20.8 us
    ppermute x2, waiting for transfers between devices: 12.1 us -> 17 us  [per_device(): left_sent = lax.ppermute(left_sent, 'mode', over_ways)]
    pallas_call x7, Pallas kernels: 23.9 us -> 20.8 us  [run_kernel(): pl.pallas_call(body, out_shape=outs, in_specs=specs, out_specs=[ANY] * le...]
    ppermute x8, starting transfers between devices: 25.1 us -> 22.2 us  [per_device(): lax.ppermute(value, ('mode', 'branch'), to_rows(a, b))]
    ppermute x2, starting transfers between devices: 2.59 us -> 0.27 us  [per_device(): lax.ppermute(right_sent, 'mode', over_places(step))]
    ppermute x8, waiting for transfers between devices: 20.7 us -> 18.8 us  [per_device(): lax.ppermute(value, ('mode', 'branch'), to_rows(a, b))]
    ppermute x1, starting transfers between devices: 2.56 us -> 1.21 us  [per_device(): top_received = lax.ppermute(top_other, 'branch', [(0, 1), (1, 0)])]
    ppermute x2, waiting for transfers between devices: 8.72 us -> 9.84 us  [per_device(): right_sent = lax.ppermute(right_sent, 'mode', over_ways)]
  transfers between devices with their start and end apart: 17 -> 17, of which waited for: 8 -> 8; matrix products, arithmetic and copies ran while one was open for 0% -> 0% of each run, Pallas kernels for 15% -> 12%
where the time goes in v5:
time: 100 us; the launch traced here: 99.2 us
  waiting for transfers between devices  45.7 us (46%)
  starting transfers between devices  29.1 us (29%)
  Pallas kernels  20.8 us (21%)
  local copies, waits for them, and re-layouts  3.4 us (3%)
    ppermute x8, starting transfers between devices, per_device(): lax.ppermute(value, ('mode', 'branch'), to_rows(a, b))  22.2 us
    pallas_call x7, Pallas kernels, run_kernel(): pl.pallas_call(body, out_shape=outs, in_specs=specs, out_specs=[ANY] * le...  20.8 us
    ppermute x8, waiting for transfers between devices, per_device(): lax.ppermute(value, ('mode', 'branch'), to_rows(a, b))  18.8 us
    ppermute x2, waiting for transfers between devices, per_device(): left_sent = lax.ppermute(left_sent, 'mode', over_ways)  17 us
    ppermute x2, waiting for transfers between devices, per_device(): right_sent = lax.ppermute(right_sent, 'mode', over_ways)  9.84 us
    unnamed x10, local copies, waits for them, and re-layouts  3.4 us
    ppermute x2, starting transfers between devices, per_device(): left_sent = lax.ppermute(left_sent, 'mode', over_ways)  2.53 us
  transfers between devices with their start and end apart: 17, of which 8 were waited for; matrix products, arithmetic and copies ran while one was open for 0% of the time, Pallas kernels for 12%

profile of v5, /device:TPU:9, one launch (start us, length us, event | category | flops | bytes accessed | tf_op | source)
XLA Modules:
  0.0 99.2 jit_solution(12652148417702384535)
XLA Ops:
  0.0 4.4 %shard_map.47 = (bf16[2,2,2,64,512]{4,3,2,1,0:T(8,128)(2,1)}, bf16[2,2,2,64,512]{4,3,2,1,0:T(8,128)(2,1)}) custom-call(s32[7]{0:T(128)} %order.7, bf16[4,2,2,512,512]{4,3,2,1,0:T(8,128)(2,1)} %leaf.3), custom_call_target="tpu_custom_call" | custom-call | flops 1073741824 | bytes 3145728 | tf_op jit(solution)/shard_map/pallas_call | solution.py:44
  4.4 1.3 %collective-permute-start.1 = (bf16[2,2,2,64,512]{4,3,2,1,0:T(8,128)(2,1)}, bf16[2,2,2,64,512]{4,3,2,1,0:T(8,128)(2,1)S(1)}, u32[]{:S(2)}, u32[]{:S(2)}) collective-permute-start(bf16[2,2,2,64,512]{4,3,2,1,0:T(8,128)(2,1)} %get-tuple-element.24), channel_id=1, source_target_pairs={{0,2},{2,0},{4,6},{6,4},{8,10},{10,8},{12,14},{14,12},{1,3},{3,1},... | collective-permute-start | bytes 1572872 | tf_op jit(solution)/shard_map/ppermute | solution.py:330
  5.9 3.4 %copy-done = bf16[4,2,2,512,512]{4,3,2,1,0:T(8,128)(2,1)S(1)} copy-done((bf16[4,2,2,512,512]{4,3,2,1,0:T(8,128)(2,1)S(1)}, bf16[4,2,2,512,512]{4,3,2,1,0:T(8,128)(2,1)}, u32[]{:S(2)}) %copy-start) | copy-done | bytes 8388632
  9.3 5.5 %shard_map.46 = (bf16[2,2,2,64,512]{4,3,2,1,0:T(8,128)(2,1)S(1)}, bf16[2,2,2,64,512]{4,3,2,1,0:T(8,128)(2,1)S(1)}, bf16[2,2,2,64,512]{4,3,2,1,0:T(8,128)(2,1)S(1...) custom-call(s32[7]{0:T(128)S(1)} %copy-done.2, ...), custom_call_target="tpu_custom_call" | custom-call | flops 3221225472 | bytes 5242880 | tf_op jit(solution)/shard_map/pallas_call | solution.py:44
  14.9 1.4 %collective-permute-start = (bf16[2,2,2,64,512]{4,3,2,1,0:T(8,128)(2,1)S(1)}, bf16[2,2,2,64,512]{4,3,2,1,0:T(8,128)(2,1)S(1)}, u32[]{:S(2)}, u32[]{:S(2)}) collective-permute-start(bf16[2,2,2,64,512]{4,3,2,1,0:T(8,128)(2,1)S(1)} %get-tuple-element.22), channel_id=1, source_target_pairs={{0,2},{2,0},{4,6},{6,4},{8,10},{10,8},{12,14},{14,12},{1,3},{3,1},... | collective-permute-start | bytes 1572872 | tf_op jit(solution)/shard_map/ppermute | solution.py:332
  18.9 1.3 %collective-permute-start.10 = (bf16[2,2,2,64,512]{4,3,2,1,0:T(8,128)(2,1)S(1)}, bf16[2,2,2,64,512]{4,3,2,1,0:T(8,128)(2,1)S(1)}, u32[]{:S(2)}, u32[]{:S(2)}) collective-permute-start(bf16[2,2,2,64,512]{4,3,2,1,0:T(8,128)(2,1)S(1)} %get-tuple-element.31.refs_2_), channel_id=1, source_target_pairs={{0,4},{2,6},{4,0},{6,2},{8,12},{10,14},{12,8},{14,10},{1,5},{3,7},... | collective-permute-start | bytes 1572872 | tf_op jit(solution)/shard_map/ppermute | solution.py:331
  20.2 8.6 %collective-permute-done.9.refs_3_ = bf16[2,2,2,64,512]{4,3,2,1,0:T(8,128)(2,1)S(1)} collective-permute-done((bf16[2,2,2,64,512]{4,3,2,1,0:T(8,128)(2,1)S(1)}, bf16[2,2,2,64,512]{4,3,2,1,0:T(8,128)(2,1)S(1)}, u32[]{:S(2)}, u32[]{:S(2)}) %collective-permute-start.9) | collective-permute-done | bytes 524320 | tf_op jit(solution)/shard_map/ppermute | solution.py:330
  28.9 11.2 %collective-permute-done.refs_1_ = bf16[2,2,2,64,512]{4,3,2,1,0:T(8,128)(2,1)S(1)} collective-permute-done((bf16[2,2,2,64,512]{4,3,2,1,0:T(8,128)(2,1)S(1)}, bf16[2,2,2,64,512]{4,3,2,1,0:T(8,128)(2,1)S(1)}, u32[]{:S(2)}, u32[]{:S(2)}) %collective-permute-start) | collective-permute-done | bytes 524320 | tf_op jit(solution)/shard_map/ppermute | solution.py:332
  40.1 2.5 %shard_map.48 = (bf16[2,2,64,512]{3,2,1,0:T(8,128)(2,1)S(1)}, bf16[2,2,64,512]{3,2,1,0:T(8,128)(2,1)S(1)}, bf16[2,2,64,512]{3,2,1,0:T(8,128)(2,1)S(1)}, bf16[2,2,64,512]{3,2,1,0:T(8,128)(2,1)S(1)}) custom-call(bf16[2,2,2,64,512]{4,3,2,1,0:T(8,128)(2,1)S(1)} %get-tuple-element.21.refs_0_, bf16[2,2,2,64,512]{4,3,2,1,0:T(8,128)(2,1)S(1)} %collective-permute-done.refs_1_, ...), custom_call_target="tpu_custom_call" | custom-call | flops 1073741824 | bytes 3145728 | tf_op jit(solution)/shard_map/pallas_call | solution.py:44
  42.6 4.5 %collective-permute-start.6 = (bf16[2,2,64,512]{3,2,1,0:T(8,128)(2,1)S(1)}, bf16[2,2,64,512]{3,2,1,0:T(8,128)(2,1)S(1)}, u32[]{:S(2)}, u32[]{:S(2)}) collective-permute-start(bf16[2,2,64,512]{3,2,1,0:T(8,128)(2,1)S(1)} %get-tuple-element.27), channel_id=1, source_target_pairs={{0,2},{1,0},{2,3},{3,1},{4,10},{5,8},{6,11},{7,9},{8,6},{9,4},{10,... | collective-permute-start | bytes 786440 | tf_op jit(solution)/shard_map/ppermute | solution.py:351
  47.1 2.0 %collective-permute-start.7 = (bf16[2,2,64,512]{3,2,1,0:T(8,128)(2,1)S(1)}, bf16[2,2,64,512]{3,2,1,0:T(8,128)(2,1)S(1)}, u32[]{:S(2)}, u32[]{:S(2)}) collective-permute-start(bf16[2,2,64,512]{3,2,1,0:T(8,128)(2,1)S(1)} %get-tuple-element.28), channel_id=1, source_target_pairs={{0,0},{1,2},{2,1},{3,3},{4,8},{5,10},{6,9},{7,11},{8,4},{9,6},{10,... | collective-permute-start | bytes 786440 | tf_op jit(solution)/shard_map/ppermute | solution.py:351
  49.1 5.8 %collective-permute-done.8.refs_1_ = bf16[2,2,2,64,512]{4,3,2,1,0:T(8,128)(2,1)S(1)} collective-permute-done((bf16[2,2,2,64,512]{4,3,2,1,0:T(8,128)(2,1)S(1)}, bf16[2,2,2,64,512]{4,3,2,1,0:T(8,128)(2,1)S(1)}, u32[]{:S(2)}, u32[]{:S(2)}) %collective-permute-start.8) | collective-permute-done | bytes 524320 | tf_op jit(solution)/shard_map/ppermute | solution.py:332
  56.0 2.8 %collective-permute-start.5 = (bf16[2,2,64,512]{3,2,1,0:T(8,128)(2,1)S(1)}, bf16[2,2,64,512]{3,2,1,0:T(8,128)(2,1)S(1)}, u32[]{:S(2)}, u32[]{:S(2)}) collective-permute-start(bf16[2,2,64,512]{3,2,1,0:T(8,128)(2,1)S(1)} %get-tuple-element.26), channel_id=1, source_target_pairs={{0,4},{1,6},{2,5},{3,7},{4,12},{5,14},{6,13},{7,15},{8,0},{9,2},{1... | collective-permute-start | bytes 786440 | tf_op jit(solution)/shard_map/ppermute | solution.py:351
  58.8 2.5 %shard_map.49 = (bf16[2,2,64,512]{3,2,1,0:T(8,128)(2,1)S(1)}, bf16[2,2,64,512]{3,2,1,0:T(8,128)(2,1)S(1)}, bf16[2,2,64,512]{3,2,1,0:T(8,128)(2,1)S(1)}, bf16[2,2,64,512]{3,2,1,0:T(8,128)(2,1)S(1)}) custom-call(bf16[2,2,2,64,512]{4,3,2,1,0:T(8,128)(2,1)S(1)} %get-tuple-element.29.refs_0_, bf16[2,2,2,64,512]{4,3,2,1,0:T(8,128)(2,1)S(1)} %collective-permute-done.8.refs_1_, ...), custom_call_target="tpu_custom_call" | custom-call | flops 1073741824 | bytes 3145728 | tf_op jit(solution)/shard_map/pallas_call | solution.py:44
  61.4 5.1 %collective-permute-start.12 = (bf16[2,2,64,512]{3,2,1,0:T(8,128)(2,1)S(1)}, bf16[2,2,64,512]{3,2,1,0:T(8,128)(2,1)S(1)}, u32[]{:S(2)}, u32[]{:S(2)}) collective-permute-start(bf16[2,2,64,512]{3,2,1,0:T(8,128)(2,1)S(1)} %get-tuple-element.33), channel_id=1, source_target_pairs={{0,6},{1,4},{2,7},{3,5},{4,14},{5,12},{6,15},{7,13},{8,2},{9,0},{1... | collective-permute-start | bytes 786440 | tf_op jit(solution)/shard_map/ppermute | solution.py:351
  66.5 4.1 %collective-permute-start.14 = (bf16[2,2,64,512]{3,2,1,0:T(8,128)(2,1)S(1)}, bf16[2,2,64,512]{3,2,1,0:T(8,128)(2,1)S(1)}, u32[]{:S(2)}, u32[]{:S(2)}) collective-permute-start(bf16[2,2,64,512]{3,2,1,0:T(8,128)(2,1)S(1)} %get-tuple-element.35), channel_id=1, source_target_pairs={{0,2},{1,0},{2,3},{3,1},{4,10},{5,8},{6,11},{7,9},{8,6},{9,4},{10,... | collective-permute-start | bytes 786440 | tf_op jit(solution)/shard_map/ppermute | solution.py:351
  70.6 2.6 %collective-permute-start.15 = (bf16[2,2,64,512]{3,2,1,0:T(8,128)(2,1)S(1)}, bf16[2,2,64,512]{3,2,1,0:T(8,128)(2,1)S(1)}, u32[]{:S(2)}, u32[]{:S(2)}) collective-permute-start(bf16[2,2,64,512]{3,2,1,0:T(8,128)(2,1)S(1)} %get-tuple-element.36), channel_id=1, source_target_pairs={{0,0},{1,2},{2,1},{3,3},{4,8},{5,10},{6,9},{7,11},{8,4},{9,6},{10,... | collective-permute-start | bytes 786440 | tf_op jit(solution)/shard_map/ppermute | solution.py:351
  73.2 1.8 %collective-permute-done.12.refs_4_ = bf16[2,2,64,512]{3,2,1,0:T(8,128)(2,1)S(1)} collective-permute-done((bf16[2,2,64,512]{3,2,1,0:T(8,128)(2,1)S(1)}, bf16[2,2,64,512]{3,2,1,0:T(8,128)(2,1)S(1)}, u32[]{:S(2)}, u32[]{:S(2)}) %collective-permute-start.12) | collective-permute-done | bytes 262176 | tf_op jit(solution)/shard_map/ppermute | solution.py:351
  75.0 7.0 %collective-permute-done.13.refs_5_ = bf16[2,2,64,512]{3,2,1,0:T(8,128)(2,1)S(1)} collective-permute-done((bf16[2,2,64,512]{3,2,1,0:T(8,128)(2,1)S(1)}, bf16[2,2,64,512]{3,2,1,0:T(8,128)(2,1)S(1)}, u32[]{:S(2)}, u32[]{:S(2)}) %collective-permute-start.13) | collective-permute-done | bytes 262176 | tf_op jit(solution)/shard_map/ppermute | solution.py:351
  82.1 4.2 %collective-permute-done.14.refs_6_ = bf16[2,2,64,512]{3,2,1,0:T(8,128)(2,1)S(1)} collective-permute-done((bf16[2,2,64,512]{3,2,1,0:T(8,128)(2,1)S(1)}, bf16[2,2,64,512]{3,2,1,0:T(8,128)(2,1)S(1)}, u32[]{:S(2)}, u32[]{:S(2)}) %collective-permute-start.14) | collective-permute-done | bytes 262176 | tf_op jit(solution)/shard_map/ppermute | solution.py:351
  86.3 5.7 %collective-permute-done.15.refs_7_ = bf16[2,2,64,512]{3,2,1,0:T(8,128)(2,1)S(1)} collective-permute-done((bf16[2,2,64,512]{3,2,1,0:T(8,128)(2,1)S(1)}, bf16[2,2,64,512]{3,2,1,0:T(8,128)(2,1)S(1)}, u32[]{:S(2)}, u32[]{:S(2)}) %collective-permute-start.15) | collective-permute-done | bytes 262176 | tf_op jit(solution)/shard_map/ppermute | solution.py:351
  92.0 1.6 %shard_map.51 = bf16[2,256,512]{2,1,0:T(8,128)(2,1)S(1)} custom-call(s32[7]{0:T(128)S(1)} %copy-done.2, bf16[2,2,64,512]{3,2,1,0:T(8,128)(2,1)S(1)} %collective-permute-done.4.refs_0_, bf16[2,2,64,512]{3,2,1,0:T(8,128)(2,1)S(1)} %collective-permute-done.5.refs_1_, bf16[2,2,64,512]{3,2,1,0:T(8,128)(2,1)S(1)} %collective-permute-done.6.refs_6_.refs_2_, ...), custom_call_target="tpu_custom_call" | custom-call | flops 536870912 | bytes 2621440 | tf_op jit(solution)/shard_map/pallas_call | solution.py:44
  94.8 1.6 %shard_map.50.own = bf16[2,256,512]{2,1,0:T(8,128)(2,1)S(1)} custom-call(s32[7]{0:T(128)S(1)} %copy-done.2, bf16[2,2,64,512]{3,2,1,0:T(8,128)(2,1)S(1)} %collective-permute-done.4.refs_0_, bf16[2,2,64,512]{3,2,1,0:T(8,128)(2,1)S(1)} %collective-permute-done.5.refs_1_, bf16[2,2,64,512]{3,2,1,0:T(8,128)(2,1)S(1)} %collective-permute-done.6.refs_6_.refs_2_, ...), custom_call_target="tpu_custom_call" | custom-call | flops 536870912 | bytes 2621440 | tf_op jit(solution)/shard_map/pallas_call | solution.py:44
  96.4 2.8 %shard_map.52 = f32[2,2,256,512]{3,2,1,0:T(8,128)} custom-call(s32[2]{0:T(128)S(1)} %copy-done.3, bf16[2,2,512,512]{3,2,1,0:T(8,128)(2,1)S(1)} %copy-done.1, bf16[2,256,512]{2,1,0:T(8,128)(2,1)S(1)} %shard_map.50.own, bf16[2,256,512]{2,1,0:T(8,128)(2,1)S(1)} %collective-permute-done.16.received), custom_call_target="tpu_custom_call" | custom-call | flops 1073741824 | bytes 4194304 | tf_op jit(solution)/shard_map/pallas_call | solution.py:44
  (27 shorter events, 5.3 us)
Async XLA Ops:
  0.0 5.9 %copy-start.2 = (s32[7]{0:T(128)S(1)}, s32[7]{0:T(128)}, u32[]{:S(2)}) copy-start(s32[7]{0:T(128)} %order.7) | copy-start | bytes 88
  4.4 13.1 %collective-permute-start.1 = (bf16[2,2,2,64,512]{4,3,2,1,0:T(8,128)(2,1)}, bf16[2,2,2,64,512]{4,3,2,1,0:T(8,128)(2,1)S(1)}, u32[]{:S(2)}, u32[]{:S(2)}) collective-permute-start(bf16[2,2,2,64,512]{4,3,2,1,0:T(8,128)(2,1)} %get-tuple-element.24), channel_id=1, source_target_pairs={{0,2},{2,0},{4,6},{6,4},{8,10},{10,8},{12,14},{14,12},{1,3},{3,1},... | collective-permute-start | bytes 1572872 | tf_op jit(solution)/shard_map/ppermute | solution.py:330
  5.8 13.2 %collective-permute-start.2 = (bf16[2,2,2,64,512]{4,3,2,1,0:T(8,128)(2,1)}, bf16[2,2,2,64,512]{4,3,2,1,0:T(8,128)(2,1)S(1)}, u32[]{:S(2)}, u32[]{:S(2)}) collective-permute-start(bf16[2,2,2,64,512]{4,3,2,1,0:T(8,128)(2,1)} %get-tuple-element.23.refs_2_), channel_id=1, source_target_pairs={{0,4},{2,6},{4,0},{6,2},{8,12},{10,14},{12,8},{14,10},{1,5},{3,7},... | collective-permute-start | bytes 1572872 | tf_op jit(solution)/shard_map/ppermute | solution.py:331
  5.9 3.4 %copy-start = (bf16[4,2,2,512,512]{4,3,2,1,0:T(8,128)(2,1)S(1)}, bf16[4,2,2,512,512]{4,3,2,1,0:T(8,128)(2,1)}, u32[]{:S(2)}) copy-start(bf16[4,2,2,512,512]{4,3,2,1,0:T(8,128)(2,1)} %leaf.3) | copy-start | bytes 25165828
  9.3 30.8 %copy-start.4 = (bf16[2,2,2,64,512]{4,3,2,1,0:T(8,128)(2,1)S(1)}, bf16[2,2,2,64,512]{4,3,2,1,0:T(8,128)(2,1)}, u32[]{:S(2)}) copy-start(bf16[2,2,2,64,512]{4,3,2,1,0:T(8,128)(2,1)} %get-tuple-element.23.refs_2_) | copy-start | bytes 1572868
  14.8 14.1 %collective-permute-start.9 = (bf16[2,2,2,64,512]{4,3,2,1,0:T(8,128)(2,1)S(1)}, bf16[2,2,2,64,512]{4,3,2,1,0:T(8,128)(2,1)S(1)}, u32[]{:S(2)}, u32[]{:S(2)}) collective-permute-start(bf16[2,2,2,64,512]{4,3,2,1,0:T(8,128)(2,1)S(1)} %get-tuple-element.32), channel_id=1, source_target_pairs={{0,2},{2,0},{4,6},{6,4},{8,10},{10,8},{12,14},{14,12},{1,3},{3,1},... | collective-permute-start | bytes 1572872 | tf_op jit(solution)/shard_map/ppermute | solution.py:330
  14.9 25.2 %collective-permute-start = (bf16[2,2,2,64,512]{4,3,2,1,0:T(8,128)(2,1)S(1)}, bf16[2,2,2,64,512]{4,3,2,1,0:T(8,128)(2,1)S(1)}, u32[]{:S(2)}, u32[]{:S(2)}) collective-permute-start(bf16[2,2,2,64,512]{4,3,2,1,0:T(8,128)(2,1)S(1)} %get-tuple-element.22), channel_id=1, source_target_pairs={{0,2},{2,0},{4,6},{6,4},{8,10},{10,8},{12,14},{14,12},{1,3},{3,1},... | collective-permute-start | bytes 1572872 | tf_op jit(solution)/shard_map/ppermute | solution.py:332
  17.5 22.6 %collective-permute-start.3 = (bf16[2,2,2,64,512]{4,3,2,1,0:T(8,128)(2,1)S(1)}, bf16[2,2,2,64,512]{4,3,2,1,0:T(8,128)(2,1)S(1)}, u32[]{:S(2)}, u32[]{:S(2)}) collective-permute-start(bf16[2,2,2,64,512]{4,3,2,1,0:T(8,128)(2,1)S(1)} %collective-permute-done.1.refs_3_), channel_id=1, source_target_pairs={{0,4},{2,6},{4,0},{6,2},{8,12},{10,14},{12,8},{14,10},{1,5},{3,7},... | collective-permute-start | bytes 1572872 | tf_op jit(solution)/shard_map/ppermute | solution.py:333
  17.8 37.1 %collective-permute-start.8 = (bf16[2,2,2,64,512]{4,3,2,1,0:T(8,128)(2,1)S(1)}, bf16[2,2,2,64,512]{4,3,2,1,0:T(8,128)(2,1)S(1)}, u32[]{:S(2)}, u32[]{:S(2)}) collective-permute-start(bf16[2,2,2,64,512]{4,3,2,1,0:T(8,128)(2,1)S(1)} %get-tuple-element.30), channel_id=1, source_target_pairs={{0,2},{2,0},{4,6},{6,4},{8,10},{10,8},{12,14},{14,12},{1,3},{3,1},... | collective-permute-start | bytes 1572872 | tf_op jit(solution)/shard_map/ppermute | solution.py:332
  18.9 37.1 %collective-permute-start.10 = (bf16[2,2,2,64,512]{4,3,2,1,0:T(8,128)(2,1)S(1)}, bf16[2,2,2,64,512]{4,3,2,1,0:T(8,128)(2,1)S(1)}, u32[]{:S(2)}, u32[]{:S(2)}) collective-permute-start(bf16[2,2,2,64,512]{4,3,2,1,0:T(8,128)(2,1)S(1)} %get-tuple-element.31.refs_2_), channel_id=1, source_target_pairs={{0,4},{2,6},{4,0},{6,2},{8,12},{10,14},{12,8},{14,10},{1,5},{3,7},... | collective-permute-start | bytes 1572872 | tf_op jit(solution)/shard_map/ppermute | solution.py:331
  28.9 30.0 %collective-permute-start.11 = (bf16[2,2,2,64,512]{4,3,2,1,0:T(8,128)(2,1)S(1)}, bf16[2,2,2,64,512]{4,3,2,1,0:T(8,128)(2,1)S(1)}, u32[]{:S(2)}, u32[]{:S(2)}) collective-permute-start(bf16[2,2,2,64,512]{4,3,2,1,0:T(8,128)(2,1)S(1)} %collective-permute-done.9.refs_3_), channel_id=1, source_target_pairs={{0,4},{2,6},{4,0},{6,2},{8,12},{10,14},{12,8},{14,10},{1,5},{3,7},... | collective-permute-start | bytes 1572872 | tf_op jit(solution)/shard_map/ppermute | solution.py:333
  42.6 16.2 %collective-permute-start.6 = (bf16[2,2,64,512]{3,2,1,0:T(8,128)(2,1)S(1)}, bf16[2,2,64,512]{3,2,1,0:T(8,128)(2,1)S(1)}, u32[]{:S(2)}, u32[]{:S(2)}) collective-permute-start(bf16[2,2,64,512]{3,2,1,0:T(8,128)(2,1)S(1)} %get-tuple-element.27), channel_id=1, source_target_pairs={{0,2},{1,0},{2,3},{3,1},{4,10},{5,8},{6,11},{7,9},{8,6},{9,4},{10,... | collective-permute-start | bytes 786440 | tf_op jit(solution)/shard_map/ppermute | solution.py:351
  47.1 11.7 %collective-permute-start.7 = (bf16[2,2,64,512]{3,2,1,0:T(8,128)(2,1)S(1)}, bf16[2,2,64,512]{3,2,1,0:T(8,128)(2,1)S(1)}, u32[]{:S(2)}, u32[]{:S(2)}) collective-permute-start(bf16[2,2,64,512]{3,2,1,0:T(8,128)(2,1)S(1)} %get-tuple-element.28), channel_id=1, source_target_pairs={{0,0},{1,2},{2,1},{3,3},{4,8},{5,10},{6,9},{7,11},{8,4},{9,6},{10,... | collective-permute-start | bytes 786440 | tf_op jit(solution)/shard_map/ppermute | solution.py:351
  54.9 15.7 %collective-permute-start.4 = (bf16[2,2,64,512]{3,2,1,0:T(8,128)(2,1)S(1)}, bf16[2,2,64,512]{3,2,1,0:T(8,128)(2,1)S(1)}, u32[]{:S(2)}, u32[]{:S(2)}) collective-permute-start(bf16[2,2,64,512]{3,2,1,0:T(8,128)(2,1)S(1)} %get-tuple-element.25), channel_id=1, source_target_pairs={{0,6},{1,4},{2,7},{3,5},{4,14},{5,12},{6,15},{7,13},{8,2},{9,0},{1... | collective-permute-start | bytes 786440 | tf_op jit(solution)/shard_map/ppermute | solution.py:351
  56.0 17.2 %collective-permute-start.5 = (bf16[2,2,64,512]{3,2,1,0:T(8,128)(2,1)S(1)}, bf16[2,2,64,512]{3,2,1,0:T(8,128)(2,1)S(1)}, u32[]{:S(2)}, u32[]{:S(2)}) collective-permute-start(bf16[2,2,64,512]{3,2,1,0:T(8,128)(2,1)S(1)} %get-tuple-element.26), channel_id=1, source_target_pairs={{0,4},{1,6},{2,5},{3,7},{4,12},{5,14},{6,13},{7,15},{8,0},{9,2},{1... | collective-permute-start | bytes 786440 | tf_op jit(solution)/shard_map/ppermute | solution.py:351
  61.4 13.6 %collective-permute-start.12 = (bf16[2,2,64,512]{3,2,1,0:T(8,128)(2,1)S(1)}, bf16[2,2,64,512]{3,2,1,0:T(8,128)(2,1)S(1)}, u32[]{:S(2)}, u32[]{:S(2)}) collective-permute-start(bf16[2,2,64,512]{3,2,1,0:T(8,128)(2,1)S(1)} %get-tuple-element.33), channel_id=1, source_target_pairs={{0,6},{1,4},{2,7},{3,5},{4,14},{5,12},{6,15},{7,13},{8,2},{9,0},{1... | collective-permute-start | bytes 786440 | tf_op jit(solution)/shard_map/ppermute | solution.py:351
  66.5 15.6 %collective-permute-start.13 = (bf16[2,2,64,512]{3,2,1,0:T(8,128)(2,1)S(1)}, bf16[2,2,64,512]{3,2,1,0:T(8,128)(2,1)S(1)}, u32[]{:S(2)}, u32[]{:S(2)}) collective-permute-start(bf16[2,2,64,512]{3,2,1,0:T(8,128)(2,1)S(1)} %get-tuple-element.34), channel_id=1, source_target_pairs={{0,4},{1,6},{2,5},{3,7},{4,12},{5,14},{6,13},{7,15},{8,0},{9,2},{1... | collective-permute-start | bytes 786440 | tf_op jit(solution)/shard_map/ppermute | solution.py:351
  66.5 19.7 %collective-permute-start.14 = (bf16[2,2,64,512]{3,2,1,0:T(8,128)(2,1)S(1)}, bf16[2,2,64,512]{3,2,1,0:T(8,128)(2,1)S(1)}, u32[]{:S(2)}, u32[]{:S(2)}) collective-permute-start(bf16[2,2,64,512]{3,2,1,0:T(8,128)(2,1)S(1)} %get-tuple-element.35), channel_id=1, source_target_pairs={{0,2},{1,0},{2,3},{3,1},{4,10},{5,8},{6,11},{7,9},{8,6},{9,4},{10,... | collective-permute-start | bytes 786440 | tf_op jit(solution)/shard_map/ppermute | solution.py:351
  70.6 25.8 %copy-start.1 = (bf16[2,2,512,512]{3,2,1,0:T(8,128)(2,1)S(1)}, bf16[2,2,512,512]{3,2,1,0:T(8,128)(2,1)}, u32[]{:S(2)}) copy-start(bf16[2,2,512,512]{3,2,1,0:T(8,128)(2,1)} %bound.1) | copy-start | bytes 6291460
  70.6 25.8 %copy-start.3 = (s32[2]{0:T(128)S(1)}, s32[2]{0:T(128)}, u32[]{:S(2)}) copy-start(s32[2]{0:T(128)} %values.1) | copy-start | bytes 28
  70.6 21.4 %collective-permute-start.15 = (bf16[2,2,64,512]{3,2,1,0:T(8,128)(2,1)S(1)}, bf16[2,2,64,512]{3,2,1,0:T(8,128)(2,1)S(1)}, u32[]{:S(2)}, u32[]{:S(2)}) collective-permute-start(bf16[2,2,64,512]{3,2,1,0:T(8,128)(2,1)S(1)} %get-tuple-element.36), channel_id=1, source_target_pairs={{0,0},{1,2},{2,1},{3,3},{4,8},{5,10},{6,9},{7,11},{8,4},{9,6},{10,... | collective-permute-start | bytes 786440 | tf_op jit(solution)/shard_map/ppermute | solution.py:351
  93.6 2.8 %collective-permute-start.16 = (bf16[2,256,512]{2,1,0:T(8,128)(2,1)S(1)}, bf16[2,256,512]{2,1,0:T(8,128)(2,1)S(1)}, u32[]{:S(2)}, u32[]{:S(2)}) collective-permute-start(bf16[2,256,512]{2,1,0:T(8,128)(2,1)S(1)} %shard_map.51), channel_id=1, source_target_pairs={{0,1},{1,0},{2,3},{3,2},{4,5},{5,4},{6,7},{7,6},{8,9},{9,8},{10,11... | collective-permute-start | bytes 1572872 | tf_op jit(solution)/shard_map/ppermute | solution.py:356

commit v6 on v5

--- a/solution.py
+++ b/solution.py
@@ -39,15 +39,16 @@
         return copy
 
 
-def run_kernel(body, outs, scratch, copies, flops, operands, specs, aliases=None, limit=VMEM_LIMIT):
+def run_kernel(
+    body, outs, scratch, copies, flops, operands, specs, limit=VMEM_LIMIT, place=ANY
+):
     moved = sum(x.size * x.dtype.itemsize for x in outs) + 2**21
     return pl.pallas_call(
         body,
         out_shape=outs,
         in_specs=specs,
-        out_specs=[ANY] * len(outs),
+        out_specs=[place] * len(outs),
         scratch_shapes=list(scratch) + [pltpu.SemaphoreType.DMA((copies,))],
-        input_output_aliases=aliases or {},
         compiler_params=pltpu.CompilerParams(vmem_limit_bytes=limit),
         cost_estimate=pl.CostEstimate(flops=flops, bytes_accessed=moved, transcendentals=0),
     )(*operands)
@@ -145,6 +146,36 @@
     return [results[2 * index : 2 * index + 2] for index in range(len(chunks))]
 
 
+def once_there(value, after):
+    def body(*refs):
+        pass
+
+    return pl.pallas_call(
+        body,
+        out_shape=jax.ShapeDtypeStruct(value.shape, value.dtype),
+        in_specs=[ANY] * (1 + len(after)),
+        out_specs=ANY,
+        input_output_aliases={0: 0},
+        compiler_params=pltpu.CompilerParams(vmem_limit_bytes=2**20),
+    )(value, *after)
+
+
+def arrival(after, micros):
+    def body(*refs):
+        refs[-1][...] = jnp.zeros((8, 128), jnp.float32)
+
+    return pl.pallas_call(
+        body,
+        out_shape=jax.ShapeDtypeStruct((8, 128), jnp.float32),
+        in_specs=[ANY] * len(after),
+        out_specs=VMEM,
+        compiler_params=pltpu.CompilerParams(vmem_limit_bytes=2**20),
+        cost_estimate=pl.CostEstimate(
+            flops=micros * 10**9, bytes_accessed=micros * 3 * 10**6, transcendentals=0
+        ),
+    )(*after)
+
+
 def second_level(plan, blocks, operands, pick):
     width, batch, rows, ways, places = plan.width, plan.batch, plan.rows, plan.ways, plan.places
     held = ways * batch * rows
@@ -159,15 +190,15 @@
         loads = []
         for block in range(blocks):
             mine = [
-                copies.start(right_kept.at[:, block], right.at[:, block, place, way]),
-                copies.start(right_sent.at[:, block], right.at[:, block, place, 1 - way]),
+                copies.start(right_kept(block), right.at[:, block, place, way]),
+                copies.start(right_sent(block), right.at[:, block, place, 1 - way]),
             ]
             for step, (kept, sent) in enumerate(others):
                 other = place ^ (step + 1)
-                mine.append(copies.start(kept.at[:, block], right.at[:, block, other, way]))
-                mine.append(copies.start(sent.at[:, block], right.at[:, block, other, 1 - way]))
-            mine.append(copies.start(left_kept.at[:, block], left.at[:, block, way]))
-            mine.append(copies.start(left_sent.at[:, block], left.at[:, block, 1 - way]))
+                mine.append(copies.start(kept(block), right.at[:, block, other, way]))
+                mine.append(copies.start(sent(block), right.at[:, block, other, 1 - way]))
+            mine.append(copies.start(left_kept(block), left.at[:, block, way]))
+            mine.append(copies.start(left_sent(block), left.at[:, block, 1 - way]))
             loads.append(mine)
         stores = []
         for block in range(blocks):
@@ -204,20 +235,15 @@
     return run_kernel(body, outs, scratch, copies, flops, operands, [ANY] * len(operands))
 
 
-def load_operands(plan, copies, order, messages, chunk_blocks, scratch):
+def place_operands(plan, order, messages, chunk_blocks, scratch):
     mode = lax.axis_index("mode")
     near, item = (mode // plan.batch) % plan.ways, mode % plan.batch
     top = jnp.where(order[order.shape[0] - 1] == 1, 1, 0)
-    loads = []
     begin = 0
     for chunk, blocks in zip(messages, chunk_blocks):
         for (a, b), message in zip(plan.steps, chunk):
-            role = item ^ b ^ top
-            loads.append(
-                copies.start(message, scratch.at[role, :, pl.ds(begin, blocks), near ^ a])
-            )
+            scratch[item ^ b ^ top, :, pl.ds(begin, blocks), near ^ a] = message[...]
         begin += blocks
-    return loads
 
 
 def top_operands(plan, scratch, half):
@@ -241,25 +267,23 @@
     half_shape = (2, plan.width // 2, plan.width)
 
     def body(order, *refs):
-        sources, (out, operands, result, sems) = refs[: len(flat)], refs[len(flat) :]
-        copies = Copies(sems)
+        sources, (out, operands, _) = refs[: len(flat)], refs[len(flat) :]
         core = lax.axis_index("branch")
         grouped = [sources[i : i + count] for i in range(0, len(flat), count)]
-        for copy in load_operands(plan, copies, order, grouped, chunk_blocks, operands):
-            copy.wait()
+        place_operands(plan, order, grouped, chunk_blocks, operands)
         parts = complex_dot(*top_operands(plan, operands, core if own else 1 - core))
         for part in range(2):
-            result[part] = parts[part].astype(jnp.bfloat16)
-        copies.start(result, out).wait()
+            out[part] = parts[part].astype(jnp.bfloat16)
 
     return run_kernel(
         body,
         [jax.ShapeDtypeStruct(half_shape, jnp.bfloat16)],
-        [top_scratch(plan), pltpu.VMEM(half_shape, jnp.bfloat16)],
-        len(flat) + 1,
+        [top_scratch(plan)],
+        1,
         4 * plan.width**3,
         [join_order, *flat],
-        [SMEM] + [ANY] * len(flat),
+        [SMEM] + [VMEM] * len(flat),
+        place=VMEM,
     )[0]
 
 
@@ -315,43 +339,55 @@
         return pairs
 
     quarter = plan.size // 4
-    parts = [x * quarter for x in (2, 2)]
-    now, later = parts[:1], parts[1:]
-    jobs = [(0, 0, parts), (1, sum(now), later)]
-    first = first_level(plan, leaves, join_order, [(1, 0, now)], VMEM_MOST)
-    rest = first_level(plan, leaves, join_order, jobs, VMEM_LIMIT)
-    left, right = rest[: len(parts)], first + rest[len(parts) :]
+    parts = [2 * quarter, 2 * quarter]
+    pieces = [[2 * quarter], [quarter, quarter]]
+    right = first_level(plan, leaves, join_order, [(1, 0, parts[:1])], VMEM_MOST)
+    rest = first_level(plan, leaves, join_order, [(0, 0, parts), (1, parts[0], parts[1:])], VMEM_LIMIT)
+    left, right = rest[: len(parts)], right + rest[len(parts) :]
     others = range(1, places)
     messages = []
-    arrived = []
-    for chunk, blocks in enumerate(parts):
-        right_kept, right_sent = right[chunk]
-        left_kept, left_sent = left[chunk]
-        right_sent = lax.ppermute(right_sent, "mode", over_ways)
+    for chunk in range(len(parts)):
+        left_kept, left_send = left[chunk]
+        right_kept, right_send = right[chunk]
+        right_sent = lax.ppermute(right_send, "mode", over_ways)
         kept_there = [lax.ppermute(right_kept, "mode", over_places(step)) for step in others]
-        left_sent = lax.ppermute(left_sent, "mode", over_ways)
-        sent_there = [lax.ppermute(right_sent, "mode", over_places(step)) for step in others]
-        operands = [
-            left_kept,
-            left_sent,
-            right_kept,
-            right_sent,
-            *kept_there,
-            *sent_there,
-            *arrived[2:],
+        left_sent = lax.ppermute(left_send, "mode", over_ways)
+        lows = [sum(pieces[chunk][:piece]) for piece in range(len(pieces[chunk]))]
+        forward = [right_sent]
+        if chunk:
+            forward = [
+                right_sent[:, low : low + count] for low, count in zip(lows, pieces[chunk])
+            ]
+            forward[1:] = [once_there(value, [messages[-1][0]]) for value in forward[1:]]
+        sent_there = [
+            [lax.ppermute(value, "mode", over_places(step)) for step in others]
+            for value in forward
         ]
-
-        def pick(refs):
-            there = refs[4 : 2 + 2 * places]
-            pairs = list(zip(there[: places - 1], there[places - 1 :]))
-            return refs[0], refs[1], refs[2], refs[3], pairs
-
-        rows = second_level(plan, blocks, operands, pick)
-        arrived = [
-            lax.ppermute(value, ("mode", "branch"), to_rows(a, b))
-            for value, (a, b) in zip(rows, plan.steps)
-        ]
-        messages.append(arrived)
+        for piece, (low, count) in enumerate(zip(lows, pieces[chunk])):
+            extra = []
+            if chunk and piece == 0:
+                extra = [messages[-1][2], arrival([*messages[-1][:2], kept_there[0]], 5)]
+            elif piece:
+                extra = [messages[-2][3]]
+            operands = [left_kept, left_sent, right_kept, right_sent]
+            operands += [*kept_there, *sent_there[piece], *extra]
+
+            def pick(refs, low=low):
+                def by(ref, base):
+                    return lambda block: ref.at[:, base + block]
+
+                there = refs[4 : 2 + 2 * places]
+                kept, sent = there[: places - 1], there[places - 1 :]
+                pairs = [(by(one, low), by(two, 0)) for one, two in zip(kept, sent)]
+                return *[by(ref, low) for ref in refs[:4]], pairs
+
+            rows = second_level(plan, count, operands, pick)
+            messages.append(
+                [
+                    lax.ppermute(value, ("mode", "branch"), to_rows(a, b))
+                    for value, (a, b) in zip(rows, plan.steps)
+                ]
+            )
     top_other = top_half(plan, join_order, messages, False)
     top_received = lax.ppermute(top_other, "branch", [(0, 1), (1, 0)])
     top_own = top_half(plan, join_order, messages, True)

time: 100 us -> 96.2 us (0.962)
  waiting for transfers between devices: 45.7 us -> 21.7 us
  starting transfers between devices: 29.1 us -> 49.4 us
    ppermute x8 -> x12, starting transfers between devices: 22.2 us -> 43.2 us  [per_device(): lax.ppermute(value, ('mode', 'branch'), to_rows(a, b))]
    ppermute x6 -> x7, waiting for transfers between devices: 26.9 us -> 11.6 us  [the longest x2 9 us: per_device(): left_sent = lax.ppermute(left_send, 'mode', over_ways)]
    ppermute x8 -> x12, waiting for transfers between devices: 18.8 us -> 9.85 us  [per_device(): lax.ppermute(value, ('mode', 'branch'), to_rows(a, b))]
    ppermute x6 -> x7, starting transfers between devices: 4.25 us -> 4.48 us  [the longest x2 2.45 us: per_device(): right_sent = lax.ppermute(right_send, 'mode', over_ways)]
    pallas_call x7 -> x10, Pallas kernels: 20.8 us -> 20.6 us  [the longest x8 20.6 us: run_kernel(): pl.pallas_call(body, out_shape=outs, in_specs=specs, out_specs=[place] *...]
  transfers between devices with their start and end apart: 17 -> 22, of which waited for: 8 -> 7; matrix products, arithmetic and copies ran while one was open for 0% -> 0% of each run, Pallas kernels for 12% -> 13%
where the time goes in v6:
time: 96.2 us; the launch traced here: 95.3 us
  starting transfers between devices  49.4 us (51%)
  waiting for transfers between devices  21.7 us (23%)
  Pallas kernels  20.6 us (21%)
  local copies, waits for them, and re-layouts  3.43 us (4%)
    ppermute x12, starting transfers between devices, per_device(): lax.ppermute(value, ('mode', 'branch'), to_rows(a, b))  43.2 us
    pallas_call x8, Pallas kernels, run_kernel(): pl.pallas_call(body, out_shape=outs, in_specs=specs, out_specs=[place] *...  20.6 us
    ppermute x12, waiting for transfers between devices, per_device(): lax.ppermute(value, ('mode', 'branch'), to_rows(a, b))  9.85 us
    ppermute x2, waiting for transfers between devices, per_device(): left_sent = lax.ppermute(left_send, 'mode', over_ways)  9 us
    unnamed x10, local copies, waits for them, and re-layouts  3.4 us
    ppermute x2, waiting for transfers between devices, per_device(): right_sent = lax.ppermute(right_send, 'mode', over_ways)  2.6 us
    ppermute x2, starting transfers between devices, per_device(): right_sent = lax.ppermute(right_send, 'mode', over_ways)  2.45 us
  transfers between devices with their start and end apart: 22, of which 7 were waited for; matrix products, arithmetic and copies ran while one was open for 0% of the time, Pallas kernels for 13%

profile of v6, /device:TPU:9, one launch (start us, length us, event | category | flops | bytes accessed | tf_op | source)
XLA Modules:
  0.0 95.3 jit_solution(17405041598138213916)
XLA Ops:
  0.0 4.5 %shard_map.47 = (bf16[2,2,2,64,512]{4,3,2,1,0:T(8,128)(2,1)}, bf16[2,2,2,64,512]{4,3,2,1,0:T(8,128)(2,1)}) custom-call(s32[7]{0:T(128)} %order.7, bf16[4,2,2,512,512]{4,3,2,1,0:T(8,128)(2,1)} %leaf.3), custom_call_target="tpu_custom_call" | custom-call | flops 1073741824 | bytes 3145728 | tf_op jit(solution)/shard_map/pallas_call | solution.py:46
  4.5 1.3 %collective-permute-start.1 = (bf16[2,2,2,64,512]{4,3,2,1,0:T(8,128)(2,1)}, bf16[2,2,2,64,512]{4,3,2,1,0:T(8,128)(2,1)S(1)}, u32[]{:S(2)}, u32[]{:S(2)}) collective-permute-start(bf16[2,2,2,64,512]{4,3,2,1,0:T(8,128)(2,1)} %get-tuple-element.28), channel_id=1, source_target_pairs={{0,2},{2,0},{4,6},{6,4},{8,10},{10,8},{12,14},{14,12},{1,3},{3,1},... | collective-permute-start | bytes 1572872 | tf_op jit(solution)/shard_map/ppermute | solution.py:352
  6.0 3.4 %copy-done = bf16[4,2,2,512,512]{4,3,2,1,0:T(8,128)(2,1)S(1)} copy-done((bf16[4,2,2,512,512]{4,3,2,1,0:T(8,128)(2,1)S(1)}, bf16[4,2,2,512,512]{4,3,2,1,0:T(8,128)(2,1)}, u32[]{:S(2)}) %copy-start) | copy-done | bytes 8388632
  9.3 5.5 %shard_map.46 = (bf16[2,2,2,64,512]{4,3,2,1,0:T(8,128)(2,1)S(1)}, bf16[2,2,2,64,512]{4,3,2,1,0:T(8,128)(2,1)S(1)}, bf16[2,2,2,64,512]{4,3,2,1,0:T(8,128)(2,1)S(1...) custom-call(s32[7]{0:T(128)S(1)} %copy-done.2, ...), custom_call_target="tpu_custom_call" | custom-call | flops 3221225472 | bytes 5242880 | tf_op jit(solution)/shard_map/pallas_call | solution.py:46
  14.9 2.6 %collective-permute-done.1.refs_3_ = bf16[2,2,2,64,512]{4,3,2,1,0:T(8,128)(2,1)S(1)} collective-permute-done((bf16[2,2,2,64,512]{4,3,2,1,0:T(8,128)(2,1)}, bf16[2,2,2,64,512]{4,3,2,1,0:T(8,128)(2,1)S(1)}, u32[]{:S(2)}, u32[]{:S(2)}) %collective-permute-start.1) | collective-permute-done | bytes 524320 | tf_op jit(solution)/shard_map/ppermute | solution.py:352
  20.2 8.6 %collective-permute-done.refs_1_ = bf16[2,2,2,64,512]{4,3,2,1,0:T(8,128)(2,1)S(1)} collective-permute-done((bf16[2,2,2,64,512]{4,3,2,1,0:T(8,128)(2,1)S(1)}, bf16[2,2,2,64,512]{4,3,2,1,0:T(8,128)(2,1)S(1)}, u32[]{:S(2)}, u32[]{:S(2)}) %collective-permute-start) | collective-permute-done | bytes 524320 | tf_op jit(solution)/shard_map/ppermute | solution.py:354
  28.9 2.5 %shard_map.48 = (bf16[2,2,64,512]{3,2,1,0:T(8,128)(2,1)S(1)}, bf16[2,2,64,512]{3,2,1,0:T(8,128)(2,1)S(1)}, bf16[2,2,64,512]{3,2,1,0:T(8,128)(2,1)S(1)}, bf16[2,2,64,512]{3,2,1,0:T(8,128)(2,1)S(1)}) custom-call(bf16[2,2,2,64,512]{4,3,2,1,0:T(8,128)(2,1)S(1)} %get-tuple-element.25.refs_0_, bf16[2,2,2,64,512]{4,3,2,1,0:T(8,128)(2,1)S(1)} %collective-permute-done.refs_1_, ...), custom_call_target="tpu_custom_call" | custom-call | flops 1073741824 | bytes 3145728 | tf_op jit(solution)/shard_map/pallas_call | solution.py:46
  31.4 8.4 %collective-permute-start.4 = (bf16[2,2,64,512]{3,2,1,0:T(8,128)(2,1)S(1)}, bf16[2,2,64,512]{3,2,1,0:T(8,128)(2,1)S(1)}, u32[]{:S(2)}, u32[]{:S(2)}) collective-permute-start(bf16[2,2,64,512]{3,2,1,0:T(8,128)(2,1)S(1)} %get-tuple-element.29), channel_id=1, source_target_pairs={{0,6},{1,4},{2,7},{3,5},{4,14},{5,12},{6,15},{7,13},{8,2},{9,0},{1... | collective-permute-start | bytes 786440 | tf_op jit(solution)/shard_map/ppermute | solution.py:387
  40.9 1.5 %collective-permute-start.11 = (bf16[2,1,2,64,512]{4,3,2,1,0:T(8,128)(2,1)S(1)}, bf16[2,1,2,64,512]{4,3,2,1,0:T(8,128)(2,1)S(1)}, u32[]{:S(2)}, u32[]{:S(2)}) collective-permute-start(bf16[2,1,2,64,512]{4,3,2,1,0:T(8,128)(2,1)S(1)} %get-tuple-element.46), channel_id=1, source_target_pairs={{0,4},{2,6},{4,0},{6,2},{8,12},{10,14},{12,8},{14,10},{1,5},{3,7},... | collective-permute-start | bytes 786440 | tf_op jit(solution)/shard_map/ppermute | solution.py:363
  42.5 3.3 %collective-permute-done.4.refs_0_.refs_1_ = bf16[2,2,64,512]{3,2,1,0:T(8,128)(2,1)S(1)} collective-permute-done((bf16[2,2,64,512]{3,2,1,0:T(8,128)(2,1)S(1)}, bf16[2,2,64,512]{3,2,1,0:T(8,128)(2,1)S(1)}, u32[]{:S(2)}, u32[]{:S(2)}) %collective-permute-start.4) | collective-permute-done | bytes 262176 | tf_op jit(solution)/shard_map/ppermute | solution.py:387
  45.8 5.3 %collective-permute-start.6 = (bf16[2,2,64,512]{3,2,1,0:T(8,128)(2,1)S(1)}, bf16[2,2,64,512]{3,2,1,0:T(8,128)(2,1)S(1)}, u32[]{:S(2)}, u32[]{:S(2)}) collective-permute-start(bf16[2,2,64,512]{3,2,1,0:T(8,128)(2,1)S(1)} %get-tuple-element.31), channel_id=1, source_target_pairs={{0,2},{1,0},{2,3},{3,1},{4,10},{5,8},{6,11},{7,9},{8,6},{9,4},{10,... | collective-permute-start | bytes 786440 | tf_op jit(solution)/shard_map/ppermute | solution.py:387
  51.1 9.6 %collective-permute-start.7 = (bf16[2,2,64,512]{3,2,1,0:T(8,128)(2,1)S(1)}, bf16[2,2,64,512]{3,2,1,0:T(8,128)(2,1)S(1)}, u32[]{:S(2)}, u32[]{:S(2)}) collective-permute-start(bf16[2,2,64,512]{3,2,1,0:T(8,128)(2,1)S(1)} %get-tuple-element.32), channel_id=1, source_target_pairs={{0,0},{1,2},{2,1},{3,3},{4,8},{5,10},{6,9},{7,11},{8,4},{9,6},{10,... | collective-permute-start | bytes 786440 | tf_op jit(solution)/shard_map/ppermute | solution.py:387
  62.4 1.3 %collective-permute-start.12 = (bf16[2,1,64,512]{3,2,1,0:T(8,128)(2,1)S(1)}, bf16[2,1,64,512]{3,2,1,0:T(8,128)(2,1)S(1)}, u32[]{:S(2)}, u32[]{:S(2)}) collective-permute-start(bf16[2,1,64,512]{3,2,1,0:T(8,128)(2,1)S(1)} %get-tuple-element.37), channel_id=1, source_target_pairs={{0,6},{1,4},{2,7},{3,5},{4,14},{5,12},{6,15},{7,13},{8,2},{9,0},{1... | collective-permute-start | bytes 393224 | tf_op jit(solution)/shard_map/ppermute | solution.py:387
  63.8 3.5 %collective-permute-start.13 = (bf16[2,1,64,512]{3,2,1,0:T(8,128)(2,1)S(1)}, bf16[2,1,64,512]{3,2,1,0:T(8,128)(2,1)S(1)}, u32[]{:S(2)}, u32[]{:S(2)}) collective-permute-start(bf16[2,1,64,512]{3,2,1,0:T(8,128)(2,1)S(1)} %get-tuple-element.38), channel_id=1, source_target_pairs={{0,4},{1,6},{2,5},{3,7},{4,12},{5,14},{6,13},{7,15},{8,0},{9,2},{1... | collective-permute-start | bytes 393224 | tf_op jit(solution)/shard_map/ppermute | solution.py:387
  67.3 2.0 %collective-permute-start.14 = (bf16[2,1,64,512]{3,2,1,0:T(8,128)(2,1)S(1)}, bf16[2,1,64,512]{3,2,1,0:T(8,128)(2,1)S(1)}, u32[]{:S(2)}, u32[]{:S(2)}) collective-permute-start(bf16[2,1,64,512]{3,2,1,0:T(8,128)(2,1)S(1)} %get-tuple-element.39), channel_id=1, source_target_pairs={{0,2},{1,0},{2,3},{3,1},{4,10},{5,8},{6,11},{7,9},{8,6},{9,4},{10,... | collective-permute-start | bytes 393224 | tf_op jit(solution)/shard_map/ppermute | solution.py:387
  69.3 1.9 %collective-permute-start.15 = (bf16[2,1,64,512]{3,2,1,0:T(8,128)(2,1)S(1)}, bf16[2,1,64,512]{3,2,1,0:T(8,128)(2,1)S(1)}, u32[]{:S(2)}, u32[]{:S(2)}) collective-permute-start(bf16[2,1,64,512]{3,2,1,0:T(8,128)(2,1)S(1)} %get-tuple-element.40), channel_id=1, source_target_pairs={{0,0},{1,2},{2,1},{3,3},{4,8},{5,10},{6,9},{7,11},{8,4},{9,6},{10,... | collective-permute-start | bytes 393224 | tf_op jit(solution)/shard_map/ppermute | solution.py:387
  72.6 2.7 %collective-permute-start.18 = (bf16[2,1,64,512]{3,2,1,0:T(8,128)(2,1)S(1)}, bf16[2,1,64,512]{3,2,1,0:T(8,128)(2,1)S(1)}, u32[]{:S(2)}, u32[]{:S(2)}) collective-permute-start(bf16[2,1,64,512]{3,2,1,0:T(8,128)(2,1)S(1)} %get-tuple-element.42), channel_id=1, source_target_pairs={{0,4},{1,6},{2,5},{3,7},{4,12},{5,14},{6,13},{7,15},{8,0},{9,2},{1... | collective-permute-start | bytes 393224 | tf_op jit(solution)/shard_map/ppermute | solution.py:387
  75.4 1.8 %collective-permute-start.19 = (bf16[2,1,64,512]{3,2,1,0:T(8,128)(2,1)S(1)}, bf16[2,1,64,512]{3,2,1,0:T(8,128)(2,1)S(1)}, u32[]{:S(2)}, u32[]{:S(2)}) collective-permute-start(bf16[2,1,64,512]{3,2,1,0:T(8,128)(2,1)S(1)} %get-tuple-element.43), channel_id=1, source_target_pairs={{0,2},{1,0},{2,3},{3,1},{4,10},{5,8},{6,11},{7,9},{8,6},{9,4},{10,... | collective-permute-start | bytes 393224 | tf_op jit(solution)/shard_map/ppermute | solution.py:387
  77.1 5.4 %collective-permute-start.20 = (bf16[2,1,64,512]{3,2,1,0:T(8,128)(2,1)S(1)}, bf16[2,1,64,512]{3,2,1,0:T(8,128)(2,1)S(1)}, u32[]{:S(2)}, u32[]{:S(2)}) collective-permute-start(bf16[2,1,64,512]{3,2,1,0:T(8,128)(2,1)S(1)} %get-tuple-element.44), channel_id=1, source_target_pairs={{0,0},{1,2},{2,1},{3,3},{4,8},{5,10},{6,9},{7,11},{8,4},{9,6},{10,... | collective-permute-start | bytes 393224 | tf_op jit(solution)/shard_map/ppermute | solution.py:387
  82.6 2.9 %collective-permute-done.19.refs_10_ = bf16[2,1,64,512]{3,2,1,0:T(8,128)(2,1)S(1)} collective-permute-done((bf16[2,1,64,512]{3,2,1,0:T(8,128)(2,1)S(1)}, bf16[2,1,64,512]{3,2,1,0:T(8,128)(2,1)S(1)}, u32[]{:S(2)}, u32[]{:S(2)}) %collective-permute-start.19) | collective-permute-done | bytes 131104 | tf_op jit(solution)/shard_map/ppermute | solution.py:387
  85.5 3.6 %collective-permute-done.20.refs_11_ = bf16[2,1,64,512]{3,2,1,0:T(8,128)(2,1)S(1)} collective-permute-done((bf16[2,1,64,512]{3,2,1,0:T(8,128)(2,1)S(1)}, bf16[2,1,64,512]{3,2,1,0:T(8,128)(2,1)S(1)}, u32[]{:S(2)}, u32[]{:S(2)}) %collective-permute-start.20) | collective-permute-done | bytes 131104 | tf_op jit(solution)/shard_map/ppermute | solution.py:387
  89.1 1.4 %shard_map.54 = bf16[2,256,512]{2,1,0:T(8,128)(2,1)S(1)} custom-call(s32[7]{0:T(128)S(1)} %copy-done.2, bf16[2,2,64,512]{3,2,1,0:T(8,128)(2,1)S(1)} %collective-permute-done.4.refs_0_.refs_1_, bf16[2,2,64,512]{3,2,1,0:T(8,128)(2,1)S(1)} %collective-permute-done.5.refs_1_, bf16[2,2,64,512]{3,2,1,0:T(8,128)(2,1)S(1)} %collective-permute-done.6.refs_6_.refs_2_, ...), custom_call_target="tpu_custom_call" | custom-call | flops 536870912 | bytes 2621440 | tf_op jit(solution)/shard_map/pallas_call | solution.py:46
  90.8 1.4 %shard_map.53.own = bf16[2,256,512]{2,1,0:T(8,128)(2,1)S(1)} custom-call(s32[7]{0:T(128)S(1)} %copy-done.2, bf16[2,2,64,512]{3,2,1,0:T(8,128)(2,1)S(1)} %collective-permute-done.4.refs_0_.refs_1_, bf16[2,2,64,512]{3,2,1,0:T(8,128)(2,1)S(1)} %collective-permute-done.5.refs_1_, bf16[2,2,64,512]{3,2,1,0:T(8,128)(2,1)S(1)} %collective-permute-done.6.refs_6_.refs_2_, ...), custom_call_target="tpu_custom_call" | custom-call | flops 536870912 | bytes 2621440 | tf_op jit(solution)/shard_map/pallas_call | solution.py:46
  92.5 2.8 %shard_map.55 = f32[2,2,256,512]{3,2,1,0:T(8,128)} custom-call(s32[2]{0:T(128)S(1)} %copy-done.3, bf16[2,2,512,512]{3,2,1,0:T(8,128)(2,1)S(1)} %copy-done.1, bf16[2,256,512]{2,1,0:T(8,128)(2,1)S(1)} %shard_map.53.own, bf16[2,256,512]{2,1,0:T(8,128)(2,1)S(1)} %collective-permute-done.21.received), custom_call_target="tpu_custom_call" | custom-call | flops 1073741824 | bytes 4194304 | tf_op jit(solution)/shard_map/pallas_call | solution.py:46
  (41 shorter events, 7.8 us)
Async XLA Ops:
  4.5 13.1 %collective-permute-start.1 = (bf16[2,2,2,64,512]{4,3,2,1,0:T(8,128)(2,1)}, bf16[2,2,2,64,512]{4,3,2,1,0:T(8,128)(2,1)S(1)}, u32[]{:S(2)}, u32[]{:S(2)}) collective-permute-start(bf16[2,2,2,64,512]{4,3,2,1,0:T(8,128)(2,1)} %get-tuple-element.28), channel_id=1, source_target_pairs={{0,2},{2,0},{4,6},{6,4},{8,10},{10,8},{12,14},{14,12},{1,3},{3,1},... | collective-permute-start | bytes 1572872 | tf_op jit(solution)/shard_map/ppermute | solution.py:352
  5.8 14.5 %collective-permute-start.2 = (bf16[2,2,2,64,512]{4,3,2,1,0:T(8,128)(2,1)}, bf16[2,2,2,64,512]{4,3,2,1,0:T(8,128)(2,1)S(1)}, u32[]{:S(2)}, u32[]{:S(2)}) collective-permute-start(bf16[2,2,2,64,512]{4,3,2,1,0:T(8,128)(2,1)} %get-tuple-element.27.refs_2_), channel_id=1, source_target_pairs={{0,4},{2,6},{4,0},{6,2},{8,12},{10,14},{12,8},{14,10},{1,5},{3,7},... | collective-permute-start | bytes 1572872 | tf_op jit(solution)/shard_map/ppermute | solution.py:353
  9.3 19.5 %copy-start.4 = (bf16[2,2,2,64,512]{4,3,2,1,0:T(8,128)(2,1)S(1)}, bf16[2,2,2,64,512]{4,3,2,1,0:T(8,128)(2,1)}, u32[]{:S(2)}) copy-start(bf16[2,2,2,64,512]{4,3,2,1,0:T(8,128)(2,1)} %get-tuple-element.27.refs_2_) | copy-start | bytes 1572868
  14.8 14.1 %collective-permute-start = (bf16[2,2,2,64,512]{4,3,2,1,0:T(8,128)(2,1)S(1)}, bf16[2,2,2,64,512]{4,3,2,1,0:T(8,128)(2,1)S(1)}, u32[]{:S(2)}, u32[]{:S(2)}) collective-permute-start(bf16[2,2,2,64,512]{4,3,2,1,0:T(8,128)(2,1)S(1)} %get-tuple-element.26), channel_id=1, source_target_pairs={{0,2},{2,0},{4,6},{6,4},{8,10},{10,8},{12,14},{14,12},{1,3},{3,1},... | collective-permute-start | bytes 1572872 | tf_op jit(solution)/shard_map/ppermute | solution.py:354
  17.5 11.3 %collective-permute-start.3 = (bf16[2,2,2,64,512]{4,3,2,1,0:T(8,128)(2,1)S(1)}, bf16[2,2,2,64,512]{4,3,2,1,0:T(8,128)(2,1)S(1)}, u32[]{:S(2)}, u32[]{:S(2)}) collective-permute-start(bf16[2,2,2,64,512]{4,3,2,1,0:T(8,128)(2,1)S(1)} %collective-permute-done.1.refs_3_), channel_id=1, source_target_pairs={{0,4},{2,6},{4,0},{6,2},{8,12},{10,14},{12,8},{14,10},{1,5},{3,7},... | collective-permute-start | bytes 1572872 | tf_op jit(solution)/shard_map/ppermute | solution.py:363
  17.8 23.1 %collective-permute-start.9 = (bf16[2,2,2,64,512]{4,3,2,1,0:T(8,128)(2,1)S(1)}, bf16[2,2,2,64,512]{4,3,2,1,0:T(8,128)(2,1)S(1)}, u32[]{:S(2)}, u32[]{:S(2)}) collective-permute-start(bf16[2,2,2,64,512]{4,3,2,1,0:T(8,128)(2,1)S(1)} %get-tuple-element.36), channel_id=1, source_target_pairs={{0,2},{2,0},{4,6},{6,4},{8,10},{10,8},{12,14},{14,12},{1,3},{3,1},... | collective-permute-start | bytes 1572872 | tf_op jit(solution)/shard_map/ppermute | solution.py:352
  19.0 32.1 %collective-permute-start.10 = (bf16[2,2,2,64,512]{4,3,2,1,0:T(8,128)(2,1)S(1)}, bf16[2,2,2,64,512]{4,3,2,1,0:T(8,128)(2,1)S(1)}, u32[]{:S(2)}, u32[]{:S(2)}) collective-permute-start(bf16[2,2,2,64,512]{4,3,2,1,0:T(8,128)(2,1)S(1)} %get-tuple-element.35.refs_2_), channel_id=1, source_target_pairs={{0,4},{2,6},{4,0},{6,2},{8,12},{10,14},{12,8},{14,10},{1,5},{3,7},... | collective-permute-start | bytes 1572872 | tf_op jit(solution)/shard_map/ppermute | solution.py:353
  31.4 14.4 %collective-permute-start.4 = (bf16[2,2,64,512]{3,2,1,0:T(8,128)(2,1)S(1)}, bf16[2,2,64,512]{3,2,1,0:T(8,128)(2,1)S(1)}, u32[]{:S(2)}, u32[]{:S(2)}) collective-permute-start(bf16[2,2,64,512]{3,2,1,0:T(8,128)(2,1)S(1)} %get-tuple-element.29), channel_id=1, source_target_pairs={{0,6},{1,4},{2,7},{3,5},{4,14},{5,12},{6,15},{7,13},{8,2},{9,0},{1... | collective-permute-start | bytes 786440 | tf_op jit(solution)/shard_map/ppermute | solution.py:387
  39.8 20.9 %collective-permute-start.5 = (bf16[2,2,64,512]{3,2,1,0:T(8,128)(2,1)S(1)}, bf16[2,2,64,512]{3,2,1,0:T(8,128)(2,1)S(1)}, u32[]{:S(2)}, u32[]{:S(2)}) collective-permute-start(bf16[2,2,64,512]{3,2,1,0:T(8,128)(2,1)S(1)} %get-tuple-element.30), channel_id=1, source_target_pairs={{0,4},{1,6},{2,5},{3,7},{4,12},{5,14},{6,13},{7,15},{8,0},{9,2},{1... | collective-permute-start | bytes 786440 | tf_op jit(solution)/shard_map/ppermute | solution.py:387
  40.9 20.3 %collective-permute-start.8 = (bf16[2,2,2,64,512]{4,3,2,1,0:T(8,128)(2,1)S(1)}, bf16[2,2,2,64,512]{4,3,2,1,0:T(8,128)(2,1)S(1)}, u32[]{:S(2)}, u32[]{:S(2)}) collective-permute-start(bf16[2,2,2,64,512]{4,3,2,1,0:T(8,128)(2,1)S(1)} %get-tuple-element.34), channel_id=1, source_target_pairs={{0,2},{2,0},{4,6},{6,4},{8,10},{10,8},{12,14},{14,12},{1,3},{3,1},... | collective-permute-start | bytes 1572872 | tf_op jit(solution)/shard_map/ppermute | solution.py:354
  40.9 20.2 %collective-permute-start.11 = (bf16[2,1,2,64,512]{4,3,2,1,0:T(8,128)(2,1)S(1)}, bf16[2,1,2,64,512]{4,3,2,1,0:T(8,128)(2,1)S(1)}, u32[]{:S(2)}, u32[]{:S(2)}) collective-permute-start(bf16[2,1,2,64,512]{4,3,2,1,0:T(8,128)(2,1)S(1)} %get-tuple-element.46), channel_id=1, source_target_pairs={{0,4},{2,6},{4,0},{6,2},{8,12},{10,14},{12,8},{14,10},{1,5},{3,7},... | collective-permute-start | bytes 786440 | tf_op jit(solution)/shard_map/ppermute | solution.py:363
  45.8 15.4 %collective-permute-start.6 = (bf16[2,2,64,512]{3,2,1,0:T(8,128)(2,1)S(1)}, bf16[2,2,64,512]{3,2,1,0:T(8,128)(2,1)S(1)}, u32[]{:S(2)}, u32[]{:S(2)}) collective-permute-start(bf16[2,2,64,512]{3,2,1,0:T(8,128)(2,1)S(1)} %get-tuple-element.31), channel_id=1, source_target_pairs={{0,2},{1,0},{2,3},{3,1},{4,10},{5,8},{6,11},{7,9},{8,6},{9,4},{10,... | collective-permute-start | bytes 786440 | tf_op jit(solution)/shard_map/ppermute | solution.py:387
  51.1 18.2 %collective-permute-start.7 = (bf16[2,2,64,512]{3,2,1,0:T(8,128)(2,1)S(1)}, bf16[2,2,64,512]{3,2,1,0:T(8,128)(2,1)S(1)}, u32[]{:S(2)}, u32[]{:S(2)}) collective-permute-start(bf16[2,2,64,512]{3,2,1,0:T(8,128)(2,1)S(1)} %get-tuple-element.32), channel_id=1, source_target_pairs={{0,0},{1,2},{2,1},{3,3},{4,8},{5,10},{6,9},{7,11},{8,4},{9,6},{10,... | collective-permute-start | bytes 786440 | tf_op jit(solution)/shard_map/ppermute | solution.py:387
  60.7 10.5 %collective-permute-start.16 = (bf16[2,1,2,64,512]{4,3,2,1,0:T(8,128)(2,1)S(1)}, bf16[2,1,2,64,512]{4,3,2,1,0:T(8,128)(2,1)S(1)}, u32[]{:S(2)}, u32[]{:S(2)}) collective-permute-start(bf16[2,1,2,64,512]{4,3,2,1,0:T(8,128)(2,1)S(1)} %shard_map.51), channel_id=1, source_target_pairs={{0,4},{2,6},{4,0},{6,2},{8,12},{10,14},{12,8},{14,10},{1,5},{3,7},... | collective-permute-start | bytes 786440 | tf_op jit(solution)/shard_map/ppermute | solution.py:363
  62.4 10.2 %collective-permute-start.12 = (bf16[2,1,64,512]{3,2,1,0:T(8,128)(2,1)S(1)}, bf16[2,1,64,512]{3,2,1,0:T(8,128)(2,1)S(1)}, u32[]{:S(2)}, u32[]{:S(2)}) collective-permute-start(bf16[2,1,64,512]{3,2,1,0:T(8,128)(2,1)S(1)} %get-tuple-element.37), channel_id=1, source_target_pairs={{0,6},{1,4},{2,7},{3,5},{4,14},{5,12},{6,15},{7,13},{8,2},{9,0},{1... | collective-permute-start | bytes 393224 | tf_op jit(solution)/shard_map/ppermute | solution.py:387
  63.8 11.6 %collective-permute-start.13 = (bf16[2,1,64,512]{3,2,1,0:T(8,128)(2,1)S(1)}, bf16[2,1,64,512]{3,2,1,0:T(8,128)(2,1)S(1)}, u32[]{:S(2)}, u32[]{:S(2)}) collective-permute-start(bf16[2,1,64,512]{3,2,1,0:T(8,128)(2,1)S(1)} %get-tuple-element.38), channel_id=1, source_target_pairs={{0,4},{1,6},{2,5},{3,7},{4,12},{5,14},{6,13},{7,15},{8,0},{9,2},{1... | collective-permute-start | bytes 393224 | tf_op jit(solution)/shard_map/ppermute | solution.py:387
  67.3 9.8 %collective-permute-start.14 = (bf16[2,1,64,512]{3,2,1,0:T(8,128)(2,1)S(1)}, bf16[2,1,64,512]{3,2,1,0:T(8,128)(2,1)S(1)}, u32[]{:S(2)}, u32[]{:S(2)}) collective-permute-start(bf16[2,1,64,512]{3,2,1,0:T(8,128)(2,1)S(1)} %get-tuple-element.39), channel_id=1, source_target_pairs={{0,2},{1,0},{2,3},{3,1},{4,10},{5,8},{6,11},{7,9},{8,6},{9,4},{10,... | collective-permute-start | bytes 393224 | tf_op jit(solution)/shard_map/ppermute | solution.py:387
  69.3 13.2 %collective-permute-start.15 = (bf16[2,1,64,512]{3,2,1,0:T(8,128)(2,1)S(1)}, bf16[2,1,64,512]{3,2,1,0:T(8,128)(2,1)S(1)}, u32[]{:S(2)}, u32[]{:S(2)}) collective-permute-start(bf16[2,1,64,512]{3,2,1,0:T(8,128)(2,1)S(1)} %get-tuple-element.40), channel_id=1, source_target_pairs={{0,0},{1,2},{2,1},{3,3},{4,8},{5,10},{6,9},{7,11},{8,4},{9,6},{10,... | collective-permute-start | bytes 393224 | tf_op jit(solution)/shard_map/ppermute | solution.py:387
  72.6 10.0 %collective-permute-start.17 = (bf16[2,1,64,512]{3,2,1,0:T(8,128)(2,1)S(1)}, bf16[2,1,64,512]{3,2,1,0:T(8,128)(2,1)S(1)}, u32[]{:S(2)}, u32[]{:S(2)}) collective-permute-start(bf16[2,1,64,512]{3,2,1,0:T(8,128)(2,1)S(1)} %get-tuple-element.41), channel_id=1, source_target_pairs={{0,6},{1,4},{2,7},{3,5},{4,14},{5,12},{6,15},{7,13},{8,2},{9,0},{1... | collective-permute-start | bytes 393224 | tf_op jit(solution)/shard_map/ppermute | solution.py:387
  72.6 9.9 %collective-permute-start.18 = (bf16[2,1,64,512]{3,2,1,0:T(8,128)(2,1)S(1)}, bf16[2,1,64,512]{3,2,1,0:T(8,128)(2,1)S(1)}, u32[]{:S(2)}, u32[]{:S(2)}) collective-permute-start(bf16[2,1,64,512]{3,2,1,0:T(8,128)(2,1)S(1)} %get-tuple-element.42), channel_id=1, source_target_pairs={{0,4},{1,6},{2,5},{3,7},{4,12},{5,14},{6,13},{7,15},{8,0},{9,2},{1... | collective-permute-start | bytes 393224 | tf_op jit(solution)/shard_map/ppermute | solution.py:387
  75.4 10.1 %collective-permute-start.19 = (bf16[2,1,64,512]{3,2,1,0:T(8,128)(2,1)S(1)}, bf16[2,1,64,512]{3,2,1,0:T(8,128)(2,1)S(1)}, u32[]{:S(2)}, u32[]{:S(2)}) collective-permute-start(bf16[2,1,64,512]{3,2,1,0:T(8,128)(2,1)S(1)} %get-tuple-element.43), channel_id=1, source_target_pairs={{0,2},{1,0},{2,3},{3,1},{4,10},{5,8},{6,11},{7,9},{8,6},{9,4},{10,... | collective-permute-start | bytes 393224 | tf_op jit(solution)/shard_map/ppermute | solution.py:387
  77.1 15.4 %copy-start.3 = (s32[2]{0:T(128)S(1)}, s32[2]{0:T(128)}, u32[]{:S(2)}) copy-start(s32[2]{0:T(128)} %values.1) | copy-start | bytes 28
  77.1 12.0 %collective-permute-start.20 = (bf16[2,1,64,512]{3,2,1,0:T(8,128)(2,1)S(1)}, bf16[2,1,64,512]{3,2,1,0:T(8,128)(2,1)S(1)}, u32[]{:S(2)}, u32[]{:S(2)}) collective-permute-start(bf16[2,1,64,512]{3,2,1,0:T(8,128)(2,1)S(1)} %get-tuple-element.44), channel_id=1, source_target_pairs={{0,0},{1,2},{2,1},{3,3},{4,8},{5,10},{6,9},{7,11},{8,4},{9,6},{10,... | collective-permute-start | bytes 393224 | tf_op jit(solution)/shard_map/ppermute | solution.py:387
  90.6 2.0 %collective-permute-start.21 = (bf16[2,256,512]{2,1,0:T(8,128)(2,1)S(1)}, bf16[2,256,512]{2,1,0:T(8,128)(2,1)S(1)}, u32[]{:S(2)}, u32[]{:S(2)}) collective-permute-start(bf16[2,256,512]{2,1,0:T(8,128)(2,1)S(1)} %shard_map.54), channel_id=1, source_target_pairs={{0,1},{1,0},{2,3},{3,2},{4,5},{5,4},{6,7},{7,6},{8,9},{9,8},{10,11... | collective-permute-start | bytes 1572872 | tf_op jit(solution)/shard_map/ppermute | solution.py:392
  (3 other events, 24.7 us)

commit v7 on v6

--- a/solution.py
+++ b/solution.py
@@ -176,7 +176,7 @@
     )(*after)
 
 
-def second_level(plan, blocks, operands, pick):
+def second_level(plan, blocks, operands, pick, direct):
     width, batch, rows, ways, places = plan.width, plan.batch, plan.rows, plan.ways, plan.places
     held = ways * batch * rows
 
@@ -189,20 +189,24 @@
         high, place, way = plan.here()
         loads = []
         for block in range(blocks):
-            mine = [
-                copies.start(right_kept(block), right.at[:, block, place, way]),
-                copies.start(right_sent(block), right.at[:, block, place, 1 - way]),
+            moves = [
+                (right_kept(block), right.at[:, block, place, way]),
+                (right_sent(block), right.at[:, block, place, 1 - way]),
+                (left_kept(block), left.at[:, block, way]),
+                (left_sent(block), left.at[:, block, 1 - way]),
             ]
             for step, (kept, sent) in enumerate(others):
                 other = place ^ (step + 1)
-                mine.append(copies.start(kept(block), right.at[:, block, other, way]))
-                mine.append(copies.start(sent(block), right.at[:, block, other, 1 - way]))
-            mine.append(copies.start(left_kept(block), left.at[:, block, way]))
-            mine.append(copies.start(left_sent(block), left.at[:, block, 1 - way]))
-            loads.append(mine)
+                moves.append((kept(block), right.at[:, block, other, way]))
+                moves.append((sent(block), right.at[:, block, other, 1 - way]))
+            if direct:
+                for source, target in moves:
+                    target[...] = source[...]
+            else:
+                loads.append([copies.start(source, target) for source, target in moves])
         stores = []
         for block in range(blocks):
-            for copy in loads[block]:
+            for copy in loads[block] if loads else []:
                 copy.wait()
             halves = [
                 jnp.concatenate([left[part, block, high ^ a, branch ^ b] for a, b in plan.steps], axis=0)
@@ -216,11 +220,16 @@
                 ),
             )
             for part in range(2):
-                result[block, part] = (
-                    parts[part].astype(jnp.bfloat16).reshape(ways * batch, rows, width)
-                )
-            for index in range(ways * batch):
-                stores.append(copies.start(result.at[block, :, index], outs[index].at[:, block]))
+                done = parts[part].astype(jnp.bfloat16).reshape(ways * batch, rows, width)
+                if direct:
+                    for index in range(ways * batch):
+                        outs[index][part, block] = done[index]
+                else:
+                    result[block, part] = done
+            if not direct:
+                for index in range(ways * batch):
+                    source = result.at[block, :, index]
+                    stores.append(copies.start(source, outs[index].at[:, block]))
         for copy in stores:
             copy.wait()
 
@@ -232,7 +241,11 @@
     ]
     copies = blocks * (2 + 2 * places + ways * batch)
     flops = 8 * blocks * held * width * width
-    return run_kernel(body, outs, scratch, copies, flops, operands, [ANY] * len(operands))
+    count = 2 + 2 * places if direct else 0
+    specs = [VMEM] * count + [ANY] * (len(operands) - count)
+    return run_kernel(
+        body, outs, scratch, copies, flops, operands, specs, place=VMEM if direct else ANY
+    )
 
 
 def place_operands(plan, order, messages, chunk_blocks, scratch):
@@ -295,13 +308,16 @@
         copies = Copies(sems)
         core = lax.axis_index("branch")
         stores = []
+        half = width // 4
         for index, (top, item) in enumerate(((own, core), (received, 1 - core))):
             value = jnp.where(values[item] == 1, 1, 0)
             chosen = bound[value].reshape(2 * width, width)
-            parts = complex_dot(top[0], top[1], chosen)
-            for part in range(2):
-                result[index, part] = parts[part]
-            stores.append(copies.start(result.at[index], out.at[:, item]))
+            for low in range(0, width // 2, half):
+                span = pl.ds(low, half)
+                parts = complex_dot(top[0, span], top[1, span], chosen)
+                for part in range(2):
+                    result[index, part, span] = parts[part]
+                stores.append(copies.start(result.at[index, :, span], out.at[:, item, span]))
         for copy in stores:
             copy.wait()
 
@@ -309,7 +325,7 @@
         body,
         [jax.ShapeDtypeStruct(shape, jnp.float32)],
         [pltpu.VMEM((plan.batch, 2, width // 2, width), jnp.float32)],
-        plan.batch,
+        2 * plan.batch,
         8 * width**3,
         [slice_values, boundary, top_own, top_received],
         [SMEM, VMEM, VMEM, VMEM],
@@ -381,7 +397,7 @@
                 pairs = [(by(one, low), by(two, 0)) for one, two in zip(kept, sent)]
                 return *[by(ref, low) for ref in refs[:4]], pairs
 
-            rows = second_level(plan, count, operands, pick)
+            rows = second_level(plan, count, operands, pick, chunk > 0)
             messages.append(
                 [
                     lax.ppermute(value, ("mode", "branch"), to_rows(a, b))

time: 96.2 us -> 95.7 us (level)
  transfers between devices with their start and end apart: 22 -> 22, of which waited for: 7 -> 7; matrix products, arithmetic and copies ran while one was open for 0% -> 0% of each run, Pallas kernels for 13% -> 12%
where the time goes in v7:
time: 95.7 us; the launch traced here: 94.8 us
  starting transfers between devices  50 us (52%)
  waiting for transfers between devices  21.4 us (22%)
  Pallas kernels  19.8 us (21%)
  local copies, waits for them, and re-layouts  3.43 us (4%)
    ppermute x12, starting transfers between devices, per_device(): lax.ppermute(value, ('mode', 'branch'), to_rows(a, b))  43.7 us
    pallas_call x8, Pallas kernels, run_kernel(): pl.pallas_call(body, out_shape=outs, in_specs=specs, out_specs=[place] *...  19.8 us
    ppermute x12, waiting for transfers between devices, per_device(): lax.ppermute(value, ('mode', 'branch'), to_rows(a, b))  9.59 us
    ppermute x2, waiting for transfers between devices, per_device(): left_sent = lax.ppermute(left_send, 'mode', over_ways)  9.01 us
    unnamed x10, local copies, waits for them, and re-layouts  3.4 us
    ppermute x2, waiting for transfers between devices, per_device(): right_sent = lax.ppermute(right_send, 'mode', over_ways)  2.6 us
    ppermute x2, starting transfers between devices, per_device(): right_sent = lax.ppermute(right_send, 'mode', over_ways)  2.45 us
  transfers between devices with their start and end apart: 22, of which 7 were waited for; matrix products, arithmetic and copies ran while one was open for 0% of the time, Pallas kernels for 12%

profile of v7, /device:TPU:9, one launch (start us, length us, event | category | flops | bytes accessed | tf_op | source)
XLA Modules:
  0.0 94.8 jit_solution(4300070194450651564)
XLA Ops:
  0.0 4.5 %shard_map.47 = (bf16[2,2,2,64,512]{4,3,2,1,0:T(8,128)(2,1)}, bf16[2,2,2,64,512]{4,3,2,1,0:T(8,128)(2,1)}) custom-call(s32[7]{0:T(128)} %order.7, bf16[4,2,2,512,512]{4,3,2,1,0:T(8,128)(2,1)} %leaf.3), custom_call_target="tpu_custom_call" | custom-call | flops 1073741824 | bytes 3145728 | tf_op jit(solution)/shard_map/pallas_call | solution.py:46
  4.5 1.3 %collective-permute-start.1 = (bf16[2,2,2,64,512]{4,3,2,1,0:T(8,128)(2,1)}, bf16[2,2,2,64,512]{4,3,2,1,0:T(8,128)(2,1)S(1)}, u32[]{:S(2)}, u32[]{:S(2)}) collective-permute-start(bf16[2,2,2,64,512]{4,3,2,1,0:T(8,128)(2,1)} %get-tuple-element.28), channel_id=1, source_target_pairs={{0,2},{2,0},{4,6},{6,4},{8,10},{10,8},{12,14},{14,12},{1,3},{3,1},... | collective-permute-start | bytes 1572872 | tf_op jit(solution)/shard_map/ppermute | solution.py:368
  6.0 3.4 %copy-done = bf16[4,2,2,512,512]{4,3,2,1,0:T(8,128)(2,1)S(1)} copy-done((bf16[4,2,2,512,512]{4,3,2,1,0:T(8,128)(2,1)S(1)}, bf16[4,2,2,512,512]{4,3,2,1,0:T(8,128)(2,1)}, u32[]{:S(2)}) %copy-start) | copy-done | bytes 8388632
  9.3 5.5 %shard_map.46 = (bf16[2,2,2,64,512]{4,3,2,1,0:T(8,128)(2,1)S(1)}, bf16[2,2,2,64,512]{4,3,2,1,0:T(8,128)(2,1)S(1)}, bf16[2,2,2,64,512]{4,3,2,1,0:T(8,128)(2,1)S(1...) custom-call(s32[7]{0:T(128)S(1)} %copy-done.2, ...), custom_call_target="tpu_custom_call" | custom-call | flops 3221225472 | bytes 5242880 | tf_op jit(solution)/shard_map/pallas_call | solution.py:46
  14.9 2.6 %collective-permute-done.1.refs_3_ = bf16[2,2,2,64,512]{4,3,2,1,0:T(8,128)(2,1)S(1)} collective-permute-done((bf16[2,2,2,64,512]{4,3,2,1,0:T(8,128)(2,1)}, bf16[2,2,2,64,512]{4,3,2,1,0:T(8,128)(2,1)S(1)}, u32[]{:S(2)}, u32[]{:S(2)}) %collective-permute-start.1) | collective-permute-done | bytes 524320 | tf_op jit(solution)/shard_map/ppermute | solution.py:368
  20.2 8.6 %collective-permute-done.refs_1_ = bf16[2,2,2,64,512]{4,3,2,1,0:T(8,128)(2,1)S(1)} collective-permute-done((bf16[2,2,2,64,512]{4,3,2,1,0:T(8,128)(2,1)S(1)}, bf16[2,2,2,64,512]{4,3,2,1,0:T(8,128)(2,1)S(1)}, u32[]{:S(2)}, u32[]{:S(2)}) %collective-permute-start) | collective-permute-done | bytes 524320 | tf_op jit(solution)/shard_map/ppermute | solution.py:370
  28.9 2.5 %shard_map.48 = (bf16[2,2,64,512]{3,2,1,0:T(8,128)(2,1)S(1)}, bf16[2,2,64,512]{3,2,1,0:T(8,128)(2,1)S(1)}, bf16[2,2,64,512]{3,2,1,0:T(8,128)(2,1)S(1)}, bf16[2,2,64,512]{3,2,1,0:T(8,128)(2,1)S(1)}) custom-call(bf16[2,2,2,64,512]{4,3,2,1,0:T(8,128)(2,1)S(1)} %get-tuple-element.25.refs_0_, bf16[2,2,2,64,512]{4,3,2,1,0:T(8,128)(2,1)S(1)} %collective-permute-done.refs_1_, ...), custom_call_target="tpu_custom_call" | custom-call | flops 1073741824 | bytes 3145728 | tf_op jit(solution)/shard_map/pallas_call | solution.py:46
  31.4 8.4 %collective-permute-start.4 = (bf16[2,2,64,512]{3,2,1,0:T(8,128)(2,1)S(1)}, bf16[2,2,64,512]{3,2,1,0:T(8,128)(2,1)S(1)}, u32[]{:S(2)}, u32[]{:S(2)}) collective-permute-start(bf16[2,2,64,512]{3,2,1,0:T(8,128)(2,1)S(1)} %get-tuple-element.29), channel_id=1, source_target_pairs={{0,6},{1,4},{2,7},{3,5},{4,14},{5,12},{6,15},{7,13},{8,2},{9,0},{1... | collective-permute-start | bytes 786440 | tf_op jit(solution)/shard_map/ppermute | solution.py:403
  41.0 1.5 %collective-permute-start.11 = (bf16[2,1,2,64,512]{4,3,2,1,0:T(8,128)(2,1)S(1)}, bf16[2,1,2,64,512]{4,3,2,1,0:T(8,128)(2,1)S(1)}, u32[]{:S(2)}, u32[]{:S(2)}) collective-permute-start(bf16[2,1,2,64,512]{4,3,2,1,0:T(8,128)(2,1)S(1)} %get-tuple-element.46), channel_id=1, source_target_pairs={{0,4},{2,6},{4,0},{6,2},{8,12},{10,14},{12,8},{14,10},{1,5},{3,7},... | collective-permute-start | bytes 786440 | tf_op jit(solution)/shard_map/ppermute | solution.py:379
  42.5 3.3 %collective-permute-done.4.refs_0_.refs_1_ = bf16[2,2,64,512]{3,2,1,0:T(8,128)(2,1)S(1)} collective-permute-done((bf16[2,2,64,512]{3,2,1,0:T(8,128)(2,1)S(1)}, bf16[2,2,64,512]{3,2,1,0:T(8,128)(2,1)S(1)}, u32[]{:S(2)}, u32[]{:S(2)}) %collective-permute-start.4) | collective-permute-done | bytes 262176 | tf_op jit(solution)/shard_map/ppermute | solution.py:403
  45.8 5.3 %collective-permute-start.6 = (bf16[2,2,64,512]{3,2,1,0:T(8,128)(2,1)S(1)}, bf16[2,2,64,512]{3,2,1,0:T(8,128)(2,1)S(1)}, u32[]{:S(2)}, u32[]{:S(2)}) collective-permute-start(bf16[2,2,64,512]{3,2,1,0:T(8,128)(2,1)S(1)} %get-tuple-element.31), channel_id=1, source_target_pairs={{0,2},{1,0},{2,3},{3,1},{4,10},{5,8},{6,11},{7,9},{8,6},{9,4},{10,... | collective-permute-start | bytes 786440 | tf_op jit(solution)/shard_map/ppermute | solution.py:403
  51.1 9.6 %collective-permute-start.7 = (bf16[2,2,64,512]{3,2,1,0:T(8,128)(2,1)S(1)}, bf16[2,2,64,512]{3,2,1,0:T(8,128)(2,1)S(1)}, u32[]{:S(2)}, u32[]{:S(2)}) collective-permute-start(bf16[2,2,64,512]{3,2,1,0:T(8,128)(2,1)S(1)} %get-tuple-element.32), channel_id=1, source_target_pairs={{0,0},{1,2},{2,1},{3,3},{4,8},{5,10},{6,9},{7,11},{8,4},{9,6},{10,... | collective-permute-start | bytes 786440 | tf_op jit(solution)/shard_map/ppermute | solution.py:403
  62.1 1.3 %collective-permute-start.12 = (bf16[2,1,64,512]{3,2,1,0:T(8,128)(2,1)S(1)}, bf16[2,1,64,512]{3,2,1,0:T(8,128)(2,1)S(1)}, u32[]{:S(2)}, u32[]{:S(2)}) collective-permute-start(bf16[2,1,64,512]{3,2,1,0:T(8,128)(2,1)S(1)} %get-tuple-element.37), channel_id=1, source_target_pairs={{0,6},{1,4},{2,7},{3,5},{4,14},{5,12},{6,15},{7,13},{8,2},{9,0},{1... | collective-permute-start | bytes 393224 | tf_op jit(solution)/shard_map/ppermute | solution.py:403
  63.4 3.5 %collective-permute-start.13 = (bf16[2,1,64,512]{3,2,1,0:T(8,128)(2,1)S(1)}, bf16[2,1,64,512]{3,2,1,0:T(8,128)(2,1)S(1)}, u32[]{:S(2)}, u32[]{:S(2)}) collective-permute-start(bf16[2,1,64,512]{3,2,1,0:T(8,128)(2,1)S(1)} %get-tuple-element.38), channel_id=1, source_target_pairs={{0,4},{1,6},{2,5},{3,7},{4,12},{5,14},{6,13},{7,15},{8,0},{9,2},{1... | collective-permute-start | bytes 393224 | tf_op jit(solution)/shard_map/ppermute | solution.py:403
  67.0 2.1 %collective-permute-start.14 = (bf16[2,1,64,512]{3,2,1,0:T(8,128)(2,1)S(1)}, bf16[2,1,64,512]{3,2,1,0:T(8,128)(2,1)S(1)}, u32[]{:S(2)}, u32[]{:S(2)}) collective-permute-start(bf16[2,1,64,512]{3,2,1,0:T(8,128)(2,1)S(1)} %get-tuple-element.39), channel_id=1, source_target_pairs={{0,2},{1,0},{2,3},{3,1},{4,10},{5,8},{6,11},{7,9},{8,6},{9,4},{10,... | collective-permute-start | bytes 393224 | tf_op jit(solution)/shard_map/ppermute | solution.py:403
  69.1 1.9 %collective-permute-start.15 = (bf16[2,1,64,512]{3,2,1,0:T(8,128)(2,1)S(1)}, bf16[2,1,64,512]{3,2,1,0:T(8,128)(2,1)S(1)}, u32[]{:S(2)}, u32[]{:S(2)}) collective-permute-start(bf16[2,1,64,512]{3,2,1,0:T(8,128)(2,1)S(1)} %get-tuple-element.40), channel_id=1, source_target_pairs={{0,0},{1,2},{2,1},{3,3},{4,8},{5,10},{6,9},{7,11},{8,4},{9,6},{10,... | collective-permute-start | bytes 393224 | tf_op jit(solution)/shard_map/ppermute | solution.py:403
  72.0 3.0 %collective-permute-start.18 = (bf16[2,1,64,512]{3,2,1,0:T(8,128)(2,1)S(1)}, bf16[2,1,64,512]{3,2,1,0:T(8,128)(2,1)S(1)}, u32[]{:S(2)}, u32[]{:S(2)}) collective-permute-start(bf16[2,1,64,512]{3,2,1,0:T(8,128)(2,1)S(1)} %get-tuple-element.42), channel_id=1, source_target_pairs={{0,4},{1,6},{2,5},{3,7},{4,12},{5,14},{6,13},{7,15},{8,0},{9,2},{1... | collective-permute-start | bytes 393224 | tf_op jit(solution)/shard_map/ppermute | solution.py:403
  75.0 1.4 %collective-permute-start.19 = (bf16[2,1,64,512]{3,2,1,0:T(8,128)(2,1)S(1)}, bf16[2,1,64,512]{3,2,1,0:T(8,128)(2,1)S(1)}, u32[]{:S(2)}, u32[]{:S(2)}) collective-permute-start(bf16[2,1,64,512]{3,2,1,0:T(8,128)(2,1)S(1)} %get-tuple-element.43), channel_id=1, source_target_pairs={{0,2},{1,0},{2,3},{3,1},{4,10},{5,8},{6,11},{7,9},{8,6},{9,4},{10,... | collective-permute-start | bytes 393224 | tf_op jit(solution)/shard_map/ppermute | solution.py:403
  76.4 6.0 %collective-permute-start.20 = (bf16[2,1,64,512]{3,2,1,0:T(8,128)(2,1)S(1)}, bf16[2,1,64,512]{3,2,1,0:T(8,128)(2,1)S(1)}, u32[]{:S(2)}, u32[]{:S(2)}) collective-permute-start(bf16[2,1,64,512]{3,2,1,0:T(8,128)(2,1)S(1)} %get-tuple-element.44), channel_id=1, source_target_pairs={{0,0},{1,2},{2,1},{3,3},{4,8},{5,10},{6,9},{7,11},{8,4},{9,6},{10,... | collective-permute-start | bytes 393224 | tf_op jit(solution)/shard_map/ppermute | solution.py:403
  82.5 2.6 %collective-permute-done.19.refs_10_ = bf16[2,1,64,512]{3,2,1,0:T(8,128)(2,1)S(1)} collective-permute-done((bf16[2,1,64,512]{3,2,1,0:T(8,128)(2,1)S(1)}, bf16[2,1,64,512]{3,2,1,0:T(8,128)(2,1)S(1)}, u32[]{:S(2)}, u32[]{:S(2)}) %collective-permute-start.19) | collective-permute-done | bytes 131104 | tf_op jit(solution)/shard_map/ppermute | solution.py:403
  85.1 3.7 %collective-permute-done.20.refs_11_ = bf16[2,1,64,512]{3,2,1,0:T(8,128)(2,1)S(1)} collective-permute-done((bf16[2,1,64,512]{3,2,1,0:T(8,128)(2,1)S(1)}, bf16[2,1,64,512]{3,2,1,0:T(8,128)(2,1)S(1)}, u32[]{:S(2)}, u32[]{:S(2)}) %collective-permute-start.20) | collective-permute-done | bytes 131104 | tf_op jit(solution)/shard_map/ppermute | solution.py:403
  88.8 1.4 %shard_map.54 = bf16[2,256,512]{2,1,0:T(8,128)(2,1)S(1)} custom-call(s32[7]{0:T(128)S(1)} %copy-done.2, bf16[2,2,64,512]{3,2,1,0:T(8,128)(2,1)S(1)} %collective-permute-done.4.refs_0_.refs_1_, bf16[2,2,64,512]{3,2,1,0:T(8,128)(2,1)S(1)} %collective-permute-done.5.refs_1_, bf16[2,2,64,512]{3,2,1,0:T(8,128)(2,1)S(1)} %collective-permute-done.6.refs_6_.refs_2_, ...), custom_call_target="tpu_custom_call" | custom-call | flops 536870912 | bytes 2621440 | tf_op jit(solution)/shard_map/pallas_call | solution.py:46
  90.5 1.4 %shard_map.53.own = bf16[2,256,512]{2,1,0:T(8,128)(2,1)S(1)} custom-call(s32[7]{0:T(128)S(1)} %copy-done.2, bf16[2,2,64,512]{3,2,1,0:T(8,128)(2,1)S(1)} %collective-permute-done.4.refs_0_.refs_1_, bf16[2,2,64,512]{3,2,1,0:T(8,128)(2,1)S(1)} %collective-permute-done.5.refs_1_, bf16[2,2,64,512]{3,2,1,0:T(8,128)(2,1)S(1)} %collective-permute-done.6.refs_6_.refs_2_, ...), custom_call_target="tpu_custom_call" | custom-call | flops 536870912 | bytes 2621440 | tf_op jit(solution)/shard_map/pallas_call | solution.py:46
  92.2 2.6 %shard_map.55 = f32[2,2,256,512]{3,2,1,0:T(8,128)} custom-call(s32[2]{0:T(128)S(1)} %copy-done.3, bf16[2,2,512,512]{3,2,1,0:T(8,128)(2,1)S(1)} %copy-done.1, bf16[2,256,512]{2,1,0:T(8,128)(2,1)S(1)} %shard_map.53.own, bf16[2,256,512]{2,1,0:T(8,128)(2,1)S(1)} %collective-permute-done.21.received), custom_call_target="tpu_custom_call" | custom-call | flops 1073741824 | bytes 4194304 | tf_op jit(solution)/shard_map/pallas_call | solution.py:46
  (41 shorter events, 7.1 us)
Async XLA Ops:
  4.5 13.1 %collective-permute-start.1 = (bf16[2,2,2,64,512]{4,3,2,1,0:T(8,128)(2,1)}, bf16[2,2,2,64,512]{4,3,2,1,0:T(8,128)(2,1)S(1)}, u32[]{:S(2)}, u32[]{:S(2)}) collective-permute-start(bf16[2,2,2,64,512]{4,3,2,1,0:T(8,128)(2,1)} %get-tuple-element.28), channel_id=1, source_target_pairs={{0,2},{2,0},{4,6},{6,4},{8,10},{10,8},{12,14},{14,12},{1,3},{3,1},... | collective-permute-start | bytes 1572872 | tf_op jit(solution)/shard_map/ppermute | solution.py:368
  5.8 14.5 %collective-permute-start.2 = (bf16[2,2,2,64,512]{4,3,2,1,0:T(8,128)(2,1)}, bf16[2,2,2,64,512]{4,3,2,1,0:T(8,128)(2,1)S(1)}, u32[]{:S(2)}, u32[]{:S(2)}) collective-permute-start(bf16[2,2,2,64,512]{4,3,2,1,0:T(8,128)(2,1)} %get-tuple-element.27.refs_2_), channel_id=1, source_target_pairs={{0,4},{2,6},{4,0},{6,2},{8,12},{10,14},{12,8},{14,10},{1,5},{3,7},... | collective-permute-start | bytes 1572872 | tf_op jit(solution)/shard_map/ppermute | solution.py:369
  9.3 19.5 %copy-start.4 = (bf16[2,2,2,64,512]{4,3,2,1,0:T(8,128)(2,1)S(1)}, bf16[2,2,2,64,512]{4,3,2,1,0:T(8,128)(2,1)}, u32[]{:S(2)}) copy-start(bf16[2,2,2,64,512]{4,3,2,1,0:T(8,128)(2,1)} %get-tuple-element.27.refs_2_) | copy-start | bytes 1572868
  14.8 14.1 %collective-permute-start = (bf16[2,2,2,64,512]{4,3,2,1,0:T(8,128)(2,1)S(1)}, bf16[2,2,2,64,512]{4,3,2,1,0:T(8,128)(2,1)S(1)}, u32[]{:S(2)}, u32[]{:S(2)}) collective-permute-start(bf16[2,2,2,64,512]{4,3,2,1,0:T(8,128)(2,1)S(1)} %get-tuple-element.26), channel_id=1, source_target_pairs={{0,2},{2,0},{4,6},{6,4},{8,10},{10,8},{12,14},{14,12},{1,3},{3,1},... | collective-permute-start | bytes 1572872 | tf_op jit(solution)/shard_map/ppermute | solution.py:370
  17.5 11.3 %collective-permute-start.3 = (bf16[2,2,2,64,512]{4,3,2,1,0:T(8,128)(2,1)S(1)}, bf16[2,2,2,64,512]{4,3,2,1,0:T(8,128)(2,1)S(1)}, u32[]{:S(2)}, u32[]{:S(2)}) collective-permute-start(bf16[2,2,2,64,512]{4,3,2,1,0:T(8,128)(2,1)S(1)} %collective-permute-done.1.refs_3_), channel_id=1, source_target_pairs={{0,4},{2,6},{4,0},{6,2},{8,12},{10,14},{12,8},{14,10},{1,5},{3,7},... | collective-permute-start | bytes 1572872 | tf_op jit(solution)/shard_map/ppermute | solution.py:379
  17.8 23.1 %collective-permute-start.9 = (bf16[2,2,2,64,512]{4,3,2,1,0:T(8,128)(2,1)S(1)}, bf16[2,2,2,64,512]{4,3,2,1,0:T(8,128)(2,1)S(1)}, u32[]{:S(2)}, u32[]{:S(2)}) collective-permute-start(bf16[2,2,2,64,512]{4,3,2,1,0:T(8,128)(2,1)S(1)} %get-tuple-element.36), channel_id=1, source_target_pairs={{0,2},{2,0},{4,6},{6,4},{8,10},{10,8},{12,14},{14,12},{1,3},{3,1},... | collective-permute-start | bytes 1572872 | tf_op jit(solution)/shard_map/ppermute | solution.py:368
  19.0 32.1 %collective-permute-start.10 = (bf16[2,2,2,64,512]{4,3,2,1,0:T(8,128)(2,1)S(1)}, bf16[2,2,2,64,512]{4,3,2,1,0:T(8,128)(2,1)S(1)}, u32[]{:S(2)}, u32[]{:S(2)}) collective-permute-start(bf16[2,2,2,64,512]{4,3,2,1,0:T(8,128)(2,1)S(1)} %get-tuple-element.35.refs_2_), channel_id=1, source_target_pairs={{0,4},{2,6},{4,0},{6,2},{8,12},{10,14},{12,8},{14,10},{1,5},{3,7},... | collective-permute-start | bytes 1572872 | tf_op jit(solution)/shard_map/ppermute | solution.py:369
  31.4 14.3 %collective-permute-start.4 = (bf16[2,2,64,512]{3,2,1,0:T(8,128)(2,1)S(1)}, bf16[2,2,64,512]{3,2,1,0:T(8,128)(2,1)S(1)}, u32[]{:S(2)}, u32[]{:S(2)}) collective-permute-start(bf16[2,2,64,512]{3,2,1,0:T(8,128)(2,1)S(1)} %get-tuple-element.29), channel_id=1, source_target_pairs={{0,6},{1,4},{2,7},{3,5},{4,14},{5,12},{6,15},{7,13},{8,2},{9,0},{1... | collective-permute-start | bytes 786440 | tf_op jit(solution)/shard_map/ppermute | solution.py:403
  39.8 20.9 %collective-permute-start.5 = (bf16[2,2,64,512]{3,2,1,0:T(8,128)(2,1)S(1)}, bf16[2,2,64,512]{3,2,1,0:T(8,128)(2,1)S(1)}, u32[]{:S(2)}, u32[]{:S(2)}) collective-permute-start(bf16[2,2,64,512]{3,2,1,0:T(8,128)(2,1)S(1)} %get-tuple-element.30), channel_id=1, source_target_pairs={{0,4},{1,6},{2,5},{3,7},{4,12},{5,14},{6,13},{7,15},{8,0},{9,2},{1... | collective-permute-start | bytes 786440 | tf_op jit(solution)/shard_map/ppermute | solution.py:403
  40.9 20.3 %collective-permute-start.8 = (bf16[2,2,2,64,512]{4,3,2,1,0:T(8,128)(2,1)S(1)}, bf16[2,2,2,64,512]{4,3,2,1,0:T(8,128)(2,1)S(1)}, u32[]{:S(2)}, u32[]{:S(2)}) collective-permute-start(bf16[2,2,2,64,512]{4,3,2,1,0:T(8,128)(2,1)S(1)} %get-tuple-element.34), channel_id=1, source_target_pairs={{0,2},{2,0},{4,6},{6,4},{8,10},{10,8},{12,14},{14,12},{1,3},{3,1},... | collective-permute-start | bytes 1572872 | tf_op jit(solution)/shard_map/ppermute | solution.py:370
  41.0 20.2 %collective-permute-start.11 = (bf16[2,1,2,64,512]{4,3,2,1,0:T(8,128)(2,1)S(1)}, bf16[2,1,2,64,512]{4,3,2,1,0:T(8,128)(2,1)S(1)}, u32[]{:S(2)}, u32[]{:S(2)}) collective-permute-start(bf16[2,1,2,64,512]{4,3,2,1,0:T(8,128)(2,1)S(1)} %get-tuple-element.46), channel_id=1, source_target_pairs={{0,4},{2,6},{4,0},{6,2},{8,12},{10,14},{12,8},{14,10},{1,5},{3,7},... | collective-permute-start | bytes 786440 | tf_op jit(solution)/shard_map/ppermute | solution.py:379
  45.8 15.4 %collective-permute-start.6 = (bf16[2,2,64,512]{3,2,1,0:T(8,128)(2,1)S(1)}, bf16[2,2,64,512]{3,2,1,0:T(8,128)(2,1)S(1)}, u32[]{:S(2)}, u32[]{:S(2)}) collective-permute-start(bf16[2,2,64,512]{3,2,1,0:T(8,128)(2,1)S(1)} %get-tuple-element.31), channel_id=1, source_target_pairs={{0,2},{1,0},{2,3},{3,1},{4,10},{5,8},{6,11},{7,9},{8,6},{9,4},{10,... | collective-permute-start | bytes 786440 | tf_op jit(solution)/shard_map/ppermute | solution.py:403
  51.1 18.0 %collective-permute-start.7 = (bf16[2,2,64,512]{3,2,1,0:T(8,128)(2,1)S(1)}, bf16[2,2,64,512]{3,2,1,0:T(8,128)(2,1)S(1)}, u32[]{:S(2)}, u32[]{:S(2)}) collective-permute-start(bf16[2,2,64,512]{3,2,1,0:T(8,128)(2,1)S(1)} %get-tuple-element.32), channel_id=1, source_target_pairs={{0,0},{1,2},{2,1},{3,3},{4,8},{5,10},{6,9},{7,11},{8,4},{9,6},{10,... | collective-permute-start | bytes 786440 | tf_op jit(solution)/shard_map/ppermute | solution.py:403
  60.7 10.3 %collective-permute-start.16 = (bf16[2,1,2,64,512]{4,3,2,1,0:T(8,128)(2,1)S(1)}, bf16[2,1,2,64,512]{4,3,2,1,0:T(8,128)(2,1)S(1)}, u32[]{:S(2)}, u32[]{:S(2)}) collective-permute-start(bf16[2,1,2,64,512]{4,3,2,1,0:T(8,128)(2,1)S(1)} %shard_map.51), channel_id=1, source_target_pairs={{0,4},{2,6},{4,0},{6,2},{8,12},{10,14},{12,8},{14,10},{1,5},{3,7},... | collective-permute-start | bytes 786440 | tf_op jit(solution)/shard_map/ppermute | solution.py:379
  62.1 9.9 %collective-permute-start.12 = (bf16[2,1,64,512]{3,2,1,0:T(8,128)(2,1)S(1)}, bf16[2,1,64,512]{3,2,1,0:T(8,128)(2,1)S(1)}, u32[]{:S(2)}, u32[]{:S(2)}) collective-permute-start(bf16[2,1,64,512]{3,2,1,0:T(8,128)(2,1)S(1)} %get-tuple-element.37), channel_id=1, source_target_pairs={{0,6},{1,4},{2,7},{3,5},{4,14},{5,12},{6,15},{7,13},{8,2},{9,0},{1... | collective-permute-start | bytes 393224 | tf_op jit(solution)/shard_map/ppermute | solution.py:403
  63.4 11.6 %collective-permute-start.13 = (bf16[2,1,64,512]{3,2,1,0:T(8,128)(2,1)S(1)}, bf16[2,1,64,512]{3,2,1,0:T(8,128)(2,1)S(1)}, u32[]{:S(2)}, u32[]{:S(2)}) collective-permute-start(bf16[2,1,64,512]{3,2,1,0:T(8,128)(2,1)S(1)} %get-tuple-element.38), channel_id=1, source_target_pairs={{0,4},{1,6},{2,5},{3,7},{4,12},{5,14},{6,13},{7,15},{8,0},{9,2},{1... | collective-permute-start | bytes 393224 | tf_op jit(solution)/shard_map/ppermute | solution.py:403
  67.0 9.4 %collective-permute-start.14 = (bf16[2,1,64,512]{3,2,1,0:T(8,128)(2,1)S(1)}, bf16[2,1,64,512]{3,2,1,0:T(8,128)(2,1)S(1)}, u32[]{:S(2)}, u32[]{:S(2)}) collective-permute-start(bf16[2,1,64,512]{3,2,1,0:T(8,128)(2,1)S(1)} %get-tuple-element.39), channel_id=1, source_target_pairs={{0,2},{1,0},{2,3},{3,1},{4,10},{5,8},{6,11},{7,9},{8,6},{9,4},{10,... | collective-permute-start | bytes 393224 | tf_op jit(solution)/shard_map/ppermute | solution.py:403
  69.1 13.4 %collective-permute-start.15 = (bf16[2,1,64,512]{3,2,1,0:T(8,128)(2,1)S(1)}, bf16[2,1,64,512]{3,2,1,0:T(8,128)(2,1)S(1)}, u32[]{:S(2)}, u32[]{:S(2)}) collective-permute-start(bf16[2,1,64,512]{3,2,1,0:T(8,128)(2,1)S(1)} %get-tuple-element.40), channel_id=1, source_target_pairs={{0,0},{1,2},{2,1},{3,3},{4,8},{5,10},{6,9},{7,11},{8,4},{9,6},{10,... | collective-permute-start | bytes 393224 | tf_op jit(solution)/shard_map/ppermute | solution.py:403
  71.9 10.5 %collective-permute-start.17 = (bf16[2,1,64,512]{3,2,1,0:T(8,128)(2,1)S(1)}, bf16[2,1,64,512]{3,2,1,0:T(8,128)(2,1)S(1)}, u32[]{:S(2)}, u32[]{:S(2)}) collective-permute-start(bf16[2,1,64,512]{3,2,1,0:T(8,128)(2,1)S(1)} %get-tuple-element.41), channel_id=1, source_target_pairs={{0,6},{1,4},{2,7},{3,5},{4,14},{5,12},{6,15},{7,13},{8,2},{9,0},{1... | collective-permute-start | bytes 393224 | tf_op jit(solution)/shard_map/ppermute | solution.py:403
  72.0 10.5 %collective-permute-start.18 = (bf16[2,1,64,512]{3,2,1,0:T(8,128)(2,1)S(1)}, bf16[2,1,64,512]{3,2,1,0:T(8,128)(2,1)S(1)}, u32[]{:S(2)}, u32[]{:S(2)}) collective-permute-start(bf16[2,1,64,512]{3,2,1,0:T(8,128)(2,1)S(1)} %get-tuple-element.42), channel_id=1, source_target_pairs={{0,4},{1,6},{2,5},{3,7},{4,12},{5,14},{6,13},{7,15},{8,0},{9,2},{1... | collective-permute-start | bytes 393224 | tf_op jit(solution)/shard_map/ppermute | solution.py:403
  75.0 10.1 %collective-permute-start.19 = (bf16[2,1,64,512]{3,2,1,0:T(8,128)(2,1)S(1)}, bf16[2,1,64,512]{3,2,1,0:T(8,128)(2,1)S(1)}, u32[]{:S(2)}, u32[]{:S(2)}) collective-permute-start(bf16[2,1,64,512]{3,2,1,0:T(8,128)(2,1)S(1)} %get-tuple-element.43), channel_id=1, source_target_pairs={{0,2},{1,0},{2,3},{3,1},{4,10},{5,8},{6,11},{7,9},{8,6},{9,4},{10,... | collective-permute-start | bytes 393224 | tf_op jit(solution)/shard_map/ppermute | solution.py:403
  76.4 15.7 %copy-start.3 = (s32[2]{0:T(128)S(1)}, s32[2]{0:T(128)}, u32[]{:S(2)}) copy-start(s32[2]{0:T(128)} %values.1) | copy-start | bytes 28
  76.4 12.3 %collective-permute-start.20 = (bf16[2,1,64,512]{3,2,1,0:T(8,128)(2,1)S(1)}, bf16[2,1,64,512]{3,2,1,0:T(8,128)(2,1)S(1)}, u32[]{:S(2)}, u32[]{:S(2)}) collective-permute-start(bf16[2,1,64,512]{3,2,1,0:T(8,128)(2,1)S(1)} %get-tuple-element.44), channel_id=1, source_target_pairs={{0,0},{1,2},{2,1},{3,3},{4,8},{5,10},{6,9},{7,11},{8,4},{9,6},{10,... | collective-permute-start | bytes 393224 | tf_op jit(solution)/shard_map/ppermute | solution.py:403
  90.2 2.0 %collective-permute-start.21 = (bf16[2,256,512]{2,1,0:T(8,128)(2,1)S(1)}, bf16[2,256,512]{2,1,0:T(8,128)(2,1)S(1)}, u32[]{:S(2)}, u32[]{:S(2)}) collective-permute-start(bf16[2,256,512]{2,1,0:T(8,128)(2,1)S(1)} %shard_map.54), channel_id=1, source_target_pairs={{0,1},{1,0},{2,3},{3,2},{4,5},{5,4},{6,7},{7,6},{8,9},{9,8},{10,11... | collective-permute-start | bytes 1572872 | tf_op jit(solution)/shard_map/ppermute | solution.py:408
  (3 other events, 25.1 us)

commit v8 on v7

--- a/solution.py
+++ b/solution.py
@@ -176,7 +176,7 @@
     )(*after)
 
 
-def second_level(plan, blocks, operands, pick, direct):
+def second_level(plan, blocks, operands, pick, direct, near):
     width, batch, rows, ways, places = plan.width, plan.batch, plan.rows, plan.ways, plan.places
     held = ways * batch * rows
 
@@ -199,7 +199,7 @@
                 other = place ^ (step + 1)
                 moves.append((kept(block), right.at[:, block, other, way]))
                 moves.append((sent(block), right.at[:, block, other, 1 - way]))
-            if direct:
+            if near:
                 for source, target in moves:
                     target[...] = source[...]
             else:
@@ -241,7 +241,7 @@
     ]
     copies = blocks * (2 + 2 * places + ways * batch)
     flops = 8 * blocks * held * width * width
-    count = 2 + 2 * places if direct else 0
+    count = 2 + 2 * places if near else 0
     specs = [VMEM] * count + [ANY] * (len(operands) - count)
     return run_kernel(
         body, outs, scratch, copies, flops, operands, specs, place=VMEM if direct else ANY
@@ -397,7 +397,7 @@
                 pairs = [(by(one, low), by(two, 0)) for one, two in zip(kept, sent)]
                 return *[by(ref, low) for ref in refs[:4]], pairs
 
-            rows = second_level(plan, count, operands, pick, chunk > 0)
+            rows = second_level(plan, count, operands, pick, chunk > 0, True)
             messages.append(
                 [
                     lax.ppermute(value, ("mode", "branch"), to_rows(a, b))

time: 95.7 us -> 95.7 us (level)
  no operation moved by 1% of the time
where the time goes in v8:
time: 95.7 us; the launch traced here: 94.8 us
  starting transfers between devices  50 us (52%)
  waiting for transfers between devices  21.4 us (22%)
  Pallas kernels  19.8 us (21%)
  local copies, waits for them, and re-layouts  3.43 us (4%)
    ppermute x12, starting transfers between devices, per_device(): lax.ppermute(value, ('mode', 'branch'), to_rows(a, b))  43.8 us
    pallas_call x8, Pallas kernels, run_kernel(): pl.pallas_call(body, out_shape=outs, in_specs=specs, out_specs=[place] *...  19.8 us
    ppermute x12, waiting for transfers between devices, per_device(): lax.ppermute(value, ('mode', 'branch'), to_rows(a, b))  9.57 us
    ppermute x2, waiting for transfers between devices, per_device(): left_sent = lax.ppermute(left_send, 'mode', over_ways)  9 us
    unnamed x10, local copies, waits for them, and re-layouts  3.4 us
    ppermute x2, waiting for transfers between devices, per_device(): right_sent = lax.ppermute(right_send, 'mode', over_ways)  2.6 us
    ppermute x2, starting transfers between devices, per_device(): right_sent = lax.ppermute(right_send, 'mode', over_ways)  2.45 us
  transfers between devices with their start and end apart: 22, of which 7 were waited for; matrix products, arithmetic and copies ran while one was open for 0% of the time, Pallas kernels for 12%

profile of v8, /device:TPU:9, one launch (start us, length us, event | category | flops | bytes accessed | tf_op | source)
XLA Modules:
  0.0 94.8 jit_solution(17933935080915402033)
XLA Ops:
  0.0 4.5 %shard_map.47 = (bf16[2,2,2,64,512]{4,3,2,1,0:T(8,128)(2,1)}, bf16[2,2,2,64,512]{4,3,2,1,0:T(8,128)(2,1)}) custom-call(s32[7]{0:T(128)} %order.7, bf16[4,2,2,512,512]{4,3,2,1,0:T(8,128)(2,1)} %leaf.3), custom_call_target="tpu_custom_call" | custom-call | flops 1073741824 | bytes 3145728 | tf_op jit(solution)/shard_map/pallas_call | solution.py:46
  4.5 1.3 %collective-permute-start.1 = (bf16[2,2,2,64,512]{4,3,2,1,0:T(8,128)(2,1)}, bf16[2,2,2,64,512]{4,3,2,1,0:T(8,128)(2,1)S(1)}, u32[]{:S(2)}, u32[]{:S(2)}) collective-permute-start(bf16[2,2,2,64,512]{4,3,2,1,0:T(8,128)(2,1)} %get-tuple-element.28), channel_id=1, source_target_pairs={{0,2},{2,0},{4,6},{6,4},{8,10},{10,8},{12,14},{14,12},{1,3},{3,1},... | collective-permute-start | bytes 1572872 | tf_op jit(solution)/shard_map/ppermute | solution.py:368
  6.0 3.4 %copy-done = bf16[4,2,2,512,512]{4,3,2,1,0:T(8,128)(2,1)S(1)} copy-done((bf16[4,2,2,512,512]{4,3,2,1,0:T(8,128)(2,1)S(1)}, bf16[4,2,2,512,512]{4,3,2,1,0:T(8,128)(2,1)}, u32[]{:S(2)}) %copy-start) | copy-done | bytes 8388632
  9.3 5.5 %shard_map.46 = (bf16[2,2,2,64,512]{4,3,2,1,0:T(8,128)(2,1)S(1)}, bf16[2,2,2,64,512]{4,3,2,1,0:T(8,128)(2,1)S(1)}, bf16[2,2,2,64,512]{4,3,2,1,0:T(8,128)(2,1)S(1...) custom-call(s32[7]{0:T(128)S(1)} %copy-done.2, ...), custom_call_target="tpu_custom_call" | custom-call | flops 3221225472 | bytes 5242880 | tf_op jit(solution)/shard_map/pallas_call | solution.py:46
  14.9 2.6 %collective-permute-done.1.refs_3_ = bf16[2,2,2,64,512]{4,3,2,1,0:T(8,128)(2,1)S(1)} collective-permute-done((bf16[2,2,2,64,512]{4,3,2,1,0:T(8,128)(2,1)}, bf16[2,2,2,64,512]{4,3,2,1,0:T(8,128)(2,1)S(1)}, u32[]{:S(2)}, u32[]{:S(2)}) %collective-permute-start.1) | collective-permute-done | bytes 524320 | tf_op jit(solution)/shard_map/ppermute | solution.py:368
  20.2 8.6 %collective-permute-done.refs_1_ = bf16[2,2,2,64,512]{4,3,2,1,0:T(8,128)(2,1)S(1)} collective-permute-done((bf16[2,2,2,64,512]{4,3,2,1,0:T(8,128)(2,1)S(1)}, bf16[2,2,2,64,512]{4,3,2,1,0:T(8,128)(2,1)S(1)}, u32[]{:S(2)}, u32[]{:S(2)}) %collective-permute-start) | collective-permute-done | bytes 524320 | tf_op jit(solution)/shard_map/ppermute | solution.py:370
  28.9 2.5 %shard_map.48 = (bf16[2,2,64,512]{3,2,1,0:T(8,128)(2,1)S(1)}, bf16[2,2,64,512]{3,2,1,0:T(8,128)(2,1)S(1)}, bf16[2,2,64,512]{3,2,1,0:T(8,128)(2,1)S(1)}, bf16[2,2,64,512]{3,2,1,0:T(8,128)(2,1)S(1)}) custom-call(bf16[2,2,2,64,512]{4,3,2,1,0:T(8,128)(2,1)S(1)} %get-tuple-element.25.refs_0_, bf16[2,2,2,64,512]{4,3,2,1,0:T(8,128)(2,1)S(1)} %collective-permute-done.refs_1_, ...), custom_call_target="tpu_custom_call" | custom-call | flops 1073741824 | bytes 3145728 | tf_op jit(solution)/shard_map/pallas_call | solution.py:46
  31.4 8.4 %collective-permute-start.4 = (bf16[2,2,64,512]{3,2,1,0:T(8,128)(2,1)S(1)}, bf16[2,2,64,512]{3,2,1,0:T(8,128)(2,1)S(1)}, u32[]{:S(2)}, u32[]{:S(2)}) collective-permute-start(bf16[2,2,64,512]{3,2,1,0:T(8,128)(2,1)S(1)} %get-tuple-element.29), channel_id=1, source_target_pairs={{0,6},{1,4},{2,7},{3,5},{4,14},{5,12},{6,15},{7,13},{8,2},{9,0},{1... | collective-permute-start | bytes 786440 | tf_op jit(solution)/shard_map/ppermute | solution.py:403
  40.9 1.5 %collective-permute-start.11 = (bf16[2,1,2,64,512]{4,3,2,1,0:T(8,128)(2,1)S(1)}, bf16[2,1,2,64,512]{4,3,2,1,0:T(8,128)(2,1)S(1)}, u32[]{:S(2)}, u32[]{:S(2)}) collective-permute-start(bf16[2,1,2,64,512]{4,3,2,1,0:T(8,128)(2,1)S(1)} %get-tuple-element.46), channel_id=1, source_target_pairs={{0,4},{2,6},{4,0},{6,2},{8,12},{10,14},{12,8},{14,10},{1,5},{3,7},... | collective-permute-start | bytes 786440 | tf_op jit(solution)/shard_map/ppermute | solution.py:379
  42.5 3.3 %collective-permute-done.4.refs_0_.refs_1_ = bf16[2,2,64,512]{3,2,1,0:T(8,128)(2,1)S(1)} collective-permute-done((bf16[2,2,64,512]{3,2,1,0:T(8,128)(2,1)S(1)}, bf16[2,2,64,512]{3,2,1,0:T(8,128)(2,1)S(1)}, u32[]{:S(2)}, u32[]{:S(2)}) %collective-permute-start.4) | collective-permute-done | bytes 262176 | tf_op jit(solution)/shard_map/ppermute | solution.py:403
  45.8 5.3 %collective-permute-start.6 = (bf16[2,2,64,512]{3,2,1,0:T(8,128)(2,1)S(1)}, bf16[2,2,64,512]{3,2,1,0:T(8,128)(2,1)S(1)}, u32[]{:S(2)}, u32[]{:S(2)}) collective-permute-start(bf16[2,2,64,512]{3,2,1,0:T(8,128)(2,1)S(1)} %get-tuple-element.31), channel_id=1, source_target_pairs={{0,2},{1,0},{2,3},{3,1},{4,10},{5,8},{6,11},{7,9},{8,6},{9,4},{10,... | collective-permute-start | bytes 786440 | tf_op jit(solution)/shard_map/ppermute | solution.py:403
  51.1 9.6 %collective-permute-start.7 = (bf16[2,2,64,512]{3,2,1,0:T(8,128)(2,1)S(1)}, bf16[2,2,64,512]{3,2,1,0:T(8,128)(2,1)S(1)}, u32[]{:S(2)}, u32[]{:S(2)}) collective-permute-start(bf16[2,2,64,512]{3,2,1,0:T(8,128)(2,1)S(1)} %get-tuple-element.32), channel_id=1, source_target_pairs={{0,0},{1,2},{2,1},{3,3},{4,8},{5,10},{6,9},{7,11},{8,4},{9,6},{10,... | collective-permute-start | bytes 786440 | tf_op jit(solution)/shard_map/ppermute | solution.py:403
  62.1 1.3 %collective-permute-start.12 = (bf16[2,1,64,512]{3,2,1,0:T(8,128)(2,1)S(1)}, bf16[2,1,64,512]{3,2,1,0:T(8,128)(2,1)S(1)}, u32[]{:S(2)}, u32[]{:S(2)}) collective-permute-start(bf16[2,1,64,512]{3,2,1,0:T(8,128)(2,1)S(1)} %get-tuple-element.37), channel_id=1, source_target_pairs={{0,6},{1,4},{2,7},{3,5},{4,14},{5,12},{6,15},{7,13},{8,2},{9,0},{1... | collective-permute-start | bytes 393224 | tf_op jit(solution)/shard_map/ppermute | solution.py:403
  63.4 3.5 %collective-permute-start.13 = (bf16[2,1,64,512]{3,2,1,0:T(8,128)(2,1)S(1)}, bf16[2,1,64,512]{3,2,1,0:T(8,128)(2,1)S(1)}, u32[]{:S(2)}, u32[]{:S(2)}) collective-permute-start(bf16[2,1,64,512]{3,2,1,0:T(8,128)(2,1)S(1)} %get-tuple-element.38), channel_id=1, source_target_pairs={{0,4},{1,6},{2,5},{3,7},{4,12},{5,14},{6,13},{7,15},{8,0},{9,2},{1... | collective-permute-start | bytes 393224 | tf_op jit(solution)/shard_map/ppermute | solution.py:403
  67.0 2.0 %collective-permute-start.14 = (bf16[2,1,64,512]{3,2,1,0:T(8,128)(2,1)S(1)}, bf16[2,1,64,512]{3,2,1,0:T(8,128)(2,1)S(1)}, u32[]{:S(2)}, u32[]{:S(2)}) collective-permute-start(bf16[2,1,64,512]{3,2,1,0:T(8,128)(2,1)S(1)} %get-tuple-element.39), channel_id=1, source_target_pairs={{0,2},{1,0},{2,3},{3,1},{4,10},{5,8},{6,11},{7,9},{8,6},{9,4},{10,... | collective-permute-start | bytes 393224 | tf_op jit(solution)/shard_map/ppermute | solution.py:403
  69.0 1.9 %collective-permute-start.15 = (bf16[2,1,64,512]{3,2,1,0:T(8,128)(2,1)S(1)}, bf16[2,1,64,512]{3,2,1,0:T(8,128)(2,1)S(1)}, u32[]{:S(2)}, u32[]{:S(2)}) collective-permute-start(bf16[2,1,64,512]{3,2,1,0:T(8,128)(2,1)S(1)} %get-tuple-element.40), channel_id=1, source_target_pairs={{0,0},{1,2},{2,1},{3,3},{4,8},{5,10},{6,9},{7,11},{8,4},{9,6},{10,... | collective-permute-start | bytes 393224 | tf_op jit(solution)/shard_map/ppermute | solution.py:403
  71.9 3.1 %collective-permute-start.18 = (bf16[2,1,64,512]{3,2,1,0:T(8,128)(2,1)S(1)}, bf16[2,1,64,512]{3,2,1,0:T(8,128)(2,1)S(1)}, u32[]{:S(2)}, u32[]{:S(2)}) collective-permute-start(bf16[2,1,64,512]{3,2,1,0:T(8,128)(2,1)S(1)} %get-tuple-element.42), channel_id=1, source_target_pairs={{0,4},{1,6},{2,5},{3,7},{4,12},{5,14},{6,13},{7,15},{8,0},{9,2},{1... | collective-permute-start | bytes 393224 | tf_op jit(solution)/shard_map/ppermute | solution.py:403
  75.0 1.4 %collective-permute-start.19 = (bf16[2,1,64,512]{3,2,1,0:T(8,128)(2,1)S(1)}, bf16[2,1,64,512]{3,2,1,0:T(8,128)(2,1)S(1)}, u32[]{:S(2)}, u32[]{:S(2)}) collective-permute-start(bf16[2,1,64,512]{3,2,1,0:T(8,128)(2,1)S(1)} %get-tuple-element.43), channel_id=1, source_target_pairs={{0,2},{1,0},{2,3},{3,1},{4,10},{5,8},{6,11},{7,9},{8,6},{9,4},{10,... | collective-permute-start | bytes 393224 | tf_op jit(solution)/shard_map/ppermute | solution.py:403
  76.4 6.0 %collective-permute-start.20 = (bf16[2,1,64,512]{3,2,1,0:T(8,128)(2,1)S(1)}, bf16[2,1,64,512]{3,2,1,0:T(8,128)(2,1)S(1)}, u32[]{:S(2)}, u32[]{:S(2)}) collective-permute-start(bf16[2,1,64,512]{3,2,1,0:T(8,128)(2,1)S(1)} %get-tuple-element.44), channel_id=1, source_target_pairs={{0,0},{1,2},{2,1},{3,3},{4,8},{5,10},{6,9},{7,11},{8,4},{9,6},{10,... | collective-permute-start | bytes 393224 | tf_op jit(solution)/shard_map/ppermute | solution.py:403
  82.5 2.6 %collective-permute-done.19.refs_10_ = bf16[2,1,64,512]{3,2,1,0:T(8,128)(2,1)S(1)} collective-permute-done((bf16[2,1,64,512]{3,2,1,0:T(8,128)(2,1)S(1)}, bf16[2,1,64,512]{3,2,1,0:T(8,128)(2,1)S(1)}, u32[]{:S(2)}, u32[]{:S(2)}) %collective-permute-start.19) | collective-permute-done | bytes 131104 | tf_op jit(solution)/shard_map/ppermute | solution.py:403
  85.1 3.7 %collective-permute-done.20.refs_11_ = bf16[2,1,64,512]{3,2,1,0:T(8,128)(2,1)S(1)} collective-permute-done((bf16[2,1,64,512]{3,2,1,0:T(8,128)(2,1)S(1)}, bf16[2,1,64,512]{3,2,1,0:T(8,128)(2,1)S(1)}, u32[]{:S(2)}, u32[]{:S(2)}) %collective-permute-start.20) | collective-permute-done | bytes 131104 | tf_op jit(solution)/shard_map/ppermute | solution.py:403
  88.8 1.4 %shard_map.54 = bf16[2,256,512]{2,1,0:T(8,128)(2,1)S(1)} custom-call(s32[7]{0:T(128)S(1)} %copy-done.2, bf16[2,2,64,512]{3,2,1,0:T(8,128)(2,1)S(1)} %collective-permute-done.4.refs_0_.refs_1_, bf16[2,2,64,512]{3,2,1,0:T(8,128)(2,1)S(1)} %collective-permute-done.5.refs_1_, bf16[2,2,64,512]{3,2,1,0:T(8,128)(2,1)S(1)} %collective-permute-done.6.refs_6_.refs_2_, ...), custom_call_target="tpu_custom_call" | custom-call | flops 536870912 | bytes 2621440 | tf_op jit(solution)/shard_map/pallas_call | solution.py:46
  90.5 1.4 %shard_map.53.own = bf16[2,256,512]{2,1,0:T(8,128)(2,1)S(1)} custom-call(s32[7]{0:T(128)S(1)} %copy-done.2, bf16[2,2,64,512]{3,2,1,0:T(8,128)(2,1)S(1)} %collective-permute-done.4.refs_0_.refs_1_, bf16[2,2,64,512]{3,2,1,0:T(8,128)(2,1)S(1)} %collective-permute-done.5.refs_1_, bf16[2,2,64,512]{3,2,1,0:T(8,128)(2,1)S(1)} %collective-permute-done.6.refs_6_.refs_2_, ...), custom_call_target="tpu_custom_call" | custom-call | flops 536870912 | bytes 2621440 | tf_op jit(solution)/shard_map/pallas_call | solution.py:46
  92.2 2.6 %shard_map.55 = f32[2,2,256,512]{3,2,1,0:T(8,128)} custom-call(s32[2]{0:T(128)S(1)} %copy-done.3, bf16[2,2,512,512]{3,2,1,0:T(8,128)(2,1)S(1)} %copy-done.1, bf16[2,256,512]{2,1,0:T(8,128)(2,1)S(1)} %shard_map.53.own, bf16[2,256,512]{2,1,0:T(8,128)(2,1)S(1)} %collective-permute-done.21.received), custom_call_target="tpu_custom_call" | custom-call | flops 1073741824 | bytes 4194304 | tf_op jit(solution)/shard_map/pallas_call | solution.py:46
  (41 shorter events, 7.1 us)
Async XLA Ops:
  4.5 13.1 %collective-permute-start.1 = (bf16[2,2,2,64,512]{4,3,2,1,0:T(8,128)(2,1)}, bf16[2,2,2,64,512]{4,3,2,1,0:T(8,128)(2,1)S(1)}, u32[]{:S(2)}, u32[]{:S(2)}) collective-permute-start(bf16[2,2,2,64,512]{4,3,2,1,0:T(8,128)(2,1)} %get-tuple-element.28), channel_id=1, source_target_pairs={{0,2},{2,0},{4,6},{6,4},{8,10},{10,8},{12,14},{14,12},{1,3},{3,1},... | collective-permute-start | bytes 1572872 | tf_op jit(solution)/shard_map/ppermute | solution.py:368
  5.8 14.5 %collective-permute-start.2 = (bf16[2,2,2,64,512]{4,3,2,1,0:T(8,128)(2,1)}, bf16[2,2,2,64,512]{4,3,2,1,0:T(8,128)(2,1)S(1)}, u32[]{:S(2)}, u32[]{:S(2)}) collective-permute-start(bf16[2,2,2,64,512]{4,3,2,1,0:T(8,128)(2,1)} %get-tuple-element.27.refs_2_), channel_id=1, source_target_pairs={{0,4},{2,6},{4,0},{6,2},{8,12},{10,14},{12,8},{14,10},{1,5},{3,7},... | collective-permute-start | bytes 1572872 | tf_op jit(solution)/shard_map/ppermute | solution.py:369
  9.3 19.5 %copy-start.4 = (bf16[2,2,2,64,512]{4,3,2,1,0:T(8,128)(2,1)S(1)}, bf16[2,2,2,64,512]{4,3,2,1,0:T(8,128)(2,1)}, u32[]{:S(2)}) copy-start(bf16[2,2,2,64,512]{4,3,2,1,0:T(8,128)(2,1)} %get-tuple-element.27.refs_2_) | copy-start | bytes 1572868
  14.8 14.1 %collective-permute-start = (bf16[2,2,2,64,512]{4,3,2,1,0:T(8,128)(2,1)S(1)}, bf16[2,2,2,64,512]{4,3,2,1,0:T(8,128)(2,1)S(1)}, u32[]{:S(2)}, u32[]{:S(2)}) collective-permute-start(bf16[2,2,2,64,512]{4,3,2,1,0:T(8,128)(2,1)S(1)} %get-tuple-element.26), channel_id=1, source_target_pairs={{0,2},{2,0},{4,6},{6,4},{8,10},{10,8},{12,14},{14,12},{1,3},{3,1},... | collective-permute-start | bytes 1572872 | tf_op jit(solution)/shard_map/ppermute | solution.py:370
  17.5 11.3 %collective-permute-start.3 = (bf16[2,2,2,64,512]{4,3,2,1,0:T(8,128)(2,1)S(1)}, bf16[2,2,2,64,512]{4,3,2,1,0:T(8,128)(2,1)S(1)}, u32[]{:S(2)}, u32[]{:S(2)}) collective-permute-start(bf16[2,2,2,64,512]{4,3,2,1,0:T(8,128)(2,1)S(1)} %collective-permute-done.1.refs_3_), channel_id=1, source_target_pairs={{0,4},{2,6},{4,0},{6,2},{8,12},{10,14},{12,8},{14,10},{1,5},{3,7},... | collective-permute-start | bytes 1572872 | tf_op jit(solution)/shard_map/ppermute | solution.py:379
  17.8 23.1 %collective-permute-start.9 = (bf16[2,2,2,64,512]{4,3,2,1,0:T(8,128)(2,1)S(1)}, bf16[2,2,2,64,512]{4,3,2,1,0:T(8,128)(2,1)S(1)}, u32[]{:S(2)}, u32[]{:S(2)}) collective-permute-start(bf16[2,2,2,64,512]{4,3,2,1,0:T(8,128)(2,1)S(1)} %get-tuple-element.36), channel_id=1, source_target_pairs={{0,2},{2,0},{4,6},{6,4},{8,10},{10,8},{12,14},{14,12},{1,3},{3,1},... | collective-permute-start | bytes 1572872 | tf_op jit(solution)/shard_map/ppermute | solution.py:368
  19.0 32.1 %collective-permute-start.10 = (bf16[2,2,2,64,512]{4,3,2,1,0:T(8,128)(2,1)S(1)}, bf16[2,2,2,64,512]{4,3,2,1,0:T(8,128)(2,1)S(1)}, u32[]{:S(2)}, u32[]{:S(2)}) collective-permute-start(bf16[2,2,2,64,512]{4,3,2,1,0:T(8,128)(2,1)S(1)} %get-tuple-element.35.refs_2_), channel_id=1, source_target_pairs={{0,4},{2,6},{4,0},{6,2},{8,12},{10,14},{12,8},{14,10},{1,5},{3,7},... | collective-permute-start | bytes 1572872 | tf_op jit(solution)/shard_map/ppermute | solution.py:369
  31.4 14.4 %collective-permute-start.4 = (bf16[2,2,64,512]{3,2,1,0:T(8,128)(2,1)S(1)}, bf16[2,2,64,512]{3,2,1,0:T(8,128)(2,1)S(1)}, u32[]{:S(2)}, u32[]{:S(2)}) collective-permute-start(bf16[2,2,64,512]{3,2,1,0:T(8,128)(2,1)S(1)} %get-tuple-element.29), channel_id=1, source_target_pairs={{0,6},{1,4},{2,7},{3,5},{4,14},{5,12},{6,15},{7,13},{8,2},{9,0},{1... | collective-permute-start | bytes 786440 | tf_op jit(solution)/shard_map/ppermute | solution.py:403
  39.8 20.9 %collective-permute-start.5 = (bf16[2,2,64,512]{3,2,1,0:T(8,128)(2,1)S(1)}, bf16[2,2,64,512]{3,2,1,0:T(8,128)(2,1)S(1)}, u32[]{:S(2)}, u32[]{:S(2)}) collective-permute-start(bf16[2,2,64,512]{3,2,1,0:T(8,128)(2,1)S(1)} %get-tuple-element.30), channel_id=1, source_target_pairs={{0,4},{1,6},{2,5},{3,7},{4,12},{5,14},{6,13},{7,15},{8,0},{9,2},{1... | collective-permute-start | bytes 786440 | tf_op jit(solution)/shard_map/ppermute | solution.py:403
  40.9 20.3 %collective-permute-start.8 = (bf16[2,2,2,64,512]{4,3,2,1,0:T(8,128)(2,1)S(1)}, bf16[2,2,2,64,512]{4,3,2,1,0:T(8,128)(2,1)S(1)}, u32[]{:S(2)}, u32[]{:S(2)}) collective-permute-start(bf16[2,2,2,64,512]{4,3,2,1,0:T(8,128)(2,1)S(1)} %get-tuple-element.34), channel_id=1, source_target_pairs={{0,2},{2,0},{4,6},{6,4},{8,10},{10,8},{12,14},{14,12},{1,3},{3,1},... | collective-permute-start | bytes 1572872 | tf_op jit(solution)/shard_map/ppermute | solution.py:370
  40.9 20.2 %collective-permute-start.11 = (bf16[2,1,2,64,512]{4,3,2,1,0:T(8,128)(2,1)S(1)}, bf16[2,1,2,64,512]{4,3,2,1,0:T(8,128)(2,1)S(1)}, u32[]{:S(2)}, u32[]{:S(2)}) collective-permute-start(bf16[2,1,2,64,512]{4,3,2,1,0:T(8,128)(2,1)S(1)} %get-tuple-element.46), channel_id=1, source_target_pairs={{0,4},{2,6},{4,0},{6,2},{8,12},{10,14},{12,8},{14,10},{1,5},{3,7},... | collective-permute-start | bytes 786440 | tf_op jit(solution)/shard_map/ppermute | solution.py:379
  45.8 15.4 %collective-permute-start.6 = (bf16[2,2,64,512]{3,2,1,0:T(8,128)(2,1)S(1)}, bf16[2,2,64,512]{3,2,1,0:T(8,128)(2,1)S(1)}, u32[]{:S(2)}, u32[]{:S(2)}) collective-permute-start(bf16[2,2,64,512]{3,2,1,0:T(8,128)(2,1)S(1)} %get-tuple-element.31), channel_id=1, source_target_pairs={{0,2},{1,0},{2,3},{3,1},{4,10},{5,8},{6,11},{7,9},{8,6},{9,4},{10,... | collective-permute-start | bytes 786440 | tf_op jit(solution)/shard_map/ppermute | solution.py:403
  51.1 17.9 %collective-permute-start.7 = (bf16[2,2,64,512]{3,2,1,0:T(8,128)(2,1)S(1)}, bf16[2,2,64,512]{3,2,1,0:T(8,128)(2,1)S(1)}, u32[]{:S(2)}, u32[]{:S(2)}) collective-permute-start(bf16[2,2,64,512]{3,2,1,0:T(8,128)(2,1)S(1)} %get-tuple-element.32), channel_id=1, source_target_pairs={{0,0},{1,2},{2,1},{3,3},{4,8},{5,10},{6,9},{7,11},{8,4},{9,6},{10,... | collective-permute-start | bytes 786440 | tf_op jit(solution)/shard_map/ppermute | solution.py:403
  60.7 10.2 %collective-permute-start.16 = (bf16[2,1,2,64,512]{4,3,2,1,0:T(8,128)(2,1)S(1)}, bf16[2,1,2,64,512]{4,3,2,1,0:T(8,128)(2,1)S(1)}, u32[]{:S(2)}, u32[]{:S(2)}) collective-permute-start(bf16[2,1,2,64,512]{4,3,2,1,0:T(8,128)(2,1)S(1)} %shard_map.51), channel_id=1, source_target_pairs={{0,4},{2,6},{4,0},{6,2},{8,12},{10,14},{12,8},{14,10},{1,5},{3,7},... | collective-permute-start | bytes 786440 | tf_op jit(solution)/shard_map/ppermute | solution.py:379
  62.1 9.8 %collective-permute-start.12 = (bf16[2,1,64,512]{3,2,1,0:T(8,128)(2,1)S(1)}, bf16[2,1,64,512]{3,2,1,0:T(8,128)(2,1)S(1)}, u32[]{:S(2)}, u32[]{:S(2)}) collective-permute-start(bf16[2,1,64,512]{3,2,1,0:T(8,128)(2,1)S(1)} %get-tuple-element.37), channel_id=1, source_target_pairs={{0,6},{1,4},{2,7},{3,5},{4,14},{5,12},{6,15},{7,13},{8,2},{9,0},{1... | collective-permute-start | bytes 393224 | tf_op jit(solution)/shard_map/ppermute | solution.py:403
  63.4 11.6 %collective-permute-start.13 = (bf16[2,1,64,512]{3,2,1,0:T(8,128)(2,1)S(1)}, bf16[2,1,64,512]{3,2,1,0:T(8,128)(2,1)S(1)}, u32[]{:S(2)}, u32[]{:S(2)}) collective-permute-start(bf16[2,1,64,512]{3,2,1,0:T(8,128)(2,1)S(1)} %get-tuple-element.38), channel_id=1, source_target_pairs={{0,4},{1,6},{2,5},{3,7},{4,12},{5,14},{6,13},{7,15},{8,0},{9,2},{1... | collective-permute-start | bytes 393224 | tf_op jit(solution)/shard_map/ppermute | solution.py:403
  67.0 9.4 %collective-permute-start.14 = (bf16[2,1,64,512]{3,2,1,0:T(8,128)(2,1)S(1)}, bf16[2,1,64,512]{3,2,1,0:T(8,128)(2,1)S(1)}, u32[]{:S(2)}, u32[]{:S(2)}) collective-permute-start(bf16[2,1,64,512]{3,2,1,0:T(8,128)(2,1)S(1)} %get-tuple-element.39), channel_id=1, source_target_pairs={{0,2},{1,0},{2,3},{3,1},{4,10},{5,8},{6,11},{7,9},{8,6},{9,4},{10,... | collective-permute-start | bytes 393224 | tf_op jit(solution)/shard_map/ppermute | solution.py:403
  69.0 13.4 %collective-permute-start.15 = (bf16[2,1,64,512]{3,2,1,0:T(8,128)(2,1)S(1)}, bf16[2,1,64,512]{3,2,1,0:T(8,128)(2,1)S(1)}, u32[]{:S(2)}, u32[]{:S(2)}) collective-permute-start(bf16[2,1,64,512]{3,2,1,0:T(8,128)(2,1)S(1)} %get-tuple-element.40), channel_id=1, source_target_pairs={{0,0},{1,2},{2,1},{3,3},{4,8},{5,10},{6,9},{7,11},{8,4},{9,6},{10,... | collective-permute-start | bytes 393224 | tf_op jit(solution)/shard_map/ppermute | solution.py:403
  71.9 10.6 %collective-permute-start.17 = (bf16[2,1,64,512]{3,2,1,0:T(8,128)(2,1)S(1)}, bf16[2,1,64,512]{3,2,1,0:T(8,128)(2,1)S(1)}, u32[]{:S(2)}, u32[]{:S(2)}) collective-permute-start(bf16[2,1,64,512]{3,2,1,0:T(8,128)(2,1)S(1)} %get-tuple-element.41), channel_id=1, source_target_pairs={{0,6},{1,4},{2,7},{3,5},{4,14},{5,12},{6,15},{7,13},{8,2},{9,0},{1... | collective-permute-start | bytes 393224 | tf_op jit(solution)/shard_map/ppermute | solution.py:403
  71.9 10.5 %collective-permute-start.18 = (bf16[2,1,64,512]{3,2,1,0:T(8,128)(2,1)S(1)}, bf16[2,1,64,512]{3,2,1,0:T(8,128)(2,1)S(1)}, u32[]{:S(2)}, u32[]{:S(2)}) collective-permute-start(bf16[2,1,64,512]{3,2,1,0:T(8,128)(2,1)S(1)} %get-tuple-element.42), channel_id=1, source_target_pairs={{0,4},{1,6},{2,5},{3,7},{4,12},{5,14},{6,13},{7,15},{8,0},{9,2},{1... | collective-permute-start | bytes 393224 | tf_op jit(solution)/shard_map/ppermute | solution.py:403
  75.0 10.1 %collective-permute-start.19 = (bf16[2,1,64,512]{3,2,1,0:T(8,128)(2,1)S(1)}, bf16[2,1,64,512]{3,2,1,0:T(8,128)(2,1)S(1)}, u32[]{:S(2)}, u32[]{:S(2)}) collective-permute-start(bf16[2,1,64,512]{3,2,1,0:T(8,128)(2,1)S(1)} %get-tuple-element.43), channel_id=1, source_target_pairs={{0,2},{1,0},{2,3},{3,1},{4,10},{5,8},{6,11},{7,9},{8,6},{9,4},{10,... | collective-permute-start | bytes 393224 | tf_op jit(solution)/shard_map/ppermute | solution.py:403
  76.4 15.7 %copy-start.3 = (s32[2]{0:T(128)S(1)}, s32[2]{0:T(128)}, u32[]{:S(2)}) copy-start(s32[2]{0:T(128)} %values.1) | copy-start | bytes 28
  76.4 12.3 %collective-permute-start.20 = (bf16[2,1,64,512]{3,2,1,0:T(8,128)(2,1)S(1)}, bf16[2,1,64,512]{3,2,1,0:T(8,128)(2,1)S(1)}, u32[]{:S(2)}, u32[]{:S(2)}) collective-permute-start(bf16[2,1,64,512]{3,2,1,0:T(8,128)(2,1)S(1)} %get-tuple-element.44), channel_id=1, source_target_pairs={{0,0},{1,2},{2,1},{3,3},{4,8},{5,10},{6,9},{7,11},{8,4},{9,6},{10,... | collective-permute-start | bytes 393224 | tf_op jit(solution)/shard_map/ppermute | solution.py:403
  90.2 2.0 %collective-permute-start.21 = (bf16[2,256,512]{2,1,0:T(8,128)(2,1)S(1)}, bf16[2,256,512]{2,1,0:T(8,128)(2,1)S(1)}, u32[]{:S(2)}, u32[]{:S(2)}) collective-permute-start(bf16[2,256,512]{2,1,0:T(8,128)(2,1)S(1)} %shard_map.54), channel_id=1, source_target_pairs={{0,1},{1,0},{2,3},{3,2},{4,5},{5,4},{6,7},{7,6},{8,9},{9,8},{10,11... | collective-permute-start | bytes 1572872 | tf_op jit(solution)/shard_map/ppermute | solution.py:408
  (3 other events, 25.1 us)
